TPU v7x, 256 devices: a whole 4x4x8 slice. The times are simulated.
256 devices in a mesh: chan: 16 (over z, core), cross: 16 (over x, y).
Axes of the slice: x: 4, y: 4, z: 8, core: 2. Of those that a mesh axis runs over, the one named last changes fastest.
Arguments:
- tracers: float32 [5, 4, 256, 32768], P(None, None, 'chan', 'cross'), may hold values from 0 to 10
- kappa_x: float32 [4, 256, 32768], P(None, 'chan', 'cross'), may hold values from 0.5 to 50
- kappa_y: float32 [4, 256, 32768], P(None, 'chan', 'cross'), may hold values from 0.05 to 0.24
- courant: float32 [4, 256, 32768], P(None, 'chan', 'cross'), may hold values from 32 to 320
- wet_mask: int32 [256, 32768], P('chan', 'cross'), may hold values from 0 to 1, as said below
- levels: int32 [256, 32768], P('chan', 'cross'), may hold values from 2 to 4, as said below
Outputs:
- updated: float32 [5, 4, 256, 32768], P(None, None, 'chan', 'cross')
Inputs may be any that keep to these rules, and one draw needn't show every extreme that they name: `wet_mask`: for every along-channel cell the dry cells are the first 1 to 2048 and the last 1 to 2048 cross-channel cells; all others are wet. `levels`: the layer count of a column depends only on its cross-channel cell.
All inputs are finite; a program needn't handle non-finite values.
Results may differ from a plain program's by a relative error of at most 0.000042.
Values sent between devices are 32-bit elements; how exact they have to be, the bound alone decides.
No kernel may reach another device: no remote copies, remote signals or barrier semaphores. Data moves between devices by JAX's collectives and lax.ppermute only.
A program may use at most 128 MiB of HBM per device.

v0:
```python
import functools

import jax
import jax.numpy as jnp
from jax import lax
from jax.experimental import pallas as pl
from jax.experimental.pallas import tpu as pltpu
from jax.sharding import PartitionSpec as P

TRACERS = 5
LAYERS = 4
ROWS = 16
CHIPS = 8
CD0, WA0, D0, F0, R0, CDN, DN, EN, RN = 0, 1, 2, 3, 4, 9, 10, 11, 12
PARTS = 17
SENT = 18
BACK = 10
F32 = jnp.float32


def folded(cells):
    lead = cells.shape[:-2]
    cells = cells.reshape(lead + (2, 8, 16, 128))
    return jnp.swapaxes(cells, len(lead) + 1, len(lead) + 2).reshape(lead + (256, 128))


def unfolded(cells):
    lead = cells.shape[:-2]
    cells = cells.reshape(lead + (2, 16, 8, 128))
    return jnp.swapaxes(cells, len(lead) + 1, len(lead) + 2).reshape(lead + (16, 2048))


def line(row, half):
    return pl.ds((row // 8) * 128 + half * 64 + row % 8, 8, stride=8)


def tile(row_tile, column_tile):
    return pl.ds(row_tile * 128 + column_tile * 8, 8)


def edges_kernel(tr_lo, tr_hi, ky_lo, ky_hi, wet_lo, wet_hi, lev_lo, lev_hi, out_lo, out_hi):
    lane = lax.broadcasted_iota(jnp.int32, (8, 128), 1)
    for tr, ky, wet, lev, out, at in (
        (tr_lo, ky_lo, wet_lo, lev_lo, out_lo, 0),
        (tr_hi, ky_hi, wet_hi, lev_hi, out_hi, 127),
    ):
        for l in range(LAYERS):
            for i in range(2):
                rows = pl.ds(i * 8, 8)
                active = (wet[rows, :] > 0) & (lev[rows, :] > l)
                parts = [tr[t, l, rows, :] for t in range(TRACERS)]
                parts.append(jnp.where(active, ky[l, rows, :], 0.0))
                packed = jnp.zeros((8, 128), F32)
                for t, part in enumerate(parts):
                    packed = jnp.where(lane == t, pltpu.roll(part, (t - at) % 128, 1), packed)
                out[l, rows, :] = packed


def edges(tracers, kappa_y, wet, levels):
    def spec(lead, at):
        zeros = (0,) * (len(lead) + 1)
        return pl.BlockSpec(lead + (16, 128), lambda i, zeros=zeros, at=at: zeros + (at,))

    return pl.pallas_call(
        edges_kernel,
        grid=(1,),
        in_specs=[
            spec((TRACERS, LAYERS), 0),
            spec((TRACERS, LAYERS), 15),
            spec((LAYERS,), 0),
            spec((LAYERS,), 15),
            spec((), 0),
            spec((), 15),
            spec((), 0),
            spec((), 15),
        ],
        out_specs=[pl.BlockSpec((LAYERS, 16, 128), lambda i: (0, 0, 0))] * 2,
        out_shape=[jax.ShapeDtypeStruct((LAYERS, 16, 128), F32)] * 2,
        name="edges",
    )(tracers, tracers, kappa_y, kappa_y, wet, wet, levels, levels)


def local_kernel(
    core, tr, kx, ky, co, wet, lev, left, right, red, fill, rho, mine, theirs, side
):
    layer = pl.program_id(0)
    first_core = core[0] == 0
    lane = lax.broadcasted_iota(jnp.int32, (8, 128), 1)
    head, tail = lane == 0, lane == 127

    for i in range(2):
        rows = pl.ds(i * 8, 8)
        lo, hi = left[0, rows, :], right[0, rows, :]

        def cross_of(j):
            active = (wet[tile(i, j), :] > 0) & (lev[tile(i, j), :] > layer)
            return jnp.where(active, ky[0, tile(i, j), :], 0.0)

        def ahead(now, following):
            return jnp.where(tail, pltpu.roll(following, 127, 1), pltpu.roll(now, 127, 1))

        faces = []
        now = cross_of(0)
        first_face = jnp.minimum(now, pltpu.roll(lo, (0 - TRACERS) % 128, 1))
        for j in range(16):
            following = cross_of(j + 1) if j < 15 else pltpu.roll(hi, (0 - TRACERS) % 128, 1)
            faces.append(jnp.minimum(now, ahead(now, following)))
            now = following
        for t in range(TRACERS):
            now = tr[t, 0, tile(i, 0), :]
            shifted = pltpu.roll(now, 127, 1)
            before = first_face * (now - pltpu.roll(lo, (0 - t) % 128, 1))
            for j in range(16):
                following = tr[t, 0, tile(i, j + 1), :] if j < 15 else pltpu.roll(hi, (0 - t) % 128, 1)
                shifted_following = pltpu.roll(following, 127, 1)
                flux = faces[j] * (jnp.where(tail, shifted_following, shifted) - now)
                behind = pltpu.roll(flux, 1, 1)
                side[t, tile(i, j), :] = now + flux - jnp.where(head, before, behind)
                before = behind
                now, shifted = following, shifted_following

    halves = []
    for half in range(2):

        def load(row):
            where = line(row, half)
            active = (wet[where, :] > 0) & (lev[where, :] > layer)
            act = jnp.where(active, 1.0, 0.0).astype(F32)
            return act, kx[0, where, :] * act, co[0, where, :]

        out = [None] * PARTS
        act_prev, cd_prev, co_prev = load(0)
        act, cd, cour = load(1)
        out[CD0] = cd_prev
        out[WA0] = act_prev * co_prev
        face_first = jnp.minimum(cd_prev, cd)
        face_down = face_first
        rho_row = None
        for row in range(1, ROWS - 1):
            act_next, cd_next, co_next = load(row + 1)
            face_up = jnp.minimum(cd, cd_next)
            low = act * (face_down + cour * act_prev)
            where = pl.ds((half * ROWS + row) * 8, 8)
            if row == 1:
                inverse = 1.0 / (1.0 + face_up + low)
                rho_row = face_up * inverse
                gain = low * inverse
                fill_row = gain
                reds = [side[t, line(row, half), :] * inverse for t in range(TRACERS)]
                sums = list(reds)
                sum_fill = fill_row
                chain = rho_row
            else:
                inverse = 1.0 / (1.0 + face_up + low * (1.0 - rho_row))
                rho_row = face_up * inverse
                gain = low * inverse
                fill_row = gain * fill_row
                reds = [side[t, line(row, half), :] * inverse + gain * reds[t] for t in range(TRACERS)]
                sums = [sums[t] + chain * reds[t] for t in range(TRACERS)]
                sum_fill = sum_fill + chain * fill_row
                chain = chain * rho_row
            rho[0, where, :] = rho_row
            fill[0, where, :] = fill_row
            for t in range(TRACERS):
                red[t, 0, where, :] = reds[t]
            act_prev = act
            act, cd, cour = act_next, cd_next, co_next
            face_down = face_up
        low = act * (face_down + cour * act_prev)
        out[D0] = 1.0 + face_first * (1.0 - sum_fill)
        out[F0] = face_first * chain
        out[CDN] = cd
        out[DN] = 1.0 + low * (1.0 - rho_row)
        out[EN] = low * fill_row
        for t in range(TRACERS):
            out[R0 + t] = side[t, line(0, half), :] + face_first * sums[t]
            out[RN + t] = side[t, line(ROWS - 1, half), :] + low * reds[t]
        halves.append(out)
    for part in range(PARTS):
        mine[part, 0] = jnp.where(first_core, halves[0][part], halves[1][part])
        theirs[part, 0] = jnp.where(first_core, halves[1][part], halves[0][part])


def local_part(core, tracers, kappa_x, kappa_y, courant, wet, levels, left, right):
    layered = lambda *lead: pl.BlockSpec(lead + (1, 256, 128), lambda l, n=len(lead): (0,) * n + (l, 0, 0))
    whole = pl.BlockSpec((256, 128), lambda l: (0, 0))
    halo = pl.BlockSpec((1, 16, 128), lambda l: (l, 0, 0))
    packed = pl.BlockSpec((PARTS, 1, 8, 128), lambda l: (0, l, 0, 0))
    return pl.pallas_call(
        local_kernel,
        grid=(LAYERS,),
        in_specs=[
            pl.BlockSpec(memory_space=pltpu.SMEM),
            layered(TRACERS),
            layered(),
            layered(),
            layered(),
            whole,
            whole,
            halo,
            halo,
        ],
        out_specs=[layered(TRACERS), layered(), layered(), packed, packed],
        out_shape=[
            jax.ShapeDtypeStruct((TRACERS, LAYERS, 256, 128), F32),
            jax.ShapeDtypeStruct((LAYERS, 256, 128), F32),
            jax.ShapeDtypeStruct((LAYERS, 256, 128), F32),
            jax.ShapeDtypeStruct((PARTS, LAYERS, 8, 128), F32),
            jax.ShapeDtypeStruct((PARTS, LAYERS, 8, 128), F32),
        ],
        scratch_shapes=[pltpu.VMEM((TRACERS, 256, 128), F32)],
        compiler_params=pltpu.CompilerParams(vmem_limit_bytes=16 * 1024 * 1024),
        name="local_part",
    )(core, tracers, kappa_x, kappa_y, courant, wet, levels, left, right)


def pair_kernel(core, mine, other, sent, kept):
    first_core = core[0] == 0
    for l in range(LAYERS):
        a = [mine[part, l] for part in range(PARTS)]
        b = [other[part, l] for part in range(PARTS)]
        lo = [jnp.where(first_core, x, y) for x, y in zip(a, b)]
        hi = [jnp.where(first_core, y, x) for x, y in zip(a, b)]
        face = jnp.minimum(lo[CDN], hi[CD0])
        down = face + jnp.where(lo[CDN] > 0.0, hi[WA0], 0.0)
        scale = 1.0 / (lo[DN] * (hi[D0] + down) + face * hi[D0])
        in_b = scale * (hi[D0] + down)
        in_g = scale * face
        in_w = scale * down
        in_a = scale * (lo[DN] + face)
        last_f, last_l = in_b * lo[EN], in_g * hi[F0]
        first_f, first_l = in_w * lo[EN], in_a * hi[F0]
        last_r = [in_b * lo[RN + t] + in_g * hi[R0 + t] for t in range(TRACERS)]
        first_r = [in_w * lo[RN + t] + in_a * hi[R0 + t] for t in range(TRACERS)]
        out = [None] * PARTS
        out[CD0], out[WA0], out[CDN] = lo[CD0], lo[WA0], hi[CDN]
        out[D0] = lo[D0] - lo[F0] * last_f
        out[F0] = lo[F0] * last_l
        out[DN] = hi[DN] - hi[EN] * first_l
        out[EN] = hi[EN] * first_f
        for t in range(TRACERS):
            out[R0 + t] = lo[R0 + t] + lo[F0] * last_r[t]
            out[RN + t] = hi[RN + t] + hi[EN] * first_r[t]
        for part in range(PARTS):
            sent[pl.ds(l * SENT + part, CHIPS, stride=LAYERS * SENT), :] = out[part]
        sent[pl.ds(l * SENT + PARTS, CHIPS, stride=LAYERS * SENT), :] = jnp.zeros((8, 128), F32)
        for k, value in enumerate(last_r + first_r + [last_f, last_l, first_f, first_l]):
            kept[k, l] = value


def pair_part(core, mine, other):
    vmem = pl.BlockSpec(memory_space=pltpu.VMEM)
    return pl.pallas_call(
        pair_kernel,
        in_specs=[pl.BlockSpec(memory_space=pltpu.SMEM), vmem, vmem],
        out_specs=[vmem, vmem],
        out_shape=[
            jax.ShapeDtypeStruct((CHIPS * LAYERS * SENT, 128), F32),
            jax.ShapeDtypeStruct((14, LAYERS, 8, 128), F32),
        ],
        name="pair_part",
    )(core, mine, other)


def chain_kernel(parts, solved):
    load = lambda chip, part: parts[pl.ds(chip * LAYERS * SENT + part, LAYERS, stride=SENT), :]
    firsts, lasts = [], []
    cd_prev = gate = ratio = reduced = None
    base, known = None, None
    for chip in range(CHIPS):
        d0, f0 = load(chip, D0), load(chip, F0)
        dn, en = load(chip, DN), load(chip, EN)
        r0 = [load(chip, R0 + t) for t in range(TRACERS)]
        rn = [load(chip, RN + t) for t in range(TRACERS)]
        if chip:
            cd0 = load(chip, CD0)
            face = jnp.minimum(cd_prev, cd0)
            down = face + jnp.where(cd_prev > 0.0, load(chip, WA0), 0.0)
            inverse = 1.0 / (base + face)
            ratio = face * inverse
            reduced = [x * inverse for x in known]
            lasts.append((ratio, reduced))
            inverse = 1.0 / (d0 + down * (1.0 - ratio))
            r0 = [x + down * y for x, y in zip(r0, reduced)]
        else:
            inverse = 1.0 / d0
        ahead = f0 * inverse
        here = [x * inverse for x in r0]
        firsts.append((ahead, here))
        base = dn - en * ahead
        known = [x + en * y for x, y in zip(rn, here)]
        cd_prev = load(chip, CDN)
    inverse = 1.0 / base
    last = [x * inverse for x in known]
    for chip in reversed(range(CHIPS)):
        ahead, here = firsts[chip]
        first = [x + ahead * y for x, y in zip(here, last)]
        for t in range(TRACERS):
            solved[pl.ds(chip * LAYERS * BACK + t, LAYERS, stride=BACK), :] = first[t]
            solved[pl.ds(chip * LAYERS * BACK + TRACERS + t, LAYERS, stride=BACK), :] = last[t]
        if chip:
            ratio, reduced = lasts[chip - 1]
            last = [x + ratio * y for x, y in zip(reduced, first)]


def chain_part(parts):
    vmem = pl.BlockSpec(memory_space=pltpu.VMEM)
    return pl.pallas_call(
        chain_kernel,
        in_specs=[vmem],
        out_specs=vmem,
        out_shape=jax.ShapeDtypeStruct((CHIPS * LAYERS * BACK, 128), F32),
        name="chain_part",
    )(parts)


def middle_kernel(core, solved, kept, mine, theirs):
    first_core = core[0] == 0
    for l in range(LAYERS):
        last_f, last_l, first_f, first_l = (kept[10 + k, l] for k in range(4))
        for t in range(TRACERS):
            first = solved[pl.ds(l * BACK + t, CHIPS, stride=LAYERS * BACK), :]
            last = solved[pl.ds(l * BACK + TRACERS + t, CHIPS, stride=LAYERS * BACK), :]
            before = kept[t, l] + last_f * first + last_l * last
            after = kept[TRACERS + t, l] + first_f * first + first_l * last
            mine[t, l] = jnp.where(first_core, first, after)
            mine[TRACERS + t, l] = jnp.where(first_core, before, last)
            theirs[t, l] = jnp.where(first_core, after, first)
            theirs[TRACERS + t, l] = jnp.where(first_core, last, before)


def middle_part(core, solved, kept):
    vmem = pl.BlockSpec(memory_space=pltpu.VMEM)
    return pl.pallas_call(
        middle_kernel,
        in_specs=[pl.BlockSpec(memory_space=pltpu.SMEM), vmem, vmem],
        out_specs=[vmem, vmem],
        out_shape=[jax.ShapeDtypeStruct((BACK, LAYERS, 8, 128), F32)] * 2,
        name="middle_part",
    )(core, solved, kept)


def final_kernel(core, red, fill, rho, mine, other, out):
    first_core = core[0] == 0
    for half in range(2):
        pick = (lambda k: jnp.where(first_core, mine[k, 0], other[k, 0])) if half == 0 else (
            lambda k: jnp.where(first_core, other[k, 0], mine[k, 0])
        )
        firsts = [pick(t) for t in range(TRACERS)]
        cells = [pick(TRACERS + t) for t in range(TRACERS)]
        for t in range(TRACERS):
            out[t, 0, line(ROWS - 1, half), :] = cells[t]
            out[t, 0, line(0, half), :] = firsts[t]
        for row in reversed(range(1, ROWS - 1)):
            where = pl.ds((half * ROWS + row) * 8, 8)
            fill_row, rho_row = fill[0, where, :], rho[0, where, :]
            for t in range(TRACERS):
                cells[t] = red[t, 0, where, :] + fill_row * firsts[t] + rho_row * cells[t]
                out[t, 0, line(row, half), :] = cells[t]


def final_part(core, red, fill, rho, mine, other):
    layered = lambda *lead: pl.BlockSpec(lead + (1, 256, 128), lambda l, n=len(lead): (0,) * n + (l, 0, 0))
    packed = pl.BlockSpec((BACK, 1, 8, 128), lambda l: (0, l, 0, 0))
    return pl.pallas_call(
        final_kernel,
        grid=(LAYERS,),
        in_specs=[
            pl.BlockSpec(memory_space=pltpu.SMEM),
            layered(TRACERS),
            layered(),
            layered(),
            packed,
            packed,
        ],
        out_specs=layered(TRACERS),
        out_shape=jax.ShapeDtypeStruct((TRACERS, LAYERS, 256, 128), F32),
        compiler_params=pltpu.CompilerParams(vmem_limit_bytes=16 * 1024 * 1024),
        name="final_part",
    )(core, red, fill, rho, mine, other)


def on_device(tracers, kappa_x, kappa_y, courant, wet_mask, levels):
    count = lax.axis_size("cross")
    core = (lax.axis_index("chan") % 2).astype(jnp.int32).reshape(1)
    pairs = [(i, i ^ 1) for i in range(2 * CHIPS)]
    lines = [[c + 2 * z for z in range(CHIPS)] for c in range(2)]

    lowest, highest = edges(tracers, kappa_y, wet_mask, levels)
    left = lax.ppermute(highest, "cross", [(i, i + 1) for i in range(count - 1)])
    right = lax.ppermute(lowest, "cross", [(i + 1, i) for i in range(count - 1)])
    red, fill, rho, mine, theirs = local_part(
        core,
        folded(tracers),
        folded(kappa_x),
        folded(kappa_y),
        folded(courant),
        folded(wet_mask),
        folded(levels),
        left,
        right,
    )
    other = lax.ppermute(theirs, "chan", pairs)
    sent, kept = pair_part(core, mine, other)
    parts = lax.all_to_all(
        sent.reshape(CHIPS, LAYERS * SENT, 128), "chan", 0, 0, axis_index_groups=lines, tiled=True
    )
    solved = chain_part(parts.reshape(CHIPS * LAYERS * SENT, 128))
    back = lax.all_to_all(
        solved.reshape(CHIPS, LAYERS * BACK, 128), "chan", 0, 0, axis_index_groups=lines, tiled=True
    )
    mine, theirs = middle_part(core, back.reshape(CHIPS * LAYERS * BACK, 128), kept)
    other = lax.ppermute(theirs, "chan", pairs)
    return unfolded(final_part(core, red, fill, rho, mine, other))


def solution(mesh):
    placed = (
        P(None, None, "chan", "cross"),
        P(None, "chan", "cross"),
        P(None, "chan", "cross"),
        P(None, "chan", "cross"),
        P("chan", "cross"),
        P("chan", "cross"),
    )
    return jax.shard_map(
        on_device,
        mesh=mesh,
        in_specs=placed,
        out_specs=P(None, None, "chan", "cross"),
        check_vma=False,
    )
```

profile of v0, /device:TPU:1, one launch (start us, length us, event | category | flops | bytes accessed | tf_op | source)
XLA Modules:
  0.0 72.8 jit_solution(12421772635629551731)
XLA Ops:
  0.0 0.0 copy-start.5
  0.0 0.0 copy-start.4
  0.0 0.0 copy-start.1
  0.0 0.0 copy-start
  0.0 2.0 %edges.1 = (f32[4,16,128]{2,1,0:T(8,128)}, f32[4,16,128]{2,1,0:T(8,128)}) custom-call(f32[5,4,16,2048]{3,2,1,0:T(8,128)} %tr_hi.1, f32[5,4,16,2048]{3,2,1,0:T(8,128)} %tr_hi.1, f32[4,16,2048]{2,1,0:T(8,128)} %ky_hi.1, f32[4,16,2048]{2,1,0:T(8,128)} %ky_hi.1, s32[16,2048]{1,0:T(8,128)} %wet_hi.1, s32[16,2048]{1,0:T(8,128)} %wet_hi.1, s32[16,2048]{1,0:T(8,128)} %lev_hi.1, ...), custom_call_target="tpu_custom_call" | custom-call | tf_op jit(solution)/shard_map/edges/pallas_call | solution.py:64
  2.0 4.0 %collective-permute-start = (f32[4,16,128]{2,1,0:T(8,128)}, f32[4,16,128]{2,1,0:T(8,128)S(1)}, u32[]{:S(2)}, u32[]{:S(2)}) collective-permute-start(f32[4,16,128]{2,1,0:T(8,128)} %get-tuple-element.16), channel_id=1, source_target_pairs={{0,1},{1,2},{2,3},{3,4},{4,5},{5,6},{6,7},{7,8},{8,9},{9,10},{10,1... | collective-permute-start | bytes 98312 | tf_op jit(solution)/shard_map/ppermute | solution.py:390
  6.0 1.3 %collective-permute-start.1 = (f32[4,16,128]{2,1,0:T(8,128)}, f32[4,16,128]{2,1,0:T(8,128)S(1)}, u32[]{:S(2)}, u32[]{:S(2)}) collective-permute-start(f32[4,16,128]{2,1,0:T(8,128)} %get-tuple-element.17), channel_id=1, source_target_pairs={{1,0},{2,1},{3,2},{4,3},{5,4},{6,5},{7,6},{8,7},{9,8},{10,9},{11,1... | collective-permute-start | bytes 98312 | tf_op jit(solution)/shard_map/ppermute | solution.py:391
  7.3 0.0 collective-permute-done.left
  7.3 3.5 %collective-permute-done.1.right = f32[4,16,128]{2,1,0:T(8,128)S(1)} collective-permute-done((f32[4,16,128]{2,1,0:T(8,128)}, f32[4,16,128]{2,1,0:T(8,128)S(1)}, u32[]{:S(2)}, u32[]{:S(2)}) %collective-permute-start.1) | collective-permute-done | bytes 32800 | tf_op jit(solution)/shard_map/ppermute | solution.py:391
  10.9 0.0 copy-done.5
  10.9 0.0 copy-done.4
  10.9 0.0 copy-done.1
  10.9 0.0 copy-done
  10.9 0.0 copy-start.6
  10.9 1.0 %copy-done.6 = f32[4,16,2048]{2,1,0:T(8,128)S(1)} copy-done((f32[4,16,2048]{2,1,0:T(8,128)S(1)}, f32[4,16,2048]{2,1,0:T(8,128)}, u32[]{:S(2)}) %copy-start.6) | copy-done | bytes 524312
  11.9 0.0 copy-start.7
  11.9 1.0 %copy-done.7 = f32[4,16,2048]{2,1,0:T(8,128)S(1)} copy-done((f32[4,16,2048]{2,1,0:T(8,128)S(1)}, f32[4,16,2048]{2,1,0:T(8,128)}, u32[]{:S(2)}) %copy-start.7) | copy-done | bytes 524312
  13.0 4.8 %local_part.1 = (f32[5,4,256,128]{3,2,1,0:T(8,128)S(1)}, f32[4,256,128]{2,1,0:T(8,128)S(1)}, f32[4,256,128]{2,1,0:T(8,128)S(1)}, f32[17,4,8,128]{3,2,1,0:T(8,128)S(1)}, f32[17,4,8,128]{3,2,1,0:T(8,128)S(1)}) custom-call(s32[1]{0:T(128)} %bitcast.core, f32[5,4,256,128]{3,2,1,0:T(8,128)S(1)} %bitcast.40, f32[4,256,128]{2,1,0:T(8,128)S(1)} %bitcast.44, ...), custom_call_target="tpu_custom_call" | custom-call | tf_op jit(solution)/shard_map/local_part/pallas_call | solution.py:189
  17.8 0.0 copy-start.2
  17.8 1.5 %copy-done.2 = f32[5,4,256,128]{3,2,1,0:T(8,128)} copy-done((f32[5,4,256,128]{3,2,1,0:T(8,128)}, f32[5,4,256,128]{3,2,1,0:T(8,128)S(1)}, u32[]{:S(2)}) %copy-start.2) | copy-done | bytes 2621464
  19.3 0.0 copy-start.8
  19.3 0.8 %copy-done.8 = f32[4,256,128]{2,1,0:T(8,128)} copy-done((f32[4,256,128]{2,1,0:T(8,128)}, f32[4,256,128]{2,1,0:T(8,128)S(1)}, u32[]{:S(2)}) %copy-start.8) | copy-done | bytes 524312
  20.1 0.0 copy-start.10
  20.1 0.8 %copy-done.10 = f32[4,256,128]{2,1,0:T(8,128)} copy-done((f32[4,256,128]{2,1,0:T(8,128)}, f32[4,256,128]{2,1,0:T(8,128)S(1)}, u32[]{:S(2)}) %copy-start.10) | copy-done | bytes 524312
  20.9 0.0 copy-start.12
  20.9 0.7 copy-done.12
  21.6 0.0 copy-start.9
  21.6 0.0 copy-start.11
  21.6 2.1 %collective-permute-start.2 = (f32[17,4,8,128]{3,2,1,0:T(8,128)S(1)}, f32[17,4,8,128]{3,2,1,0:T(8,128)S(1)}, u32[]{:S(2)}, u32[]{:S(2)}) collective-permute-start(f32[17,4,8,128]{3,2,1,0:T(8,128)S(1)} %get-tuple-element.22), channel_id=1, source_target_pairs={{0,16},{16,0},{32,48},{48,32},{64,80},{80,64},{96,112},{112,96},{1... | collective-permute-start | bytes 835592 | tf_op jit(solution)/shard_map/ppermute | solution.py:403
  23.7 1.2 %collective-permute-done.2.other = f32[17,4,8,128]{3,2,1,0:T(8,128)S(1)} collective-permute-done((f32[17,4,8,128]{3,2,1,0:T(8,128)S(1)}, f32[17,4,8,128]{3,2,1,0:T(8,128)S(1)}, u32[]{:S(2)}, u32[]{:S(2)}) %collective-permute-start.2) | collective-permute-done | bytes 278560 | tf_op jit(solution)/shard_map/ppermute | solution.py:403
  24.9 0.0 copy-start.14
  24.9 0.7 copy-done.14
  25.7 2.0 %pair_part.1 = (f32[576,128]{1,0:T(8,128)}, f32[14,4,8,128]{3,2,1,0:T(8,128)}) custom-call(s32[1]{0:T(128)} %bitcast.core, f32[17,4,8,128]{3,2,1,0:T(8,128)} %copy-done.12, f32[17,4,8,128]{3,2,1,0:T(8,128)} %copy-done.14), custom_call_target="tpu_custom_call" | custom-call | tf_op jit(solution)/shard_map/pair_part/pallas_call | solution.py:253
  27.6 20.5 %all_to_all.10 = f32[8,72,128]{2,1,0:T(8,128)} all-to-all(f32[8,72,128]{2,1,0:T(8,128)} %bitcast.49), channel_id=1, replica_groups={{0,32,64,96,128,160,192,224},{16,48,80,112,144,176,208,240},{1,33,65,97..., dimensions={0} | all-to-all | bytes 589824 | tf_op jit(solution)/shard_map/all_to_all | solution.py:405
  48.1 1.8 %chain_part.1 = f32[320,128]{1,0:T(8,128)} custom-call(f32[576,128]{1,0:T(8,128)} %bitcast.46), custom_call_target="tpu_custom_call" | custom-call | tf_op jit(solution)/shard_map/chain_part/pallas_call | solution.py:308
  49.9 12.1 %all_to_all.11 = f32[8,40,128]{2,1,0:T(8,128)} all-to-all(f32[8,40,128]{2,1,0:T(8,128)} %bitcast.47), channel_id=1, replica_groups={{0,32,64,96,128,160,192,224},{16,48,80,112,144,176,208,240},{1,33,65,97..., dimensions={0} | all-to-all | bytes 327680 | tf_op jit(solution)/shard_map/all_to_all | solution.py:409
  62.0 1.8 %middle_part.1 = (f32[10,4,8,128]{3,2,1,0:T(8,128)}, f32[10,4,8,128]{3,2,1,0:T(8,128)}) custom-call(s32[1]{0:T(128)} %bitcast.core, f32[320,128]{1,0:T(8,128)} %bitcast.48, f32[14,4,8,128]{3,2,1,0:T(8,128)} %get-tuple-element.24.kept), custom_call_target="tpu_custom_call" | custom-call | tf_op jit(solution)/shard_map/middle_part/pallas_call | solution.py:334
  63.8 2.7 %collective-permute-start.3 = (f32[10,4,8,128]{3,2,1,0:T(8,128)}, f32[10,4,8,128]{3,2,1,0:T(8,128)S(1)}, u32[]{:S(2)}, u32[]{:S(2)}) collective-permute-start(f32[10,4,8,128]{3,2,1,0:T(8,128)} %get-tuple-element.26), channel_id=1, source_target_pairs={{0,16},{16,0},{32,48},{48,32},{64,80},{80,64},{96,112},{112,96},{1... | collective-permute-start | bytes 491528 | tf_op jit(solution)/shard_map/ppermute | solution.py:413
  66.5 1.2 %collective-permute-done.3.other = f32[10,4,8,128]{3,2,1,0:T(8,128)S(1)} collective-permute-done((f32[10,4,8,128]{3,2,1,0:T(8,128)}, f32[10,4,8,128]{3,2,1,0:T(8,128)S(1)}, u32[]{:S(2)}, u32[]{:S(2)}) %collective-permute-start.3) | collective-permute-done | bytes 163872 | tf_op jit(solution)/shard_map/ppermute | solution.py:413
  67.8 0.0 copy-done.9
  67.8 0.0 copy-done.11
  67.8 0.0 copy-start.3
  67.8 1.7 %copy-done.3 = f32[5,4,256,128]{3,2,1,0:T(8,128)S(1)} copy-done((f32[5,4,256,128]{3,2,1,0:T(8,128)S(1)}, f32[5,4,256,128]{3,2,1,0:T(8,128)}, u32[]{:S(2)}) %copy-start.3) | copy-done | bytes 2621464
  69.5 0.0 copy-start.13
  69.5 0.9 %copy-done.13 = f32[10,4,8,128]{3,2,1,0:T(8,128)S(1)} copy-done((f32[10,4,8,128]{3,2,1,0:T(8,128)S(1)}, f32[10,4,8,128]{3,2,1,0:T(8,128)}, u32[]{:S(2)}) %copy-start.13) | copy-done | bytes 163864
  70.4 2.3 %final_part.1 = f32[5,4,256,128]{3,2,1,0:T(8,128)} custom-call(s32[1]{0:T(128)} %bitcast.core, f32[5,4,256,128]{3,2,1,0:T(8,128)S(1)} %copy-done.3, f32[4,256,128]{2,1,0:T(8,128)S(1)} %copy-done.9, f32[4,256,128]{2,1,0:T(8,128)S(1)} %copy-done.11, f32[10,4,8,128]{3,2,1,0:T(8,128)S(1)} %copy-done.13, f32[10,4,8,128]{3,2,1,0:T(8,128)S(1)} %collective-permute-done.3.other), custom_call_target="tpu_custom_call" | custom-call | tf_op jit(solution)/shard_map/final_part/pallas_call | solution.py:365
Async XLA Ops:
  0.0 10.9 %copy-start.5 = (s32[16,2048]{1,0:T(8,128)S(1)}, s32[16,2048]{1,0:T(8,128)}, u32[]{:S(2)}) copy-start(s32[16,2048]{1,0:T(8,128)} %lev_hi.1) | copy-start | bytes 393220
  0.0 10.9 %copy-start.4 = (s32[16,2048]{1,0:T(8,128)S(1)}, s32[16,2048]{1,0:T(8,128)}, u32[]{:S(2)}) copy-start(s32[16,2048]{1,0:T(8,128)} %wet_hi.1) | copy-start | bytes 393220
  0.0 10.9 %copy-start.1 = (f32[4,16,2048]{2,1,0:T(8,128)S(1)}, f32[4,16,2048]{2,1,0:T(8,128)}, u32[]{:S(2)}) copy-start(f32[4,16,2048]{2,1,0:T(8,128)} %ky_hi.1) | copy-start | bytes 1572868
  0.0 10.9 %copy-start = (f32[5,4,16,2048]{3,2,1,0:T(8,128)S(1)}, f32[5,4,16,2048]{3,2,1,0:T(8,128)}, u32[]{:S(2)}) copy-start(f32[5,4,16,2048]{3,2,1,0:T(8,128)} %tr_hi.1) | copy-start | bytes 7864324
  2.0 5.3 %collective-permute-start = (f32[4,16,128]{2,1,0:T(8,128)}, f32[4,16,128]{2,1,0:T(8,128)S(1)}, u32[]{:S(2)}, u32[]{:S(2)}) collective-permute-start(f32[4,16,128]{2,1,0:T(8,128)} %get-tuple-element.16), channel_id=1, source_target_pairs={{0,1},{1,2},{2,3},{3,4},{4,5},{5,6},{6,7},{7,8},{8,9},{9,10},{10,1... | collective-permute-start | bytes 98312 | tf_op jit(solution)/shard_map/ppermute | solution.py:390
  6.0 4.9 %collective-permute-start.1 = (f32[4,16,128]{2,1,0:T(8,128)}, f32[4,16,128]{2,1,0:T(8,128)S(1)}, u32[]{:S(2)}, u32[]{:S(2)}) collective-permute-start(f32[4,16,128]{2,1,0:T(8,128)} %get-tuple-element.17), channel_id=1, source_target_pairs={{1,0},{2,1},{3,2},{4,3},{5,4},{6,5},{7,6},{8,7},{9,8},{10,9},{11,1... | collective-permute-start | bytes 98312 | tf_op jit(solution)/shard_map/ppermute | solution.py:391
  10.9 1.0 %copy-start.6 = (f32[4,16,2048]{2,1,0:T(8,128)S(1)}, f32[4,16,2048]{2,1,0:T(8,128)}, u32[]{:S(2)}) copy-start(f32[4,16,2048]{2,1,0:T(8,128)} %param.7) | copy-start | bytes 1572868
  11.9 1.0 %copy-start.7 = (f32[4,16,2048]{2,1,0:T(8,128)S(1)}, f32[4,16,2048]{2,1,0:T(8,128)}, u32[]{:S(2)}) copy-start(f32[4,16,2048]{2,1,0:T(8,128)} %param.9) | copy-start | bytes 1572868
  17.8 1.5 %copy-start.2 = (f32[5,4,256,128]{3,2,1,0:T(8,128)}, f32[5,4,256,128]{3,2,1,0:T(8,128)S(1)}, u32[]{:S(2)}) copy-start(f32[5,4,256,128]{3,2,1,0:T(8,128)S(1)} %get-tuple-element.18.red) | copy-start | bytes 7864324
  19.3 0.8 %copy-start.8 = (f32[4,256,128]{2,1,0:T(8,128)}, f32[4,256,128]{2,1,0:T(8,128)S(1)}, u32[]{:S(2)}) copy-start(f32[4,256,128]{2,1,0:T(8,128)S(1)} %get-tuple-element.19.fill) | copy-start | bytes 1572868
  20.1 0.8 %copy-start.10 = (f32[4,256,128]{2,1,0:T(8,128)}, f32[4,256,128]{2,1,0:T(8,128)S(1)}, u32[]{:S(2)}) copy-start(f32[4,256,128]{2,1,0:T(8,128)S(1)} %get-tuple-element.20.rho) | copy-start | bytes 1572868
  20.9 0.7 copy-start.12
  21.6 46.1 %copy-start.9 = (f32[4,256,128]{2,1,0:T(8,128)S(1)}, f32[4,256,128]{2,1,0:T(8,128)}, u32[]{:S(2)}) copy-start(f32[4,256,128]{2,1,0:T(8,128)} %copy-done.8) | copy-start | bytes 1572868
  21.6 46.1 %copy-start.11 = (f32[4,256,128]{2,1,0:T(8,128)S(1)}, f32[4,256,128]{2,1,0:T(8,128)}, u32[]{:S(2)}) copy-start(f32[4,256,128]{2,1,0:T(8,128)} %copy-done.10) | copy-start | bytes 1572868
  21.6 3.3 %collective-permute-start.2 = (f32[17,4,8,128]{3,2,1,0:T(8,128)S(1)}, f32[17,4,8,128]{3,2,1,0:T(8,128)S(1)}, u32[]{:S(2)}, u32[]{:S(2)}) collective-permute-start(f32[17,4,8,128]{3,2,1,0:T(8,128)S(1)} %get-tuple-element.22), channel_id=1, source_target_pairs={{0,16},{16,0},{32,48},{48,32},{64,80},{80,64},{96,112},{112,96},{1... | collective-permute-start | bytes 835592 | tf_op jit(solution)/shard_map/ppermute | solution.py:403
  24.9 0.7 copy-start.14
  63.8 4.0 %collective-permute-start.3 = (f32[10,4,8,128]{3,2,1,0:T(8,128)}, f32[10,4,8,128]{3,2,1,0:T(8,128)S(1)}, u32[]{:S(2)}, u32[]{:S(2)}) collective-permute-start(f32[10,4,8,128]{3,2,1,0:T(8,128)} %get-tuple-element.26), channel_id=1, source_target_pairs={{0,16},{16,0},{32,48},{48,32},{64,80},{80,64},{96,112},{112,96},{1... | collective-permute-start | bytes 491528 | tf_op jit(solution)/shard_map/ppermute | solution.py:413
  67.8 1.7 %copy-start.3 = (f32[5,4,256,128]{3,2,1,0:T(8,128)S(1)}, f32[5,4,256,128]{3,2,1,0:T(8,128)}, u32[]{:S(2)}) copy-start(f32[5,4,256,128]{3,2,1,0:T(8,128)} %copy-done.2) | copy-start | bytes 7864324
  69.5 0.9 %copy-start.13 = (f32[10,4,8,128]{3,2,1,0:T(8,128)S(1)}, f32[10,4,8,128]{3,2,1,0:T(8,128)}, u32[]{:S(2)}) copy-start(f32[10,4,8,128]{3,2,1,0:T(8,128)} %get-tuple-element.25.mine) | copy-start | bytes 491524
where the time goes:
time: 74.2 us; the launch traced here: 72.8 us
  blocking collectives  32.5 us (44%)
  Pallas kernels  14.8 us (20%)
  starting transfers between devices  10.1 us (14%)
  local copies, waits for them, and re-layouts  9.27 us (12%)
  waiting for transfers between devices  5.98 us (8%)
    all_to_all x1, blocking collectives, on_device(): lax.all_to_all(sent.reshape(CHIPS, LAYERS * SENT, 128), 'chan', 0, 0, axi...  20.5 us
    all_to_all x1, blocking collectives, on_device(): lax.all_to_all(solved.reshape(CHIPS, LAYERS * BACK, 128), 'chan', 0, 0, a...  12.1 us
    unnamed x30, local copies, waits for them, and re-layouts  9.27 us
    pallas_call x1, Pallas kernels, local_part(): pl.pallas_call(local_kernel, grid=(LAYERS,), in_specs=[pl.BlockSpec(memor...  4.84 us
    ppermute x2, starting transfers between devices, on_device(): other = lax.ppermute(theirs, 'chan', pairs)  4.82 us
    ppermute x1, starting transfers between devices, on_device(): lax.ppermute(highest, 'cross', [(i, i + 1) for i in range(count - 1)])  4.02 us
    ppermute x1, waiting for transfers between devices, on_device(): lax.ppermute(lowest, 'cross', [(i + 1, i) for i in range(count - 1)])  3.55 us
    ppermute x2, waiting for transfers between devices, on_device(): other = lax.ppermute(theirs, 'chan', pairs)  2.42 us
  transfers between devices with their start and end apart: 4, of which 3 were waited for; matrix products, arithmetic and copies ran while one was open for 0% of the time, Pallas kernels for 0%

commit v1 on v0

--- a/solution.py
+++ b/solution.py
@@ -16,6 +16,7 @@
 SENT = 18
 BACK = 10
 F32 = jnp.float32
+SMALL = pltpu.CompilerParams(vmem_limit_bytes=4 * 1024 * 1024)
 
 
 def folded(cells):
@@ -76,6 +77,7 @@
         ],
         out_specs=[pl.BlockSpec((LAYERS, 16, 128), lambda i: (0, 0, 0))] * 2,
         out_shape=[jax.ShapeDtypeStruct((LAYERS, 16, 128), F32)] * 2,
+        compiler_params=SMALL,
         name="edges",
     )(tracers, tracers, kappa_y, kappa_y, wet, wet, levels, levels)
 
@@ -83,18 +85,30 @@
 def local_kernel(
     core, tr, kx, ky, co, wet, lev, left, right, red, fill, rho, mine, theirs, side
 ):
-    layer = pl.program_id(0)
+    lax.fori_loop(
+        0,
+        LAYERS,
+        lambda layer, none: local_layer(
+            layer, core, tr, kx, ky, co, wet, lev, left, right, red, fill, rho, mine, theirs, side
+        ),
+        None,
+    )
+
+
+def local_layer(
+    layer, core, tr, kx, ky, co, wet, lev, left, right, red, fill, rho, mine, theirs, side
+):
     first_core = core[0] == 0
     lane = lax.broadcasted_iota(jnp.int32, (8, 128), 1)
     head, tail = lane == 0, lane == 127
 
     for i in range(2):
         rows = pl.ds(i * 8, 8)
-        lo, hi = left[0, rows, :], right[0, rows, :]
+        lo, hi = left[layer, rows, :], right[layer, rows, :]
 
         def cross_of(j):
             active = (wet[tile(i, j), :] > 0) & (lev[tile(i, j), :] > layer)
-            return jnp.where(active, ky[0, tile(i, j), :], 0.0)
+            return jnp.where(active, ky[layer, tile(i, j), :], 0.0)
 
         def ahead(now, following):
             return jnp.where(tail, pltpu.roll(following, 127, 1), pltpu.roll(now, 127, 1))
@@ -107,11 +121,11 @@
             faces.append(jnp.minimum(now, ahead(now, following)))
             now = following
         for t in range(TRACERS):
-            now = tr[t, 0, tile(i, 0), :]
+            now = tr[t, layer, tile(i, 0), :]
             shifted = pltpu.roll(now, 127, 1)
             before = first_face * (now - pltpu.roll(lo, (0 - t) % 128, 1))
             for j in range(16):
-                following = tr[t, 0, tile(i, j + 1), :] if j < 15 else pltpu.roll(hi, (0 - t) % 128, 1)
+                following = tr[t, layer, tile(i, j + 1), :] if j < 15 else pltpu.roll(hi, (0 - t) % 128, 1)
                 shifted_following = pltpu.roll(following, 127, 1)
                 flux = faces[j] * (jnp.where(tail, shifted_following, shifted) - now)
                 behind = pltpu.roll(flux, 1, 1)
@@ -126,7 +140,7 @@
             where = line(row, half)
             active = (wet[where, :] > 0) & (lev[where, :] > layer)
             act = jnp.where(active, 1.0, 0.0).astype(F32)
-            return act, kx[0, where, :] * act, co[0, where, :]
+            return act, kx[layer, where, :] * act, co[layer, where, :]
 
         out = [None] * PARTS
         act_prev, cd_prev, co_prev = load(0)
@@ -159,10 +173,10 @@
                 sums = [sums[t] + chain * reds[t] for t in range(TRACERS)]
                 sum_fill = sum_fill + chain * fill_row
                 chain = chain * rho_row
-            rho[0, where, :] = rho_row
-            fill[0, where, :] = fill_row
+            rho[layer, where, :] = rho_row
+            fill[layer, where, :] = fill_row
             for t in range(TRACERS):
-                red[t, 0, where, :] = reds[t]
+                red[t, layer, where, :] = reds[t]
             act_prev = act
             act, cd, cour = act_next, cd_next, co_next
             face_down = face_up
@@ -177,30 +191,16 @@
             out[RN + t] = side[t, line(ROWS - 1, half), :] + low * reds[t]
         halves.append(out)
     for part in range(PARTS):
-        mine[part, 0] = jnp.where(first_core, halves[0][part], halves[1][part])
-        theirs[part, 0] = jnp.where(first_core, halves[1][part], halves[0][part])
+        mine[part, layer] = jnp.where(first_core, halves[0][part], halves[1][part])
+        theirs[part, layer] = jnp.where(first_core, halves[1][part], halves[0][part])
 
 
 def local_part(core, tracers, kappa_x, kappa_y, courant, wet, levels, left, right):
-    layered = lambda *lead: pl.BlockSpec(lead + (1, 256, 128), lambda l, n=len(lead): (0,) * n + (l, 0, 0))
-    whole = pl.BlockSpec((256, 128), lambda l: (0, 0))
-    halo = pl.BlockSpec((1, 16, 128), lambda l: (l, 0, 0))
-    packed = pl.BlockSpec((PARTS, 1, 8, 128), lambda l: (0, l, 0, 0))
+    vmem = pl.BlockSpec(memory_space=pltpu.VMEM)
     return pl.pallas_call(
         local_kernel,
-        grid=(LAYERS,),
-        in_specs=[
-            pl.BlockSpec(memory_space=pltpu.SMEM),
-            layered(TRACERS),
-            layered(),
-            layered(),
-            layered(),
-            whole,
-            whole,
-            halo,
-            halo,
-        ],
-        out_specs=[layered(TRACERS), layered(), layered(), packed, packed],
+        in_specs=[pl.BlockSpec(memory_space=pltpu.SMEM)] + [vmem] * 8,
+        out_specs=[vmem] * 5,
         out_shape=[
             jax.ShapeDtypeStruct((TRACERS, LAYERS, 256, 128), F32),
             jax.ShapeDtypeStruct((LAYERS, 256, 128), F32),
@@ -209,7 +209,7 @@
             jax.ShapeDtypeStruct((PARTS, LAYERS, 8, 128), F32),
         ],
         scratch_shapes=[pltpu.VMEM((TRACERS, 256, 128), F32)],
-        compiler_params=pltpu.CompilerParams(vmem_limit_bytes=16 * 1024 * 1024),
+        compiler_params=pltpu.CompilerParams(vmem_limit_bytes=12 * 1024 * 1024),
         name="local_part",
     )(core, tracers, kappa_x, kappa_y, courant, wet, levels, left, right)
 
@@ -258,6 +258,7 @@
             jax.ShapeDtypeStruct((CHIPS * LAYERS * SENT, 128), F32),
             jax.ShapeDtypeStruct((14, LAYERS, 8, 128), F32),
         ],
+        compiler_params=SMALL,
         name="pair_part",
     )(core, mine, other)
 
@@ -310,6 +311,7 @@
         in_specs=[vmem],
         out_specs=vmem,
         out_shape=jax.ShapeDtypeStruct((CHIPS * LAYERS * BACK, 128), F32),
+        compiler_params=SMALL,
         name="chain_part",
     )(parts)
 
@@ -336,6 +338,7 @@
         in_specs=[pl.BlockSpec(memory_space=pltpu.SMEM), vmem, vmem],
         out_specs=[vmem, vmem],
         out_shape=[jax.ShapeDtypeStruct((BACK, LAYERS, 8, 128), F32)] * 2,
+        compiler_params=SMALL,
         name="middle_part",
     )(core, solved, kept)
 
@@ -375,7 +378,7 @@
         ],
         out_specs=layered(TRACERS),
         out_shape=jax.ShapeDtypeStruct((TRACERS, LAYERS, 256, 128), F32),
-        compiler_params=pltpu.CompilerParams(vmem_limit_bytes=16 * 1024 * 1024),
+        compiler_params=pltpu.CompilerParams(vmem_limit_bytes=12 * 1024 * 1024),
         name="final_part",
     )(core, red, fill, rho, mine, other)
 

time: 74.2 us -> 62.1 us (0.84)
  Pallas kernels: 14.8 us -> 7.28 us
  local copies, waits for them, and re-layouts: 9.27 us -> 6.68 us
  blocking collectives: 32.5 us -> 30.6 us
    unnamed x30 -> x20, local copies, waits for them, and re-layouts: 9.27 us -> 6.68 us
    pallas_call x1, Pallas kernels: 1.96 us -> 0.1 us  [pair_part(): pl.pallas_call(pair_kernel, in_specs=[pl.BlockSpec(memory_space=pltpu.SME...]
    pallas_call x1, Pallas kernels: 1.96 us -> 0.16 us  [edges(): pl.pallas_call(edges_kernel, grid=(1,), in_specs=[spec((TRACERS, LAYERS),...]
    pallas_call x1, Pallas kernels: 1.83 us -> 0.05 us  [middle_part(): pl.pallas_call(middle_kernel, in_specs=[pl.BlockSpec(memory_space=pltpu.S...]
    pallas_call x1, Pallas kernels: 1.83 us -> 0.19 us  [chain_part(): pl.pallas_call(chain_kernel, in_specs=[vmem], out_specs=vmem, out_shape=j...]
    all_to_all x1, blocking collectives: 12.1 us -> 10.4 us  [on_device(): lax.all_to_all(solved.reshape(CHIPS, LAYERS * BACK, 128), 'chan', 0, 0, a...]
where the time goes in v1:
time: 62.1 us; the launch traced here: 60.8 us
  blocking collectives  30.6 us (49%)
  starting transfers between devices  10.6 us (17%)
  Pallas kernels  7.28 us (12%)
  local copies, waits for them, and re-layouts  6.68 us (11%)
  waiting for transfers between devices  5.55 us (9%)
    all_to_all x1, blocking collectives, on_device(): lax.all_to_all(sent.reshape(CHIPS, LAYERS * SENT, 128), 'chan', 0, 0, axi...  20.2 us
    all_to_all x1, blocking collectives, on_device(): lax.all_to_all(solved.reshape(CHIPS, LAYERS * BACK, 128), 'chan', 0, 0, a...  10.4 us
    unnamed x20, local copies, waits for them, and re-layouts  6.68 us
    ppermute x2, starting transfers between devices, on_device(): other = lax.ppermute(theirs, 'chan', pairs)  4.99 us
    pallas_call x1, Pallas kernels, local_part(): pl.pallas_call(local_kernel, in_specs=[pl.BlockSpec(memory_space=pltpu.SM...  4.43 us
    ppermute x1, starting transfers between devices, on_device(): lax.ppermute(highest, 'cross', [(i, i + 1) for i in range(count - 1)])  4.29 us
    ppermute x1, waiting for transfers between devices, on_device(): lax.ppermute(lowest, 'cross', [(i + 1, i) for i in range(count - 1)])  3.34 us
    pallas_call x1, Pallas kernels, final_part(): pl.pallas_call(final_kernel, grid=(LAYERS,), in_specs=[pl.BlockSpec(memor...  2.36 us
  transfers between devices with their start and end apart: 4, of which 3 were waited for; matrix products, arithmetic and copies ran while one was open for 0% of the time, Pallas kernels for 0%

profile of v1, /device:TPU:1, one launch (start us, length us, event | category | flops | bytes accessed | tf_op | source)
XLA Modules:
  0.0 60.8 jit_solution(12529511227690147504)
XLA Ops:
  0.0 0.0 copy-start
  0.0 1.7 %copy-done = f32[5,4,16,2048]{3,2,1,0:T(8,128)S(1)} copy-done((f32[5,4,16,2048]{3,2,1,0:T(8,128)S(1)}, f32[5,4,16,2048]{3,2,1,0:T(8,128)}, u32[]{:S(2)}) %copy-start) | copy-done | bytes 2621464
  1.7 0.0 copy-start.2
  1.7 1.0 %copy-done.2 = f32[4,16,2048]{2,1,0:T(8,128)S(1)} copy-done((f32[4,16,2048]{2,1,0:T(8,128)S(1)}, f32[4,16,2048]{2,1,0:T(8,128)}, u32[]{:S(2)}) %copy-start.2) | copy-done | bytes 524312
  2.8 0.0 copy-start.4
  2.8 0.9 %copy-done.4 = s32[16,2048]{1,0:T(8,128)S(1)} copy-done((s32[16,2048]{1,0:T(8,128)S(1)}, s32[16,2048]{1,0:T(8,128)}, u32[]{:S(2)}) %copy-start.4) | copy-done | bytes 131096
  3.7 0.0 copy-start.6
  3.7 0.9 %copy-done.6 = s32[16,2048]{1,0:T(8,128)S(1)} copy-done((s32[16,2048]{1,0:T(8,128)S(1)}, s32[16,2048]{1,0:T(8,128)}, u32[]{:S(2)}) %copy-start.6) | copy-done | bytes 131096
  4.6 0.0 copy-start.1
  4.6 0.0 copy-start.3
  4.6 0.0 copy-start.5
  4.6 0.0 copy-start.7
  4.6 0.2 edges.1
  4.8 4.3 %collective-permute-start = (f32[4,16,128]{2,1,0:T(8,128)S(1)}, f32[4,16,128]{2,1,0:T(8,128)S(1)}, u32[]{:S(2)}, u32[]{:S(2)}) collective-permute-start(f32[4,16,128]{2,1,0:T(8,128)S(1)} %get-tuple-element.16), channel_id=1, source_target_pairs={{0,1},{1,2},{2,3},{3,4},{4,5},{5,6},{6,7},{7,8},{8,9},{9,10},{10,1... | collective-permute-start | bytes 98312 | tf_op jit(solution)/shard_map/ppermute | solution.py:393
  9.1 1.3 %collective-permute-start.1 = (f32[4,16,128]{2,1,0:T(8,128)S(1)}, f32[4,16,128]{2,1,0:T(8,128)S(1)}, u32[]{:S(2)}, u32[]{:S(2)}) collective-permute-start(f32[4,16,128]{2,1,0:T(8,128)S(1)} %get-tuple-element.17), channel_id=1, source_target_pairs={{1,0},{2,1},{3,2},{4,3},{5,4},{6,5},{7,6},{8,7},{9,8},{10,9},{11,1... | collective-permute-start | bytes 98312 | tf_op jit(solution)/shard_map/ppermute | solution.py:394
  10.4 0.0 collective-permute-done.left
  10.4 3.3 %collective-permute-done.1.right = f32[4,16,128]{2,1,0:T(8,128)S(1)} collective-permute-done((f32[4,16,128]{2,1,0:T(8,128)S(1)}, f32[4,16,128]{2,1,0:T(8,128)S(1)}, u32[]{:S(2)}, u32[]{:S(2)}) %collective-permute-start.1) | collective-permute-done | bytes 32800 | tf_op jit(solution)/shard_map/ppermute | solution.py:394
  13.7 0.0 copy-done.1
  13.7 0.0 copy-done.3
  13.7 0.0 copy-done.5
  13.7 0.0 copy-done.7
  13.8 0.0 copy-start.8
  13.8 1.0 %copy-done.8 = f32[4,16,2048]{2,1,0:T(8,128)S(1)} copy-done((f32[4,16,2048]{2,1,0:T(8,128)S(1)}, f32[4,16,2048]{2,1,0:T(8,128)}, u32[]{:S(2)}) %copy-start.8) | copy-done | bytes 524312
  14.8 0.0 copy-start.9
  14.8 1.0 %copy-done.9 = f32[4,16,2048]{2,1,0:T(8,128)S(1)} copy-done((f32[4,16,2048]{2,1,0:T(8,128)S(1)}, f32[4,16,2048]{2,1,0:T(8,128)}, u32[]{:S(2)}) %copy-start.9) | copy-done | bytes 524312
  15.8 4.4 %local_part.1 = (f32[5,4,256,128]{3,2,1,0:T(8,128)S(1)}, f32[4,256,128]{2,1,0:T(8,128)S(1)}, f32[4,256,128]{2,1,0:T(8,128)S(1)}, f32[17,4,8,128]{3,2,1,0:T(8,128)S(1)}, f32[17,4,8,128]{3,2,1,0:T(8,128)S(1)}) custom-call(s32[1]{0:T(128)} %bitcast.core, f32[5,4,256,128]{3,2,1,0:T(8,128)S(1)} %bitcast.40, f32[4,256,128]{2,1,0:T(8,128)S(1)} %bitcast.47, ...), custom_call_target="tpu_custom_call" | custom-call | tf_op jit(solution)/shard_map/local_part/pallas_call | solution.py:200
  20.3 2.2 %collective-permute-start.2 = (f32[17,4,8,128]{3,2,1,0:T(8,128)S(1)}, f32[17,4,8,128]{3,2,1,0:T(8,128)S(1)}, u32[]{:S(2)}, u32[]{:S(2)}) collective-permute-start(f32[17,4,8,128]{3,2,1,0:T(8,128)S(1)} %get-tuple-element.22), channel_id=1, source_target_pairs={{0,16},{16,0},{32,48},{48,32},{64,80},{80,64},{96,112},{112,96},{1... | collective-permute-start | bytes 835592 | tf_op jit(solution)/shard_map/ppermute | solution.py:406
  22.5 1.2 %collective-permute-done.2.other = f32[17,4,8,128]{3,2,1,0:T(8,128)S(1)} collective-permute-done((f32[17,4,8,128]{3,2,1,0:T(8,128)S(1)}, f32[17,4,8,128]{3,2,1,0:T(8,128)S(1)}, u32[]{:S(2)}, u32[]{:S(2)}) %collective-permute-start.2) | collective-permute-done | bytes 278560 | tf_op jit(solution)/shard_map/ppermute | solution.py:406
  23.7 0.1 pair_part.1
  23.8 20.2 %all_to_all.10 = f32[8,72,128]{2,1,0:T(8,128)S(1)} all-to-all(f32[8,72,128]{2,1,0:T(8,128)S(1)} %bitcast.49), channel_id=1, replica_groups={{0,32,64,96,128,160,192,224},{16,48,80,112,144,176,208,240},{1,33,65,97..., dimensions={0} | all-to-all | bytes 589824 | tf_op jit(solution)/shard_map/all_to_all | solution.py:408
  43.9 0.2 chain_part.1
  44.1 10.4 %all_to_all.11 = f32[8,40,128]{2,1,0:T(8,128)S(1)} all-to-all(f32[8,40,128]{2,1,0:T(8,128)S(1)} %bitcast.45), channel_id=1, replica_groups={{0,32,64,96,128,160,192,224},{16,48,80,112,144,176,208,240},{1,33,65,97..., dimensions={0} | all-to-all | bytes 327680 | tf_op jit(solution)/shard_map/all_to_all | solution.py:412
  54.6 2.8 %collective-permute-start.3 = (f32[10,4,8,128]{3,2,1,0:T(8,128)S(1)}, f32[10,4,8,128]{3,2,1,0:T(8,128)S(1)}, u32[]{:S(2)}, u32[]{:S(2)}) collective-permute-start(f32[10,4,8,128]{3,2,1,0:T(8,128)S(1)} %get-tuple-element.26), channel_id=1, source_target_pairs={{0,16},{16,0},{32,48},{48,32},{64,80},{80,64},{96,112},{112,96},{1... | collective-permute-start | bytes 491528 | tf_op jit(solution)/shard_map/ppermute | solution.py:416
  57.4 1.0 %collective-permute-done.3.other = f32[10,4,8,128]{3,2,1,0:T(8,128)S(1)} collective-permute-done((f32[10,4,8,128]{3,2,1,0:T(8,128)S(1)}, f32[10,4,8,128]{3,2,1,0:T(8,128)S(1)}, u32[]{:S(2)}, u32[]{:S(2)}) %collective-permute-start.3) | collective-permute-done | bytes 163872 | tf_op jit(solution)/shard_map/ppermute | solution.py:416
  58.5 2.4 %final_part.1 = f32[5,4,256,128]{3,2,1,0:T(8,128)} custom-call(s32[1]{0:T(128)} %bitcast.core, f32[5,4,256,128]{3,2,1,0:T(8,128)S(1)} %get-tuple-element.18.red, f32[4,256,128]{2,1,0:T(8,128)S(1)} %get-tuple-element.19.fill, f32[4,256,128]{2,1,0:T(8,128)S(1)} %get-tuple-element.20.rho, f32[10,4,8,128]{3,2,1,0:T(8,128)S(1)} %get-tuple-element.25.mine, ...), custom_call_target="tpu_custom_call" | custom-call | tf_op jit(solution)/shard_map/final_part/pallas_call | solution.py:368
  (1 shorter events, 0.0 us)
Async XLA Ops:
  0.0 1.7 %copy-start = (f32[5,4,16,2048]{3,2,1,0:T(8,128)S(1)}, f32[5,4,16,2048]{3,2,1,0:T(8,128)}, u32[]{:S(2)}) copy-start(f32[5,4,16,2048]{3,2,1,0:T(8,128)} %tr_hi.1) | copy-start | bytes 7864324
  1.7 1.0 %copy-start.2 = (f32[4,16,2048]{2,1,0:T(8,128)S(1)}, f32[4,16,2048]{2,1,0:T(8,128)}, u32[]{:S(2)}) copy-start(f32[4,16,2048]{2,1,0:T(8,128)} %ky_hi.1) | copy-start | bytes 1572868
  2.8 0.9 %copy-start.4 = (s32[16,2048]{1,0:T(8,128)S(1)}, s32[16,2048]{1,0:T(8,128)}, u32[]{:S(2)}) copy-start(s32[16,2048]{1,0:T(8,128)} %wet_hi.1) | copy-start | bytes 393220
  3.7 0.9 %copy-start.6 = (s32[16,2048]{1,0:T(8,128)S(1)}, s32[16,2048]{1,0:T(8,128)}, u32[]{:S(2)}) copy-start(s32[16,2048]{1,0:T(8,128)} %lev_hi.1) | copy-start | bytes 393220
  4.6 9.1 %copy-start.1 = (f32[5,4,16,2048]{3,2,1,0:T(8,128)S(1)}, f32[5,4,16,2048]{3,2,1,0:T(8,128)}, u32[]{:S(2)}) copy-start(f32[5,4,16,2048]{3,2,1,0:T(8,128)} %tr_hi.1) | copy-start | bytes 7864324
  4.6 9.1 %copy-start.3 = (f32[4,16,2048]{2,1,0:T(8,128)S(1)}, f32[4,16,2048]{2,1,0:T(8,128)}, u32[]{:S(2)}) copy-start(f32[4,16,2048]{2,1,0:T(8,128)} %ky_hi.1) | copy-start | bytes 1572868
  4.6 9.1 %copy-start.5 = (s32[16,2048]{1,0:T(8,128)S(1)}, s32[16,2048]{1,0:T(8,128)}, u32[]{:S(2)}) copy-start(s32[16,2048]{1,0:T(8,128)} %wet_hi.1) | copy-start | bytes 393220
  4.6 9.1 %copy-start.7 = (s32[16,2048]{1,0:T(8,128)S(1)}, s32[16,2048]{1,0:T(8,128)}, u32[]{:S(2)}) copy-start(s32[16,2048]{1,0:T(8,128)} %lev_hi.1) | copy-start | bytes 393220
  4.8 5.6 %collective-permute-start = (f32[4,16,128]{2,1,0:T(8,128)S(1)}, f32[4,16,128]{2,1,0:T(8,128)S(1)}, u32[]{:S(2)}, u32[]{:S(2)}) collective-permute-start(f32[4,16,128]{2,1,0:T(8,128)S(1)} %get-tuple-element.16), channel_id=1, source_target_pairs={{0,1},{1,2},{2,3},{3,4},{4,5},{5,6},{6,7},{7,8},{8,9},{9,10},{10,1... | collective-permute-start | bytes 98312 | tf_op jit(solution)/shard_map/ppermute | solution.py:393
  9.1 4.7 %collective-permute-start.1 = (f32[4,16,128]{2,1,0:T(8,128)S(1)}, f32[4,16,128]{2,1,0:T(8,128)S(1)}, u32[]{:S(2)}, u32[]{:S(2)}) collective-permute-start(f32[4,16,128]{2,1,0:T(8,128)S(1)} %get-tuple-element.17), channel_id=1, source_target_pairs={{1,0},{2,1},{3,2},{4,3},{5,4},{6,5},{7,6},{8,7},{9,8},{10,9},{11,1... | collective-permute-start | bytes 98312 | tf_op jit(solution)/shard_map/ppermute | solution.py:394
  13.8 1.0 %copy-start.8 = (f32[4,16,2048]{2,1,0:T(8,128)S(1)}, f32[4,16,2048]{2,1,0:T(8,128)}, u32[]{:S(2)}) copy-start(f32[4,16,2048]{2,1,0:T(8,128)} %param.7) | copy-start | bytes 1572868
  14.8 1.0 %copy-start.9 = (f32[4,16,2048]{2,1,0:T(8,128)S(1)}, f32[4,16,2048]{2,1,0:T(8,128)}, u32[]{:S(2)}) copy-start(f32[4,16,2048]{2,1,0:T(8,128)} %param.9) | copy-start | bytes 1572868
  20.3 3.4 %collective-permute-start.2 = (f32[17,4,8,128]{3,2,1,0:T(8,128)S(1)}, f32[17,4,8,128]{3,2,1,0:T(8,128)S(1)}, u32[]{:S(2)}, u32[]{:S(2)}) collective-permute-start(f32[17,4,8,128]{3,2,1,0:T(8,128)S(1)} %get-tuple-element.22), channel_id=1, source_target_pairs={{0,16},{16,0},{32,48},{48,32},{64,80},{80,64},{96,112},{112,96},{1... | collective-permute-start | bytes 835592 | tf_op jit(solution)/shard_map/ppermute | solution.py:406
  54.6 3.8 %collective-permute-start.3 = (f32[10,4,8,128]{3,2,1,0:T(8,128)S(1)}, f32[10,4,8,128]{3,2,1,0:T(8,128)S(1)}, u32[]{:S(2)}, u32[]{:S(2)}) collective-permute-start(f32[10,4,8,128]{3,2,1,0:T(8,128)S(1)} %get-tuple-element.26), channel_id=1, source_target_pairs={{0,16},{16,0},{32,48},{48,32},{64,80},{80,64},{96,112},{112,96},{1... | collective-permute-start | bytes 491528 | tf_op jit(solution)/shard_map/ppermute | solution.py:416

commit v2 on v1

--- a/solution.py
+++ b/solution.py
@@ -49,11 +49,10 @@
             for i in range(2):
                 rows = pl.ds(i * 8, 8)
                 active = (wet[rows, :] > 0) & (lev[rows, :] > l)
-                parts = [tr[t, l, rows, :] for t in range(TRACERS)]
-                parts.append(jnp.where(active, ky[l, rows, :], 0.0))
-                packed = jnp.zeros((8, 128), F32)
-                for t, part in enumerate(parts):
-                    packed = jnp.where(lane == t, pltpu.roll(part, (t - at) % 128, 1), packed)
+                cross = jnp.where(active, ky[l, rows, :], 0.0)
+                packed = jnp.where(lane < 64, 0.0, jnp.broadcast_to(cross[:, at : at + 1], (8, 128)))
+                for t in range(TRACERS):
+                    packed = jnp.where(lane == t, pltpu.roll(tr[t, l, rows, :], (t - at) % 128, 1), packed)
                 out[l, rows, :] = packed
 
 
@@ -79,32 +78,30 @@
         out_shape=[jax.ShapeDtypeStruct((LAYERS, 16, 128), F32)] * 2,
         compiler_params=SMALL,
         name="edges",
-    )(tracers, tracers, kappa_y, kappa_y, wet, wet, levels, levels)
+    )(*(pltpu.with_memory_space_constraint(x, pltpu.HBM) for x in (tracers, tracers, kappa_y, kappa_y, wet, wet, levels, levels)))
 
 
 def local_kernel(
-    core, tr, kx, ky, co, wet, lev, left, right, red, fill, rho, mine, theirs, side
+    core, tr, kx, ky, co, wet, lev, red, fill, rho, inv, gain, mine, theirs, side
 ):
     lax.fori_loop(
         0,
         LAYERS,
         lambda layer, none: local_layer(
-            layer, core, tr, kx, ky, co, wet, lev, left, right, red, fill, rho, mine, theirs, side
+            layer, core, tr, kx, ky, co, wet, lev, red, fill, rho, inv, gain, mine, theirs, side
         ),
         None,
     )
 
 
 def local_layer(
-    layer, core, tr, kx, ky, co, wet, lev, left, right, red, fill, rho, mine, theirs, side
+    layer, core, tr, kx, ky, co, wet, lev, red, fill, rho, inv, gain, mine, theirs, side
 ):
     first_core = core[0] == 0
     lane = lax.broadcasted_iota(jnp.int32, (8, 128), 1)
     head, tail = lane == 0, lane == 127
 
     for i in range(2):
-        rows = pl.ds(i * 8, 8)
-        lo, hi = left[layer, rows, :], right[layer, rows, :]
 
         def cross_of(j):
             active = (wet[tile(i, j), :] > 0) & (lev[tile(i, j), :] > layer)
@@ -115,19 +112,24 @@
 
         faces = []
         now = cross_of(0)
-        first_face = jnp.minimum(now, pltpu.roll(lo, (0 - TRACERS) % 128, 1))
         for j in range(16):
-            following = cross_of(j + 1) if j < 15 else pltpu.roll(hi, (0 - TRACERS) % 128, 1)
-            faces.append(jnp.minimum(now, ahead(now, following)))
-            now = following
+            if j < 15:
+                following = cross_of(j + 1)
+                faces.append(jnp.minimum(now, ahead(now, following)))
+                now = following
+            else:
+                faces.append(jnp.where(tail, 0.0, jnp.minimum(now, pltpu.roll(now, 127, 1))))
         for t in range(TRACERS):
             now = tr[t, layer, tile(i, 0), :]
             shifted = pltpu.roll(now, 127, 1)
-            before = first_face * (now - pltpu.roll(lo, (0 - t) % 128, 1))
+            before = jnp.zeros((8, 128), F32)
             for j in range(16):
-                following = tr[t, layer, tile(i, j + 1), :] if j < 15 else pltpu.roll(hi, (0 - t) % 128, 1)
-                shifted_following = pltpu.roll(following, 127, 1)
-                flux = faces[j] * (jnp.where(tail, shifted_following, shifted) - now)
+                if j < 15:
+                    following = tr[t, layer, tile(i, j + 1), :]
+                    shifted_following = pltpu.roll(following, 127, 1)
+                    flux = faces[j] * (jnp.where(tail, shifted_following, shifted) - now)
+                else:
+                    flux = faces[j] * (shifted - now)
                 behind = pltpu.roll(flux, 1, 1)
                 side[t, tile(i, j), :] = now + flux - jnp.where(head, before, behind)
                 before = behind
@@ -158,8 +160,8 @@
             if row == 1:
                 inverse = 1.0 / (1.0 + face_up + low)
                 rho_row = face_up * inverse
-                gain = low * inverse
-                fill_row = gain
+                gain_row = low * inverse
+                fill_row = gain_row
                 reds = [side[t, line(row, half), :] * inverse for t in range(TRACERS)]
                 sums = list(reds)
                 sum_fill = fill_row
@@ -167,20 +169,24 @@
             else:
                 inverse = 1.0 / (1.0 + face_up + low * (1.0 - rho_row))
                 rho_row = face_up * inverse
-                gain = low * inverse
-                fill_row = gain * fill_row
-                reds = [side[t, line(row, half), :] * inverse + gain * reds[t] for t in range(TRACERS)]
+                gain_row = low * inverse
+                fill_row = gain_row * fill_row
+                reds = [side[t, line(row, half), :] * inverse + gain_row * reds[t] for t in range(TRACERS)]
                 sums = [sums[t] + chain * reds[t] for t in range(TRACERS)]
                 sum_fill = sum_fill + chain * fill_row
                 chain = chain * rho_row
             rho[layer, where, :] = rho_row
             fill[layer, where, :] = fill_row
+            inv[layer, where, :] = inverse
+            gain[layer, where, :] = gain_row
             for t in range(TRACERS):
                 red[t, layer, where, :] = reds[t]
             act_prev = act
             act, cd, cour = act_next, cd_next, co_next
             face_down = face_up
         low = act * (face_down + cour * act_prev)
+        gain[layer, pl.ds(half * ROWS * 8, 8), :] = face_first
+        gain[layer, pl.ds((half * ROWS + ROWS - 1) * 8, 8), :] = low
         out[D0] = 1.0 + face_first * (1.0 - sum_fill)
         out[F0] = face_first * chain
         out[CDN] = cd
@@ -195,14 +201,16 @@
         theirs[part, layer] = jnp.where(first_core, halves[1][part], halves[0][part])
 
 
-def local_part(core, tracers, kappa_x, kappa_y, courant, wet, levels, left, right):
+def local_part(core, tracers, kappa_x, kappa_y, courant, wet, levels):
     vmem = pl.BlockSpec(memory_space=pltpu.VMEM)
     return pl.pallas_call(
         local_kernel,
-        in_specs=[pl.BlockSpec(memory_space=pltpu.SMEM)] + [vmem] * 8,
-        out_specs=[vmem] * 5,
+        in_specs=[pl.BlockSpec(memory_space=pltpu.SMEM)] + [vmem] * 6,
+        out_specs=[vmem] * 7,
         out_shape=[
             jax.ShapeDtypeStruct((TRACERS, LAYERS, 256, 128), F32),
+            jax.ShapeDtypeStruct((LAYERS, 256, 128), F32),
+            jax.ShapeDtypeStruct((LAYERS, 256, 128), F32),
             jax.ShapeDtypeStruct((LAYERS, 256, 128), F32),
             jax.ShapeDtypeStruct((LAYERS, 256, 128), F32),
             jax.ShapeDtypeStruct((PARTS, LAYERS, 8, 128), F32),
@@ -211,7 +219,73 @@
         scratch_shapes=[pltpu.VMEM((TRACERS, 256, 128), F32)],
         compiler_params=pltpu.CompilerParams(vmem_limit_bytes=12 * 1024 * 1024),
         name="local_part",
-    )(core, tracers, kappa_x, kappa_y, courant, wet, levels, left, right)
+    )(core, tracers, kappa_x, kappa_y, courant, wet, levels)
+
+
+def outer_kernel(
+    where_am_i, own_lo, own_hi, left, right, inv, gain, rho, mine_in, theirs_in, mine, theirs, fix_lo, fix_hi
+):
+    mine[...] = mine_in[...]
+    theirs[...] = theirs_in[...]
+    lane = lax.broadcasted_iota(jnp.int32, (LAYERS, 128), 1)
+    for e, (own, halo, fix) in enumerate(((own_lo, left, fix_lo), (own_hi, right, fix_hi))):
+        at, sub = (0, 0) if e == 0 else (127, 7)
+        inside = where_am_i[1 + e] > 0
+
+        def coefficient(ref, row):
+            values = ref[pl.ds((e * ROWS + row) * 8 + sub, LAYERS, stride=256), :]
+            return jnp.broadcast_to(values[:, at : at + 1], (LAYERS, 128))
+
+        deltas = []
+        for row in range(ROWS):
+            here = own[pl.ds(row, LAYERS, stride=ROWS), :]
+            there = jnp.where(inside, halo[pl.ds(row, LAYERS, stride=ROWS), :], 0.0)
+            face = pltpu.roll(jnp.minimum(here, there), 64, 1)
+            deltas.append(face * (there - here))
+        rhos = [None] + [coefficient(rho, row) for row in range(1, ROWS - 1)]
+        reds = [None] * ROWS
+        for row in range(1, ROWS - 1):
+            reds[row] = deltas[row] * coefficient(inv, row)
+            if row == 1:
+                total, chain = reds[1], rhos[1]
+            else:
+                reds[row] = reds[row] + coefficient(gain, row) * reds[row - 1]
+                total = total + chain * reds[row]
+                chain = chain * rhos[row]
+        first = deltas[0] + coefficient(gain, 0) * total
+        last = deltas[ROWS - 1] + coefficient(gain, ROWS - 1) * reds[ROWS - 2]
+        zero = jnp.zeros((LAYERS, 128), F32)
+        fix[pl.ds(0, LAYERS, stride=ROWS), :] = zero
+        fix[pl.ds(ROWS - 1, LAYERS, stride=ROWS), :] = zero
+        value = zero
+        for row in reversed(range(1, ROWS - 1)):
+            value = reds[row] + rhos[row] * value
+            fix[pl.ds(row, LAYERS, stride=ROWS), :] = value
+
+        def add_to(ref):
+            for t in range(TRACERS):
+                for part, change in ((R0 + t, first), (RN + t, last)):
+                    rows = pl.ds(part * LAYERS * 8 + sub, LAYERS, stride=8)
+                    ref[rows, :] = ref[rows, :] + jnp.where(lane == at, pltpu.roll(change, (at - t) % 128, 1), 0.0)
+
+        pl.when(where_am_i[0] == e)(lambda: add_to(mine))
+        pl.when(where_am_i[0] != e)(lambda: add_to(theirs))
+
+
+def outer_part(where_am_i, own_lo, own_hi, left, right, inv, gain, rho, mine, theirs):
+    vmem = pl.BlockSpec(memory_space=pltpu.VMEM)
+    flat = lambda x: x.reshape(-1, 128)
+    mine, theirs, fix_lo, fix_hi = pl.pallas_call(
+        outer_kernel,
+        in_specs=[pl.BlockSpec(memory_space=pltpu.SMEM)] + [vmem] * 9,
+        out_specs=[vmem] * 4,
+        out_shape=[jax.ShapeDtypeStruct((PARTS * LAYERS * 8, 128), F32)] * 2
+        + [jax.ShapeDtypeStruct((LAYERS * ROWS, 128), F32)] * 2,
+        compiler_params=SMALL,
+        name="outer_part",
+    )(where_am_i, *(flat(x) for x in (own_lo, own_hi, left, right, inv, gain, rho, mine, theirs)))
+    packed = (PARTS, LAYERS, 8, 128)
+    return mine.reshape(packed), theirs.reshape(packed), fix_lo, fix_hi
 
 
 def pair_kernel(core, mine, other, sent, kept):
@@ -343,7 +417,7 @@
     )(core, solved, kept)
 
 
-def final_kernel(core, red, fill, rho, mine, other, out):
+def final_kernel(core, red, fill, rho, mine, other, fix_lo, fix_hi, out):
     first_core = core[0] == 0
     for half in range(2):
         pick = (lambda k: jnp.where(first_core, mine[k, 0], other[k, 0])) if half == 0 else (
@@ -360,9 +434,17 @@
             for t in range(TRACERS):
                 cells[t] = red[t, 0, where, :] + fill_row * firsts[t] + rho_row * cells[t]
                 out[t, 0, line(row, half), :] = cells[t]
-
-
-def final_part(core, red, fill, rho, mine, other):
+    lane = lax.broadcasted_iota(jnp.int32, (8, 128), 1)
+    for i in range(2):
+        for fix, at, column in ((fix_lo, 0, 0), (fix_hi, 127, 15)):
+            change = fix[pl.ds(i * 8, 8), :]
+            for t in range(TRACERS):
+                where = tile(i, column)
+                moved = jnp.where(lane == at, pltpu.roll(change, (at - t) % 128, 1), 0.0)
+                out[t, 0, where, :] = out[t, 0, where, :] + moved
+
+
+def final_part(core, red, fill, rho, mine, other, fix_lo, fix_hi):
     layered = lambda *lead: pl.BlockSpec(lead + (1, 256, 128), lambda l, n=len(lead): (0,) * n + (l, 0, 0))
     packed = pl.BlockSpec((BACK, 1, 8, 128), lambda l: (0, l, 0, 0))
     return pl.pallas_call(
@@ -375,24 +457,27 @@
             layered(),
             packed,
             packed,
+            pl.BlockSpec((ROWS, 128), lambda l: (l, 0)),
+            pl.BlockSpec((ROWS, 128), lambda l: (l, 0)),
         ],
         out_specs=layered(TRACERS),
         out_shape=jax.ShapeDtypeStruct((TRACERS, LAYERS, 256, 128), F32),
         compiler_params=pltpu.CompilerParams(vmem_limit_bytes=12 * 1024 * 1024),
         name="final_part",
-    )(core, red, fill, rho, mine, other)
+    )(core, red, fill, rho, mine, other, fix_lo, fix_hi)
 
 
 def on_device(tracers, kappa_x, kappa_y, courant, wet_mask, levels):
     count = lax.axis_size("cross")
-    core = (lax.axis_index("chan") % 2).astype(jnp.int32).reshape(1)
+    along, across = lax.axis_index("chan"), lax.axis_index("cross")
+    core = jnp.stack([along % 2, across > 0, across < count - 1]).astype(jnp.int32)
     pairs = [(i, i ^ 1) for i in range(2 * CHIPS)]
     lines = [[c + 2 * z for z in range(CHIPS)] for c in range(2)]
 
     lowest, highest = edges(tracers, kappa_y, wet_mask, levels)
-    left = lax.ppermute(highest, "cross", [(i, i + 1) for i in range(count - 1)])
-    right = lax.ppermute(lowest, "cross", [(i + 1, i) for i in range(count - 1)])
-    red, fill, rho, mine, theirs = local_part(
+    left = lax.ppermute(highest, "cross", [(i, (i + 1) % count) for i in range(count)])
+    right = lax.ppermute(lowest, "cross", [((i + 1) % count, i) for i in range(count)])
+    red, fill, rho, inv, gain, mine, theirs = local_part(
         core,
         folded(tracers),
         folded(kappa_x),
@@ -400,8 +485,9 @@
         folded(courant),
         folded(wet_mask),
         folded(levels),
-        left,
-        right,
+    )
+    mine, theirs, fix_lo, fix_hi = outer_part(
+        core, lowest, highest, left, right, inv, gain, rho, mine, theirs
     )
     other = lax.ppermute(theirs, "chan", pairs)
     sent, kept = pair_part(core, mine, other)
@@ -414,7 +500,7 @@
     )
     mine, theirs = middle_part(core, back.reshape(CHIPS * LAYERS * BACK, 128), kept)
     other = lax.ppermute(theirs, "chan", pairs)
-    return unfolded(final_part(core, red, fill, rho, mine, other))
+    return unfolded(final_part(core, red, fill, rho, mine, other, fix_lo, fix_hi))
 
 
 def solution(mesh):

time: 62.1 us -> 56.6 us (0.911); the launches traced: 60.8 us -> 56.4 us
  local copies, waits for them, and re-layouts: 6.68 us -> 2.09 us
  Pallas kernels: 7.28 us -> 11.5 us
  waiting for transfers between devices: 5.55 us -> 2.22 us
  starting transfers between devices: 10.6 us -> 9.78 us
    unnamed x20 -> x12, local copies, waits for them, and re-layouts: 6.68 us -> 2.09 us
    ppermute x2, waiting for transfers between devices: 3.34 us -> 0.01 us  [the longest x1 0.01 us: on_device(): lax.ppermute(lowest, 'cross', [((i + 1) % count, i) for i in range(count)])]
    pallas_call x1, Pallas kernels: 0.16 us -> 1.35 us  [edges(): pl.pallas_call(edges_kernel, grid=(1,), in_specs=[spec((TRACERS, LAYERS),...]
    ppermute x2, starting transfers between devices: 4.99 us -> 3.94 us  [on_device(): other = lax.ppermute(theirs, 'chan', pairs)]
    pallas_call x0 -> x1, Pallas kernels: none -> 1 us  [outer_part(): pl.pallas_call(outer_kernel, in_specs=[pl.BlockSpec(memory_space=pltpu.SM...]
  transfers between devices with their start and end apart: 4 -> 4, of which waited for: 3 -> 2; matrix products, arithmetic and copies ran while one was open for 0% -> 0% of each run, Pallas kernels for 0% -> 9%
where the time goes in v2:
time: 56.6 us; the launch traced here: 56.4 us
  blocking collectives  30.6 us (54%)
  Pallas kernels  11.5 us (20%)
  starting transfers between devices  9.78 us (17%)
  waiting for transfers between devices  2.22 us (4%)
  local copies, waits for them, and re-layouts  2.09 us (4%)
    all_to_all x1, blocking collectives, on_device(): lax.all_to_all(sent.reshape(CHIPS, LAYERS * SENT, 128), 'chan', 0, 0, axi...  20.2 us
    all_to_all x1, blocking collectives, on_device(): lax.all_to_all(solved.reshape(CHIPS, LAYERS * BACK, 128), 'chan', 0, 0, a...  10.4 us
    ppermute x1, starting transfers between devices, on_device(): lax.ppermute(lowest, 'cross', [((i + 1) % count, i) for i in range(count)])  5.84 us
    pallas_call x1, Pallas kernels, local_part(): pl.pallas_call(local_kernel, in_specs=[pl.BlockSpec(memory_space=pltpu.SM...  4.9 us
    ppermute x2, starting transfers between devices, on_device(): other = lax.ppermute(theirs, 'chan', pairs)  3.94 us
    pallas_call x1, Pallas kernels, final_part(): pl.pallas_call(final_kernel, grid=(LAYERS,), in_specs=[pl.BlockSpec(memor...  2.87 us
    ppermute x2, waiting for transfers between devices, on_device(): other = lax.ppermute(theirs, 'chan', pairs)  2.21 us
    unnamed x12, local copies, waits for them, and re-layouts  2.09 us
  transfers between devices with their start and end apart: 4, of which 2 were waited for; matrix products, arithmetic and copies ran while one was open for 0% of the time, Pallas kernels for 9%

profile of v2, /device:TPU:1, one launch (start us, length us, event | category | flops | bytes accessed | tf_op | source)
XLA Modules:
  0.0 56.4 jit_solution(16148340742531876036)
XLA Ops:
  0.0 0.0 copy-start.3
  0.0 0.0 copy-start.2
  0.0 0.0 copy-start.1
  0.0 0.0 copy-start
  0.0 1.3 %edges.1 = (f32[4,16,128]{2,1,0:T(8,128)S(1)}, f32[4,16,128]{2,1,0:T(8,128)S(1)}) custom-call(f32[5,4,16,2048]{3,2,1,0:T(8,128)} %tr_hi.1, f32[5,4,16,2048]{3,2,1,0:T(8,128)} %tr_hi.1, f32[4,16,2048]{2,1,0:T(8,128)} %ky_hi.1, f32[4,16,2048]{2,1,0:T(8,128)} %ky_hi.1, s32[16,2048]{1,0:T(8,128)} %wet_hi.1, s32[16,2048]{1,0:T(8,128)} %wet_hi.1, ...), custom_call_target="tpu_custom_call" | custom-call | tf_op jit(solution)/shard_map/edges/pallas_call | solution.py:64
  1.4 5.8 %collective-permute-start.1 = (f32[4,16,128]{2,1,0:T(8,128)S(1)}, f32[4,16,128]{2,1,0:T(8,128)S(1)}, u32[]{:S(2)}, u32[]{:S(2)}) collective-permute-start(f32[4,16,128]{2,1,0:T(8,128)S(1)} %get-tuple-element.25), channel_id=1, source_target_pairs={{1,0},{2,1},{3,2},{4,3},{5,4},{6,5},{7,6},{8,7},{9,8},{10,9},{11,1... | collective-permute-start | bytes 98312 | tf_op jit(solution)/shard_map/ppermute | solution.py:479
  7.2 0.0 collective-permute-start
  7.2 0.1 pad_add_fusion.core.where_am_i
  7.3 0.0 copy-done.3
  7.3 0.0 copy-done.2
  7.3 0.0 copy-done.1
  7.3 0.0 copy-done
  7.3 0.0 copy-start.4
  7.3 1.0 %copy-done.4 = f32[4,16,2048]{2,1,0:T(8,128)S(1)} copy-done((f32[4,16,2048]{2,1,0:T(8,128)S(1)}, f32[4,16,2048]{2,1,0:T(8,128)}, u32[]{:S(2)}) %copy-start.4) | copy-done | bytes 524312
  8.4 0.0 copy-start.5
  8.4 1.0 %copy-done.5 = f32[4,16,2048]{2,1,0:T(8,128)S(1)} copy-done((f32[4,16,2048]{2,1,0:T(8,128)S(1)}, f32[4,16,2048]{2,1,0:T(8,128)}, u32[]{:S(2)}) %copy-start.5) | copy-done | bytes 524312
  9.4 4.9 %local_part.1 = (f32[5,4,256,128]{3,2,1,0:T(8,128)S(1)}, f32[4,256,128]{2,1,0:T(8,128)S(1)}, f32[4,256,128]{2,1,0:T(8,128)S(1)}, f32[4,256,128]{2,1,0:T(8,128)S(...) custom-call(s32[3]{0:T(128)S(1)} %pad_add_fusion.core.where_am_i, ...), custom_call_target="tpu_custom_call" | custom-call | tf_op jit(solution)/shard_map/local_part/pallas_call | solution.py:206
  14.3 0.0 collective-permute-done.1
  14.3 0.0 collective-permute-done
  14.3 1.0 %outer_part.1 = (f32[544,128]{1,0:T(8,128)S(1)}, f32[544,128]{1,0:T(8,128)S(1)}, f32[64,128]{1,0:T(8,128)S(1)}, f32[64,128]{1,0:T(8,128)S(1)}) custom-call(s32[3]{0:T(128)S(1)} %pad_add_fusion.core.where_am_i, f32[64,128]{1,0:T(8,128)S(1)} %bitcast.69, f32[64,128]{1,0:T(8,128)S(1)} %bitcast.70, f32[64,128]{1,0:T(8,128)S(1)} %bitcast.72, ...), custom_call_target="tpu_custom_call" | custom-call | tf_op jit(solution)/shard_map/outer_part/pallas_call | solution.py:278
  15.3 1.1 %collective-permute-start.2 = (f32[17,4,8,128]{3,2,1,0:T(8,128)S(1)}, f32[17,4,8,128]{3,2,1,0:T(8,128)S(1)}, u32[]{:S(2)}, u32[]{:S(2)}) collective-permute-start(f32[17,4,8,128]{3,2,1,0:T(8,128)S(1)} %bitcast.73), channel_id=1, source_target_pairs={{0,16},{16,0},{32,48},{48,32},{64,80},{80,64},{96,112},{112,96},{1... | collective-permute-start | bytes 835592 | tf_op jit(solution)/shard_map/ppermute | solution.py:492
  16.5 1.2 %collective-permute-done.2.other = f32[17,4,8,128]{3,2,1,0:T(8,128)S(1)} collective-permute-done((f32[17,4,8,128]{3,2,1,0:T(8,128)S(1)}, f32[17,4,8,128]{3,2,1,0:T(8,128)S(1)}, u32[]{:S(2)}, u32[]{:S(2)}) %collective-permute-start.2) | collective-permute-done | bytes 278560 | tf_op jit(solution)/shard_map/ppermute | solution.py:492
  17.7 0.6 %pair_part.1 = (f32[576,128]{1,0:T(8,128)S(1)}, f32[14,4,8,128]{3,2,1,0:T(8,128)S(1)}) custom-call(s32[3]{0:T(128)S(1)} %pad_add_fusion.core.where_am_i, f32[17,4,8,128]{3,2,1,0:T(8,128)S(1)} %bitcast.68, f32[17,4,8,128]{3,2,1,0:T(8,128)S(1)} %collective-permute-done.2.other), custom_call_target="tpu_custom_call" | custom-call | tf_op jit(solution)/shard_map/pair_part/pallas_call | solution.py:327
  18.3 20.2 %all_to_all.10 = f32[8,72,128]{2,1,0:T(8,128)S(1)} all-to-all(f32[8,72,128]{2,1,0:T(8,128)S(1)} %bitcast.65), channel_id=1, replica_groups={{0,32,64,96,128,160,192,224},{16,48,80,112,144,176,208,240},{1,33,65,97..., dimensions={0} | all-to-all | bytes 589824 | tf_op jit(solution)/shard_map/all_to_all | solution.py:494
  38.5 0.2 chain_part.1
  38.7 10.4 %all_to_all.11 = f32[8,40,128]{2,1,0:T(8,128)S(1)} all-to-all(f32[8,40,128]{2,1,0:T(8,128)S(1)} %bitcast.59), channel_id=1, replica_groups={{0,32,64,96,128,160,192,224},{16,48,80,112,144,176,208,240},{1,33,65,97..., dimensions={0} | all-to-all | bytes 327680 | tf_op jit(solution)/shard_map/all_to_all | solution.py:498
  49.1 0.6 %middle_part.1 = (f32[10,4,8,128]{3,2,1,0:T(8,128)S(1)}, f32[10,4,8,128]{3,2,1,0:T(8,128)S(1)}) custom-call(s32[3]{0:T(128)S(1)} %pad_add_fusion.core.where_am_i, f32[320,128]{1,0:T(8,128)S(1)} %bitcast.60, f32[14,4,8,128]{3,2,1,0:T(8,128)S(1)} %get-tuple-element.34.kept), custom_call_target="tpu_custom_call" | custom-call | tf_op jit(solution)/shard_map/middle_part/pallas_call | solution.py:410
  49.7 2.8 %collective-permute-start.3 = (f32[10,4,8,128]{3,2,1,0:T(8,128)S(1)}, f32[10,4,8,128]{3,2,1,0:T(8,128)S(1)}, u32[]{:S(2)}, u32[]{:S(2)}) collective-permute-start(f32[10,4,8,128]{3,2,1,0:T(8,128)S(1)} %get-tuple-element.36), channel_id=1, source_target_pairs={{0,16},{16,0},{32,48},{48,32},{64,80},{80,64},{96,112},{112,96},{1... | collective-permute-start | bytes 491528 | tf_op jit(solution)/shard_map/ppermute | solution.py:502
  52.5 1.0 %collective-permute-done.3.other = f32[10,4,8,128]{3,2,1,0:T(8,128)S(1)} collective-permute-done((f32[10,4,8,128]{3,2,1,0:T(8,128)S(1)}, f32[10,4,8,128]{3,2,1,0:T(8,128)S(1)}, u32[]{:S(2)}, u32[]{:S(2)}) %collective-permute-start.3) | collective-permute-done | bytes 163872 | tf_op jit(solution)/shard_map/ppermute | solution.py:502
  53.5 2.9 %final_part.1 = f32[5,4,256,128]{3,2,1,0:T(8,128)} custom-call(s32[3]{0:T(128)S(1)} %pad_add_fusion.core.where_am_i, f32[5,4,256,128]{3,2,1,0:T(8,128)S(1)} %get-tuple-element.22.red, f32[4,256,128]{2,1,0:T(8,128)S(1)} %get-tuple-element.23.fill, f32[4,256,128]{2,1,0:T(8,128)S(1)} %get-tuple-element.24.rho, f32[10,4,8,128]{3,2,1,0:T(8,128)S(1)} %get-tuple-element.35.mine, ...), custom_call_target="tpu_custom_call" | custom-call | tf_op jit(solution)/shard_map/final_part/pallas_call | solution.py:450
Async XLA Ops:
  0.0 7.3 %copy-start.3 = (s32[16,2048]{1,0:T(8,128)S(1)}, s32[16,2048]{1,0:T(8,128)}, u32[]{:S(2)}) copy-start(s32[16,2048]{1,0:T(8,128)} %lev_hi.1) | copy-start | bytes 393220
  0.0 7.3 %copy-start.2 = (s32[16,2048]{1,0:T(8,128)S(1)}, s32[16,2048]{1,0:T(8,128)}, u32[]{:S(2)}) copy-start(s32[16,2048]{1,0:T(8,128)} %wet_hi.1) | copy-start | bytes 393220
  0.0 7.3 %copy-start.1 = (f32[4,16,2048]{2,1,0:T(8,128)S(1)}, f32[4,16,2048]{2,1,0:T(8,128)}, u32[]{:S(2)}) copy-start(f32[4,16,2048]{2,1,0:T(8,128)} %ky_hi.1) | copy-start | bytes 1572868
  0.0 7.3 %copy-start = (f32[5,4,16,2048]{3,2,1,0:T(8,128)S(1)}, f32[5,4,16,2048]{3,2,1,0:T(8,128)}, u32[]{:S(2)}) copy-start(f32[5,4,16,2048]{3,2,1,0:T(8,128)} %tr_hi.1) | copy-start | bytes 7864324
  1.4 12.9 %collective-permute-start.1 = (f32[4,16,128]{2,1,0:T(8,128)S(1)}, f32[4,16,128]{2,1,0:T(8,128)S(1)}, u32[]{:S(2)}, u32[]{:S(2)}) collective-permute-start(f32[4,16,128]{2,1,0:T(8,128)S(1)} %get-tuple-element.25), channel_id=1, source_target_pairs={{1,0},{2,1},{3,2},{4,3},{5,4},{6,5},{7,6},{8,7},{9,8},{10,9},{11,1... | collective-permute-start | bytes 98312 | tf_op jit(solution)/shard_map/ppermute | solution.py:479
  7.2 7.1 %collective-permute-start = (f32[4,16,128]{2,1,0:T(8,128)S(1)}, f32[4,16,128]{2,1,0:T(8,128)S(1)}, u32[]{:S(2)}, u32[]{:S(2)}) collective-permute-start(f32[4,16,128]{2,1,0:T(8,128)S(1)} %get-tuple-element.26), channel_id=1, source_target_pairs={{0,1},{1,2},{2,3},{3,4},{4,5},{5,6},{6,7},{7,8},{8,9},{9,10},{10,1... | collective-permute-start | bytes 98312 | tf_op jit(solution)/shard_map/ppermute | solution.py:478
  7.3 1.0 %copy-start.4 = (f32[4,16,2048]{2,1,0:T(8,128)S(1)}, f32[4,16,2048]{2,1,0:T(8,128)}, u32[]{:S(2)}) copy-start(f32[4,16,2048]{2,1,0:T(8,128)} %param.7) | copy-start | bytes 1572868
  8.4 1.0 %copy-start.5 = (f32[4,16,2048]{2,1,0:T(8,128)S(1)}, f32[4,16,2048]{2,1,0:T(8,128)}, u32[]{:S(2)}) copy-start(f32[4,16,2048]{2,1,0:T(8,128)} %param.9) | copy-start | bytes 1572868
  15.3 2.3 %collective-permute-start.2 = (f32[17,4,8,128]{3,2,1,0:T(8,128)S(1)}, f32[17,4,8,128]{3,2,1,0:T(8,128)S(1)}, u32[]{:S(2)}, u32[]{:S(2)}) collective-permute-start(f32[17,4,8,128]{3,2,1,0:T(8,128)S(1)} %bitcast.73), channel_id=1, source_target_pairs={{0,16},{16,0},{32,48},{48,32},{64,80},{80,64},{96,112},{112,96},{1... | collective-permute-start | bytes 835592 | tf_op jit(solution)/shard_map/ppermute | solution.py:492
  49.7 3.8 %collective-permute-start.3 = (f32[10,4,8,128]{3,2,1,0:T(8,128)S(1)}, f32[10,4,8,128]{3,2,1,0:T(8,128)S(1)}, u32[]{:S(2)}, u32[]{:S(2)}) collective-permute-start(f32[10,4,8,128]{3,2,1,0:T(8,128)S(1)} %get-tuple-element.36), channel_id=1, source_target_pairs={{0,16},{16,0},{32,48},{48,32},{64,80},{80,64},{96,112},{112,96},{1... | collective-permute-start | bytes 491528 | tf_op jit(solution)/shard_map/ppermute | solution.py:502

commit v3 on v2

--- a/solution.py
+++ b/solution.py
@@ -31,8 +31,16 @@
     return jnp.swapaxes(cells, len(lead) + 1, len(lead) + 2).reshape(lead + (16, 2048))
 
 
+def in_hbm(cells):
+    return pltpu.with_memory_space_constraint(cells, pltpu.HBM)
+
+
 def line(row, half):
     return pl.ds((row // 8) * 128 + half * 64 + row % 8, 8, stride=8)
+
+
+def is_first_core():
+    return lax.axis_index("chan") % 2 == 0
 
 
 def tile(row_tile, column_tile):
@@ -78,26 +86,32 @@
         out_shape=[jax.ShapeDtypeStruct((LAYERS, 16, 128), F32)] * 2,
         compiler_params=SMALL,
         name="edges",
-    )(*(pltpu.with_memory_space_constraint(x, pltpu.HBM) for x in (tracers, tracers, kappa_y, kappa_y, wet, wet, levels, levels)))
+    )(*(in_hbm(x) for x in (tracers, tracers, kappa_y, kappa_y, wet, wet, levels, levels)))
 
 
 def local_kernel(
-    core, tr, kx, ky, co, wet, lev, red, fill, rho, inv, gain, mine, theirs, side
+    tr, kx_hbm, ky, co_hbm, wet, lev, red, fill, rho, inv, gain, mine, theirs, side, kx, co, sems
 ):
-    lax.fori_loop(
-        0,
-        LAYERS,
-        lambda layer, none: local_layer(
-            layer, core, tr, kx, ky, co, wet, lev, red, fill, rho, inv, gain, mine, theirs, side
-        ),
-        None,
-    )
-
-
-def local_layer(
-    layer, core, tr, kx, ky, co, wet, lev, red, fill, rho, inv, gain, mine, theirs, side
-):
-    first_core = core[0] == 0
+    copies = [
+        pltpu.make_async_copy(kx_hbm, kx, sems.at[0]),
+        pltpu.make_async_copy(co_hbm, co, sems.at[1]),
+    ]
+    for copy in copies:
+        copy.start()
+    def one(layer, none):
+        right_sides(layer, tr, ky, wet, lev, side)
+
+        @pl.when(layer == 0)
+        def _():
+            for copy in copies:
+                copy.wait()
+
+        eliminate(layer, kx, co, wet, lev, red, fill, rho, inv, gain, mine, theirs, side)
+
+    lax.fori_loop(0, LAYERS, one, None)
+
+
+def right_sides(layer, tr, ky, wet, lev, side):
     lane = lax.broadcasted_iota(jnp.int32, (8, 128), 1)
     head, tail = lane == 0, lane == 127
 
@@ -135,6 +149,9 @@
                 before = behind
                 now, shifted = following, shifted_following
 
+
+def eliminate(layer, kx, co, wet, lev, red, fill, rho, inv, gain, mine, theirs, side):
+    first_core = is_first_core()
     halves = []
     for half in range(2):
 
@@ -201,36 +218,38 @@
         theirs[part, layer] = jnp.where(first_core, halves[1][part], halves[0][part])
 
 
-def local_part(core, tracers, kappa_x, kappa_y, courant, wet, levels):
-    vmem = pl.BlockSpec(memory_space=pltpu.VMEM)
+def local_part(tracers, kappa_x, kappa_y, courant, wet, levels):
+    vmem = pl.BlockSpec(memory_space=pltpu.VMEM)
+    hbm = pl.BlockSpec(memory_space=pltpu.HBM)
+    layered = jax.ShapeDtypeStruct((LAYERS, 256, 128), F32)
+    packed = jax.ShapeDtypeStruct((PARTS, LAYERS, 8, 128), F32)
     return pl.pallas_call(
         local_kernel,
-        in_specs=[pl.BlockSpec(memory_space=pltpu.SMEM)] + [vmem] * 6,
+        in_specs=[vmem, hbm, vmem, hbm, vmem, vmem],
         out_specs=[vmem] * 7,
-        out_shape=[
-            jax.ShapeDtypeStruct((TRACERS, LAYERS, 256, 128), F32),
-            jax.ShapeDtypeStruct((LAYERS, 256, 128), F32),
-            jax.ShapeDtypeStruct((LAYERS, 256, 128), F32),
-            jax.ShapeDtypeStruct((LAYERS, 256, 128), F32),
-            jax.ShapeDtypeStruct((LAYERS, 256, 128), F32),
-            jax.ShapeDtypeStruct((PARTS, LAYERS, 8, 128), F32),
-            jax.ShapeDtypeStruct((PARTS, LAYERS, 8, 128), F32),
+        out_shape=[jax.ShapeDtypeStruct((TRACERS, LAYERS, 256, 128), F32)] + [layered] * 4 + [packed] * 2,
+        scratch_shapes=[
+            pltpu.VMEM((TRACERS, 256, 128), F32),
+            pltpu.VMEM((LAYERS, 256, 128), F32),
+            pltpu.VMEM((LAYERS, 256, 128), F32),
+            pltpu.SemaphoreType.DMA((2,)),
         ],
-        scratch_shapes=[pltpu.VMEM((TRACERS, 256, 128), F32)],
         compiler_params=pltpu.CompilerParams(vmem_limit_bytes=12 * 1024 * 1024),
         name="local_part",
-    )(core, tracers, kappa_x, kappa_y, courant, wet, levels)
+    )(tracers, in_hbm(kappa_x), kappa_y, in_hbm(courant), wet, levels)
 
 
 def outer_kernel(
-    where_am_i, own_lo, own_hi, left, right, inv, gain, rho, mine_in, theirs_in, mine, theirs, fix_lo, fix_hi
+    own_lo, own_hi, left, right, inv, gain, rho, mine_in, theirs_in, mine, theirs, fix_lo, fix_hi
 ):
+    place = lax.axis_index("cross")
+    first_core = is_first_core()
     mine[...] = mine_in[...]
     theirs[...] = theirs_in[...]
     lane = lax.broadcasted_iota(jnp.int32, (LAYERS, 128), 1)
     for e, (own, halo, fix) in enumerate(((own_lo, left, fix_lo), (own_hi, right, fix_hi))):
         at, sub = (0, 0) if e == 0 else (127, 7)
-        inside = where_am_i[1 + e] > 0
+        inside = (place > 0) if e == 0 else (place < lax.axis_size("cross") - 1)
 
         def coefficient(ref, row):
             values = ref[pl.ds((e * ROWS + row) * 8 + sub, LAYERS, stride=256), :]
@@ -268,28 +287,28 @@
                     rows = pl.ds(part * LAYERS * 8 + sub, LAYERS, stride=8)
                     ref[rows, :] = ref[rows, :] + jnp.where(lane == at, pltpu.roll(change, (at - t) % 128, 1), 0.0)
 
-        pl.when(where_am_i[0] == e)(lambda: add_to(mine))
-        pl.when(where_am_i[0] != e)(lambda: add_to(theirs))
-
-
-def outer_part(where_am_i, own_lo, own_hi, left, right, inv, gain, rho, mine, theirs):
+        pl.when(first_core if e == 0 else jnp.logical_not(first_core))(lambda: add_to(mine))
+        pl.when(jnp.logical_not(first_core) if e == 0 else first_core)(lambda: add_to(theirs))
+
+
+def outer_part(own_lo, own_hi, left, right, inv, gain, rho, mine, theirs):
     vmem = pl.BlockSpec(memory_space=pltpu.VMEM)
     flat = lambda x: x.reshape(-1, 128)
     mine, theirs, fix_lo, fix_hi = pl.pallas_call(
         outer_kernel,
-        in_specs=[pl.BlockSpec(memory_space=pltpu.SMEM)] + [vmem] * 9,
+        in_specs=[vmem] * 9,
         out_specs=[vmem] * 4,
         out_shape=[jax.ShapeDtypeStruct((PARTS * LAYERS * 8, 128), F32)] * 2
         + [jax.ShapeDtypeStruct((LAYERS * ROWS, 128), F32)] * 2,
         compiler_params=SMALL,
         name="outer_part",
-    )(where_am_i, *(flat(x) for x in (own_lo, own_hi, left, right, inv, gain, rho, mine, theirs)))
+    )(*(flat(x) for x in (own_lo, own_hi, left, right, inv, gain, rho, mine, theirs)))
     packed = (PARTS, LAYERS, 8, 128)
     return mine.reshape(packed), theirs.reshape(packed), fix_lo, fix_hi
 
 
-def pair_kernel(core, mine, other, sent, kept):
-    first_core = core[0] == 0
+def pair_kernel(mine, other, sent, kept):
+    first_core = is_first_core()
     for l in range(LAYERS):
         a = [mine[part, l] for part in range(PARTS)]
         b = [other[part, l] for part in range(PARTS)]
@@ -322,11 +341,11 @@
             kept[k, l] = value
 
 
-def pair_part(core, mine, other):
+def pair_part(mine, other):
     vmem = pl.BlockSpec(memory_space=pltpu.VMEM)
     return pl.pallas_call(
         pair_kernel,
-        in_specs=[pl.BlockSpec(memory_space=pltpu.SMEM), vmem, vmem],
+        in_specs=[vmem, vmem],
         out_specs=[vmem, vmem],
         out_shape=[
             jax.ShapeDtypeStruct((CHIPS * LAYERS * SENT, 128), F32),
@@ -334,7 +353,7 @@
         ],
         compiler_params=SMALL,
         name="pair_part",
-    )(core, mine, other)
+    )(mine, other)
 
 
 def chain_kernel(parts, solved):
@@ -390,8 +409,8 @@
     )(parts)
 
 
-def middle_kernel(core, solved, kept, mine, theirs):
-    first_core = core[0] == 0
+def middle_kernel(solved, kept, mine, theirs):
+    first_core = is_first_core()
     for l in range(LAYERS):
         last_f, last_l, first_f, first_l = (kept[10 + k, l] for k in range(4))
         for t in range(TRACERS):
@@ -405,72 +424,112 @@
             theirs[TRACERS + t, l] = jnp.where(first_core, last, before)
 
 
-def middle_part(core, solved, kept):
+def middle_part(solved, kept):
     vmem = pl.BlockSpec(memory_space=pltpu.VMEM)
     return pl.pallas_call(
         middle_kernel,
-        in_specs=[pl.BlockSpec(memory_space=pltpu.SMEM), vmem, vmem],
+        in_specs=[vmem, vmem],
         out_specs=[vmem, vmem],
         out_shape=[jax.ShapeDtypeStruct((BACK, LAYERS, 8, 128), F32)] * 2,
         compiler_params=SMALL,
         name="middle_part",
-    )(core, solved, kept)
-
-
-def final_kernel(core, red, fill, rho, mine, other, fix_lo, fix_hi, out):
-    first_core = core[0] == 0
-    for half in range(2):
-        pick = (lambda k: jnp.where(first_core, mine[k, 0], other[k, 0])) if half == 0 else (
-            lambda k: jnp.where(first_core, other[k, 0], mine[k, 0])
-        )
-        firsts = [pick(t) for t in range(TRACERS)]
-        cells = [pick(TRACERS + t) for t in range(TRACERS)]
-        for t in range(TRACERS):
-            out[t, 0, line(ROWS - 1, half), :] = cells[t]
-            out[t, 0, line(0, half), :] = firsts[t]
-        for row in reversed(range(1, ROWS - 1)):
-            where = pl.ds((half * ROWS + row) * 8, 8)
-            fill_row, rho_row = fill[0, where, :], rho[0, where, :]
-            for t in range(TRACERS):
-                cells[t] = red[t, 0, where, :] + fill_row * firsts[t] + rho_row * cells[t]
-                out[t, 0, line(row, half), :] = cells[t]
+    )(solved, kept)
+
+
+def spread_kernel(red, fill, rho, fix_lo, fix_hi, base, of_first, of_last):
     lane = lax.broadcasted_iota(jnp.int32, (8, 128), 1)
-    for i in range(2):
-        for fix, at, column in ((fix_lo, 0, 0), (fix_hi, 127, 15)):
-            change = fix[pl.ds(i * 8, 8), :]
-            for t in range(TRACERS):
-                where = tile(i, column)
-                moved = jnp.where(lane == at, pltpu.roll(change, (at - t) % 128, 1), 0.0)
-                out[t, 0, where, :] = out[t, 0, where, :] + moved
-
-
-def final_part(core, red, fill, rho, mine, other, fix_lo, fix_hi):
-    layered = lambda *lead: pl.BlockSpec(lead + (1, 256, 128), lambda l, n=len(lead): (0,) * n + (l, 0, 0))
-    packed = pl.BlockSpec((BACK, 1, 8, 128), lambda l: (0, l, 0, 0))
+    zero, one = jnp.zeros((8, 128), F32), jnp.ones((8, 128), F32)
+
+    def one_layer(layer, none):
+        for half in range(2):
+            for row, first, last in ((0, one, zero), (ROWS - 1, zero, one)):
+                of_first[layer, line(row, half), :] = first
+                of_last[layer, line(row, half), :] = last
+                for t in range(TRACERS):
+                    base[t, layer, line(row, half), :] = zero
+            values, first, last = [zero] * TRACERS, zero, one
+            for row in reversed(range(1, ROWS - 1)):
+                where = pl.ds((half * ROWS + row) * 8, 8)
+                ratio = rho[layer, where, :]
+                first = fill[layer, where, :] + ratio * first
+                last = ratio * last
+                of_first[layer, line(row, half), :] = first
+                of_last[layer, line(row, half), :] = last
+                for t in range(TRACERS):
+                    values[t] = red[t, layer, where, :] + ratio * values[t]
+                    base[t, layer, line(row, half), :] = values[t]
+        for i in range(2):
+            for fix, at, column in ((fix_lo, 0, 0), (fix_hi, 127, 15)):
+                change = fix[pl.ds(layer * ROWS + i * 8, 8), :]
+                for t in range(TRACERS):
+                    where = tile(i, column)
+                    moved = jnp.where(lane == at, pltpu.roll(change, (at - t) % 128, 1), 0.0)
+                    base[t, layer, where, :] = base[t, layer, where, :] + moved
+
+    lax.fori_loop(0, LAYERS, one_layer, None)
+
+
+def spread_part(red, fill, rho, fix_lo, fix_hi):
+    vmem = pl.BlockSpec(memory_space=pltpu.VMEM)
+    layered = jax.ShapeDtypeStruct((LAYERS, 256, 128), F32)
+    return pl.pallas_call(
+        spread_kernel,
+        in_specs=[vmem] * 5,
+        out_specs=[vmem] * 3,
+        out_shape=[jax.ShapeDtypeStruct((TRACERS, LAYERS, 256, 128), F32), layered, layered],
+        compiler_params=pltpu.CompilerParams(vmem_limit_bytes=12 * 1024 * 1024),
+        name="spread_part",
+    )(red, fill, rho, fix_lo, fix_hi)
+
+
+def final_kernel(base, of_first, of_last, mine, other, out, ready, sems):
+    first_core = is_first_core()
+
+    def copy_of(layer):
+        return pltpu.make_async_copy(ready.at[:, layer], out.at[:, layer], sems.at[layer])
+
+    def one_layer(layer, none):
+        def fill_in(low, high):
+            for half, ends in ((0, low), (1, high)):
+                for j in range(8):
+                    spread = lambda k: jnp.broadcast_to(ends[k, layer, pl.ds(j, 1), :], (8, 128))
+                    firsts = [spread(t) for t in range(TRACERS)]
+                    lasts = [spread(TRACERS + t) for t in range(TRACERS)]
+                    for i in range(2):
+                        where = tile(i, half * 8 + j)
+                        by_first, by_last = of_first[layer, where, :], of_last[layer, where, :]
+                        for t in range(TRACERS):
+                            ready[t, layer, where, :] = (
+                                base[t, layer, where, :] + by_first * firsts[t] + by_last * lasts[t]
+                            )
+
+        pl.when(first_core)(lambda: fill_in(mine, other))
+        pl.when(jnp.logical_not(first_core))(lambda: fill_in(other, mine))
+        copy_of(layer).start()
+
+    lax.fori_loop(0, LAYERS, one_layer, None)
+    for layer in range(LAYERS):
+        copy_of(layer).wait()
+
+
+def final_part(base, of_first, of_last, mine, other):
+    vmem = pl.BlockSpec(memory_space=pltpu.VMEM)
     return pl.pallas_call(
         final_kernel,
-        grid=(LAYERS,),
-        in_specs=[
-            pl.BlockSpec(memory_space=pltpu.SMEM),
-            layered(TRACERS),
-            layered(),
-            layered(),
-            packed,
-            packed,
-            pl.BlockSpec((ROWS, 128), lambda l: (l, 0)),
-            pl.BlockSpec((ROWS, 128), lambda l: (l, 0)),
+        in_specs=[vmem] * 5,
+        out_specs=pl.BlockSpec(memory_space=pltpu.HBM),
+        out_shape=jax.ShapeDtypeStruct((TRACERS, LAYERS, 256, 128), F32),
+        scratch_shapes=[
+            pltpu.VMEM((TRACERS, LAYERS, 256, 128), F32),
+            pltpu.SemaphoreType.DMA((LAYERS,)),
         ],
-        out_specs=layered(TRACERS),
-        out_shape=jax.ShapeDtypeStruct((TRACERS, LAYERS, 256, 128), F32),
         compiler_params=pltpu.CompilerParams(vmem_limit_bytes=12 * 1024 * 1024),
         name="final_part",
-    )(core, red, fill, rho, mine, other, fix_lo, fix_hi)
+    )(base, of_first, of_last, mine, other)
 
 
 def on_device(tracers, kappa_x, kappa_y, courant, wet_mask, levels):
     count = lax.axis_size("cross")
-    along, across = lax.axis_index("chan"), lax.axis_index("cross")
-    core = jnp.stack([along % 2, across > 0, across < count - 1]).astype(jnp.int32)
     pairs = [(i, i ^ 1) for i in range(2 * CHIPS)]
     lines = [[c + 2 * z for z in range(CHIPS)] for c in range(2)]
 
@@ -478,7 +537,6 @@
     left = lax.ppermute(highest, "cross", [(i, (i + 1) % count) for i in range(count)])
     right = lax.ppermute(lowest, "cross", [((i + 1) % count, i) for i in range(count)])
     red, fill, rho, inv, gain, mine, theirs = local_part(
-        core,
         folded(tracers),
         folded(kappa_x),
         folded(kappa_y),
@@ -487,10 +545,11 @@
         folded(levels),
     )
     mine, theirs, fix_lo, fix_hi = outer_part(
-        core, lowest, highest, left, right, inv, gain, rho, mine, theirs
+        lowest, highest, left, right, inv, gain, rho, mine, theirs
     )
     other = lax.ppermute(theirs, "chan", pairs)
-    sent, kept = pair_part(core, mine, other)
+    base, of_first, of_last = spread_part(red, fill, rho, fix_lo, fix_hi)
+    sent, kept = pair_part(mine, other)
     parts = lax.all_to_all(
         sent.reshape(CHIPS, LAYERS * SENT, 128), "chan", 0, 0, axis_index_groups=lines, tiled=True
     )
@@ -498,9 +557,9 @@
     back = lax.all_to_all(
         solved.reshape(CHIPS, LAYERS * BACK, 128), "chan", 0, 0, axis_index_groups=lines, tiled=True
     )
-    mine, theirs = middle_part(core, back.reshape(CHIPS * LAYERS * BACK, 128), kept)
+    mine, theirs = middle_part(back.reshape(CHIPS * LAYERS * BACK, 128), kept)
     other = lax.ppermute(theirs, "chan", pairs)
-    return unfolded(final_part(core, red, fill, rho, mine, other, fix_lo, fix_hi))
+    return unfolded(final_part(base, of_first, of_last, mine, other))
 
 
 def solution(mesh):

time: 56.6 us -> 52.1 us (0.920)
  local copies, waits for them, and re-layouts: 2.09 us -> 0.02 us
  starting transfers between devices: 9.78 us -> 11.5 us
  blocking collectives: 30.6 us -> 28.9 us
  Pallas kernels: 11.5 us -> 9.82 us
  waiting for transfers between devices: 2.22 us -> 1.59 us
    ppermute x1, starting transfers between devices: 0.01 us -> 2.2 us  [on_device(): lax.ppermute(highest, 'cross', [(i, (i + 1) % count) for i in range(count)])]
    ppermute x1, starting transfers between devices: 5.84 us -> 3.72 us  [on_device(): lax.ppermute(lowest, 'cross', [((i + 1) % count, i) for i in range(count)])]
    unnamed x12 -> x8, local copies, waits for them, and re-layouts: 2.09 us -> 0.02 us
    all_to_all x1, blocking collectives: 20.2 us -> 18.5 us  [on_device(): lax.all_to_all(sent.reshape(CHIPS, LAYERS * SENT, 128), 'chan', 0, 0, axi...]
    pallas_call x5 -> x6, Pallas kernels: 9.99 us -> 8.29 us  [the longest x1 5.43 us: local_part(): pl.pallas_call(local_kernel, in_specs=[vmem, hbm, vmem, hbm, vmem, vmem],...]
    ppermute x2, starting transfers between devices: 3.94 us -> 5.62 us  [on_device(): other = lax.ppermute(theirs, 'chan', pairs)]
    ppermute x2, waiting for transfers between devices: 2.21 us -> 1.59 us  [on_device(): other = lax.ppermute(theirs, 'chan', pairs)]
  transfers between devices with their start and end apart: 4 -> 4, of which waited for: 2 -> 2; matrix products, arithmetic and copies ran while one was open for 0% -> 0% of each run, Pallas kernels for 9% -> 12%
where the time goes in v3:
time: 52.1 us; the launch traced here: 52 us
  blocking collectives  28.9 us (55%)
  starting transfers between devices  11.5 us (22%)
  Pallas kernels  9.82 us (19%)
  waiting for transfers between devices  1.59 us (3%)
    all_to_all x1, blocking collectives, on_device(): lax.all_to_all(sent.reshape(CHIPS, LAYERS * SENT, 128), 'chan', 0, 0, axi...  18.5 us
    all_to_all x1, blocking collectives, on_device(): lax.all_to_all(solved.reshape(CHIPS, LAYERS * BACK, 128), 'chan', 0, 0, a...  10.4 us
    ppermute x2, starting transfers between devices, on_device(): other = lax.ppermute(theirs, 'chan', pairs)  5.62 us
    pallas_call x1, Pallas kernels, local_part(): pl.pallas_call(local_kernel, in_specs=[vmem, hbm, vmem, hbm, vmem, vmem],...  5.43 us
    ppermute x1, starting transfers between devices, on_device(): lax.ppermute(lowest, 'cross', [((i + 1) % count, i) for i in range(count)])  3.72 us
    ppermute x1, starting transfers between devices, on_device(): lax.ppermute(highest, 'cross', [(i, (i + 1) % count) for i in range(count)])  2.2 us
    pallas_call x1, Pallas kernels, final_part(): pl.pallas_call(final_kernel, in_specs=[vmem] * 5, out_specs=pl.BlockSpec(...  1.62 us
    ppermute x2, waiting for transfers between devices, on_device(): other = lax.ppermute(theirs, 'chan', pairs)  1.59 us
  transfers between devices with their start and end apart: 4, of which 2 were waited for; matrix products, arithmetic and copies ran while one was open for 0% of the time, Pallas kernels for 12%

profile of v3, /device:TPU:1, one launch (start us, length us, event | category | flops | bytes accessed | tf_op | source)
XLA Modules:
  0.0 52.0 jit_solution(15704412656549595083)
XLA Ops:
  0.0 0.0 copy-start.2
  0.0 0.0 copy-start.3
  0.0 0.0 copy-start
  0.0 0.0 copy-start.1
  0.0 1.3 %edges.1 = (f32[4,16,128]{2,1,0:T(8,128)S(1)}, f32[4,16,128]{2,1,0:T(8,128)S(1)}) custom-call(f32[5,4,16,2048]{3,2,1,0:T(8,128)} %tr_hi.1, f32[5,4,16,2048]{3,2,1,0:T(8,128)} %tr_hi.1, f32[4,16,2048]{2,1,0:T(8,128)} %ky_hi.1, f32[4,16,2048]{2,1,0:T(8,128)} %ky_hi.1, s32[16,2048]{1,0:T(8,128)} %wet_hi.1, s32[16,2048]{1,0:T(8,128)} %wet_hi.1, ...), custom_call_target="tpu_custom_call" | custom-call | tf_op jit(solution)/shard_map/edges/pallas_call | solution.py:72
  1.4 2.2 %collective-permute-start = (f32[4,16,128]{2,1,0:T(8,128)S(1)}, f32[4,16,128]{2,1,0:T(8,128)S(1)}, u32[]{:S(2)}, u32[]{:S(2)}) collective-permute-start(f32[4,16,128]{2,1,0:T(8,128)S(1)} %get-tuple-element.29), channel_id=1, source_target_pairs={{0,1},{1,2},{2,3},{3,4},{4,5},{5,6},{6,7},{7,8},{8,9},{9,10},{10,1... | collective-permute-start | bytes 98312 | tf_op jit(solution)/shard_map/ppermute | solution.py:537
  3.6 3.7 %collective-permute-start.1 = (f32[4,16,128]{2,1,0:T(8,128)S(1)}, f32[4,16,128]{2,1,0:T(8,128)S(1)}, u32[]{:S(2)}, u32[]{:S(2)}) collective-permute-start(f32[4,16,128]{2,1,0:T(8,128)S(1)} %get-tuple-element.28), channel_id=1, source_target_pairs={{1,0},{2,1},{3,2},{4,3},{5,4},{6,5},{7,6},{8,7},{9,8},{10,9},{11,1... | collective-permute-start | bytes 98312 | tf_op jit(solution)/shard_map/ppermute | solution.py:538
  7.3 0.0 copy-done.2
  7.3 0.0 copy-done.3
  7.3 0.0 copy-done
  7.3 0.0 copy-done.1
  7.3 5.4 %local_part.1 = (f32[5,4,256,128]{3,2,1,0:T(8,128)S(1)}, f32[4,256,128]{2,1,0:T(8,128)S(1)}, f32[4,256,128]{2,1,0:T(8,128)S(1)}, f32[4,256,128]{2,1,0:T(8,128)S(...) custom-call(f32[5,4,256,128]{3,2,1,0:T(8,128)S(1)} %bitcast.50, ...), custom_call_target="tpu_custom_call" | custom-call | tf_op jit(solution)/shard_map/local_part/pallas_call | solution.py:226
  12.7 0.0 collective-permute-done
  12.8 0.0 collective-permute-done.1
  12.8 0.5 outer_part.1
  13.2 2.8 %collective-permute-start.2 = (f32[17,4,8,128]{3,2,1,0:T(8,128)S(1)}, f32[17,4,8,128]{3,2,1,0:T(8,128)S(1)}, u32[]{:S(2)}, u32[]{:S(2)}) collective-permute-start(f32[17,4,8,128]{3,2,1,0:T(8,128)S(1)} %bitcast.68), channel_id=1, source_target_pairs={{0,16},{16,0},{32,48},{48,32},{64,80},{80,64},{96,112},{112,96},{1... | collective-permute-start | bytes 835592 | tf_op jit(solution)/shard_map/ppermute | solution.py:550
  16.0 1.2 %collective-permute-done.2.other = f32[17,4,8,128]{3,2,1,0:T(8,128)S(1)} collective-permute-done((f32[17,4,8,128]{3,2,1,0:T(8,128)S(1)}, f32[17,4,8,128]{3,2,1,0:T(8,128)S(1)}, u32[]{:S(2)}, u32[]{:S(2)}) %collective-permute-start.2) | collective-permute-done | bytes 278560 | tf_op jit(solution)/shard_map/ppermute | solution.py:550
  17.2 0.1 pair_part.1
  17.3 18.5 %all_to_all.10 = f32[8,72,128]{2,1,0:T(8,128)S(1)} all-to-all(f32[8,72,128]{2,1,0:T(8,128)S(1)} %bitcast.60), channel_id=1, replica_groups={{0,32,64,96,128,160,192,224},{16,48,80,112,144,176,208,240},{1,33,65,97..., dimensions={0} | all-to-all | bytes 589824 | tf_op jit(solution)/shard_map/all_to_all | solution.py:553
  35.8 0.2 chain_part.1
  36.0 10.4 %all_to_all.11 = f32[8,40,128]{2,1,0:T(8,128)S(1)} all-to-all(f32[8,40,128]{2,1,0:T(8,128)S(1)} %bitcast.56), channel_id=1, replica_groups={{0,32,64,96,128,160,192,224},{16,48,80,112,144,176,208,240},{1,33,65,97..., dimensions={0} | all-to-all | bytes 327680 | tf_op jit(solution)/shard_map/all_to_all | solution.py:557
  46.4 0.1 middle_part.1
  46.5 2.8 %collective-permute-start.3 = (f32[10,4,8,128]{3,2,1,0:T(8,128)S(1)}, f32[10,4,8,128]{3,2,1,0:T(8,128)S(1)}, u32[]{:S(2)}, u32[]{:S(2)}) collective-permute-start(f32[10,4,8,128]{3,2,1,0:T(8,128)S(1)} %get-tuple-element.44), channel_id=1, source_target_pairs={{0,16},{16,0},{32,48},{48,32},{64,80},{80,64},{96,112},{112,96},{1... | collective-permute-start | bytes 491528 | tf_op jit(solution)/shard_map/ppermute | solution.py:561
  49.3 0.6 %spread_part.1 = (f32[5,4,256,128]{3,2,1,0:T(8,128)S(1)}, f32[4,256,128]{2,1,0:T(8,128)S(1)}, f32[4,256,128]{2,1,0:T(8,128)S(1)}) custom-call(f32[5,4,256,128]{3,2,1,0:T(8,128)S(1)} %get-tuple-element.25.red, f32[4,256,128]{2,1,0:T(8,128)S(1)} %get-tuple-element.26.fill, f32[4,256,128]{2,1,0:T(8,128)S(1)} %get-tuple-element.27.rho, ...), custom_call_target="tpu_custom_call" | custom-call | tf_op jit(solution)/shard_map/spread_part/pallas_call | solution.py:475
  49.9 0.4 collective-permute-done.3.other
  50.3 1.6 %final_part.1 = f32[5,4,256,128]{3,2,1,0:T(8,128)} custom-call(f32[5,4,256,128]{3,2,1,0:T(8,128)S(1)} %get-tuple-element.36.base, f32[4,256,128]{2,1,0:T(8,128)S(1)} %get-tuple-element.37.of_first, f32[4,256,128]{2,1,0:T(8,128)S(1)} %get-tuple-element.38.of_last, f32[10,4,8,128]{3,2,1,0:T(8,128)S(1)} %get-tuple-element.43.mine, ...), custom_call_target="tpu_custom_call" | custom-call | tf_op jit(solution)/shard_map/final_part/pallas_call | solution.py:517
Async XLA Ops:
  0.0 7.3 %copy-start.2 = (s32[16,2048]{1,0:T(8,128)S(1)}, s32[16,2048]{1,0:T(8,128)}, u32[]{:S(2)}) copy-start(s32[16,2048]{1,0:T(8,128)} %wet_hi.1) | copy-start | bytes 393220
  0.0 7.3 %copy-start.3 = (s32[16,2048]{1,0:T(8,128)S(1)}, s32[16,2048]{1,0:T(8,128)}, u32[]{:S(2)}) copy-start(s32[16,2048]{1,0:T(8,128)} %lev_hi.1) | copy-start | bytes 393220
  0.0 7.3 %copy-start = (f32[5,4,16,2048]{3,2,1,0:T(8,128)S(1)}, f32[5,4,16,2048]{3,2,1,0:T(8,128)}, u32[]{:S(2)}) copy-start(f32[5,4,16,2048]{3,2,1,0:T(8,128)} %tr_hi.1) | copy-start | bytes 7864324
  0.0 7.3 %copy-start.1 = (f32[4,16,2048]{2,1,0:T(8,128)S(1)}, f32[4,16,2048]{2,1,0:T(8,128)}, u32[]{:S(2)}) copy-start(f32[4,16,2048]{2,1,0:T(8,128)} %ky_hi.1) | copy-start | bytes 1572868
  1.4 11.4 %collective-permute-start = (f32[4,16,128]{2,1,0:T(8,128)S(1)}, f32[4,16,128]{2,1,0:T(8,128)S(1)}, u32[]{:S(2)}, u32[]{:S(2)}) collective-permute-start(f32[4,16,128]{2,1,0:T(8,128)S(1)} %get-tuple-element.29), channel_id=1, source_target_pairs={{0,1},{1,2},{2,3},{3,4},{4,5},{5,6},{6,7},{7,8},{8,9},{9,10},{10,1... | collective-permute-start | bytes 98312 | tf_op jit(solution)/shard_map/ppermute | solution.py:537
  3.6 9.2 %collective-permute-start.1 = (f32[4,16,128]{2,1,0:T(8,128)S(1)}, f32[4,16,128]{2,1,0:T(8,128)S(1)}, u32[]{:S(2)}, u32[]{:S(2)}) collective-permute-start(f32[4,16,128]{2,1,0:T(8,128)S(1)} %get-tuple-element.28), channel_id=1, source_target_pairs={{1,0},{2,1},{3,2},{4,3},{5,4},{6,5},{7,6},{8,7},{9,8},{10,9},{11,1... | collective-permute-start | bytes 98312 | tf_op jit(solution)/shard_map/ppermute | solution.py:538
  13.2 4.0 %collective-permute-start.2 = (f32[17,4,8,128]{3,2,1,0:T(8,128)S(1)}, f32[17,4,8,128]{3,2,1,0:T(8,128)S(1)}, u32[]{:S(2)}, u32[]{:S(2)}) collective-permute-start(f32[17,4,8,128]{3,2,1,0:T(8,128)S(1)} %bitcast.68), channel_id=1, source_target_pairs={{0,16},{16,0},{32,48},{48,32},{64,80},{80,64},{96,112},{112,96},{1... | collective-permute-start | bytes 835592 | tf_op jit(solution)/shard_map/ppermute | solution.py:550
  46.5 3.8 %collective-permute-start.3 = (f32[10,4,8,128]{3,2,1,0:T(8,128)S(1)}, f32[10,4,8,128]{3,2,1,0:T(8,128)S(1)}, u32[]{:S(2)}, u32[]{:S(2)}) collective-permute-start(f32[10,4,8,128]{3,2,1,0:T(8,128)S(1)} %get-tuple-element.44), channel_id=1, source_target_pairs={{0,16},{16,0},{32,48},{48,32},{64,80},{80,64},{96,112},{112,96},{1... | collective-permute-start | bytes 491528 | tf_op jit(solution)/shard_map/ppermute | solution.py:561

commit v4 on v3

--- a/solution.py
+++ b/solution.py
@@ -90,7 +90,7 @@
 
 
 def local_kernel(
-    tr, kx_hbm, ky, co_hbm, wet, lev, red, fill, rho, inv, gain, mine, theirs, side, kx, co, sems
+    tr, kx_hbm, ky, co_hbm, wet, lev, red, fill, rho, inv, gain, mine, theirs, side, kx, co, shift, moved, sems
 ):
     copies = [
         pltpu.make_async_copy(kx_hbm, kx, sems.at[0]),
@@ -98,124 +98,163 @@
     ]
     for copy in copies:
         copy.start()
-    def one(layer, none):
-        right_sides(layer, tr, ky, wet, lev, side)
-
-        @pl.when(layer == 0)
-        def _():
-            for copy in copies:
-                copy.wait()
-
-        eliminate(layer, kx, co, wet, lev, red, fill, rho, inv, gain, mine, theirs, side)
-
-    lax.fori_loop(0, LAYERS, one, None)
-
-
-def right_sides(layer, tr, ky, wet, lev, side):
+    source = lax.broadcasted_iota(jnp.int32, (256, 256), 0) % 128
+    target = lax.broadcasted_iota(jnp.int32, (256, 256), 1)
+    wanted = jnp.where(target < 128, target + 1, target + 127) % 128
+    shift[...] = jnp.where(source == wanted, 1.0, 0.0).astype(jnp.bfloat16)
+    lax.fori_loop(
+        0, LAYERS, lambda layer, none: right_sides(layer, tr, ky, wet, lev, side, shift, moved), None
+    )
+    for copy in copies:
+        copy.wait()
+    eliminate_bands(kx, co, wet, lev, fill, rho, inv, gain, mine, theirs)
+    lax.fori_loop(
+        0, LAYERS, lambda layer, none: eliminate_sides(layer, red, rho, inv, gain, mine, theirs, side), None
+    )
+
+
+def right_sides(layer, tr, ky, wet, lev, side, shift, moved):
     lane = lax.broadcasted_iota(jnp.int32, (8, 128), 1)
     head, tail = lane == 0, lane == 127
 
+    def move(k, cells):
+        coarse = cells.astype(jnp.bfloat16)
+        rest = (cells - coarse.astype(F32)).astype(jnp.bfloat16)
+        moved[k] = jnp.dot(
+            jnp.concatenate([coarse, rest], axis=1), shift[...], preferred_element_type=F32
+        )
+
+    def ahead(k, i, j):
+        here = moved[k, tile(i, j), 0:128]
+        return here if j == 15 else jnp.where(tail, moved[k, tile(i, j + 1), 0:128], here)
+
+    def behind(k, i, j):
+        here = moved[k, tile(i, j), 128:256]
+        return here if j == 0 else jnp.where(head, moved[k, tile(i, j - 1), 128:256], here)
+
+    cross = jnp.where((wet[...] > 0) & (lev[...] > layer), ky[layer], 0.0)
+    move(TRACERS, cross)
+    for t in range(TRACERS):
+        move(t, tr[t, layer])
     for i in range(2):
-
-        def cross_of(j):
-            active = (wet[tile(i, j), :] > 0) & (lev[tile(i, j), :] > layer)
-            return jnp.where(active, ky[layer, tile(i, j), :], 0.0)
-
-        def ahead(now, following):
-            return jnp.where(tail, pltpu.roll(following, 127, 1), pltpu.roll(now, 127, 1))
-
-        faces = []
-        now = cross_of(0)
         for j in range(16):
-            if j < 15:
-                following = cross_of(j + 1)
-                faces.append(jnp.minimum(now, ahead(now, following)))
-                now = following
+            now = cross[i * 128 + j * 8 : i * 128 + j * 8 + 8]
+            upper = jnp.minimum(now, ahead(TRACERS, i, j))
+            lower = jnp.minimum(now, behind(TRACERS, i, j))
+            if j == 15:
+                upper = jnp.where(tail, 0.0, upper)
+            if j == 0:
+                lower = jnp.where(head, 0.0, lower)
+            for t in range(TRACERS):
+                centre = tr[t, layer, tile(i, j), :]
+                side[layer, t, tile(i, j), :] = (
+                    centre + upper * (ahead(t, i, j) - centre) - lower * (centre - behind(t, i, j))
+                )
+
+
+def row_of(half, row):
+    return pl.ds((half * ROWS + row) * 8, 8)
+
+
+def put(mine, theirs, part, layer, halves):
+    first_core = is_first_core()
+    mine[part, layer] = jnp.where(first_core, halves[0], halves[1])
+    theirs[part, layer] = jnp.where(first_core, halves[1], halves[0])
+
+
+def eliminate_bands(kx, co, wet, lev, fill, rho, inv, gain, mine, theirs):
+    groups = [(layer, half) for layer in range(LAYERS) for half in range(2)]
+    depth = [lev[line(0, half), :] for half in range(2)]
+    deep = {g: depth[g[1]] > g[0] for g in groups}
+
+    def load(row):
+        diff, flow = {}, {}
+        for half in range(2):
+            where = line(row, half)
+            water = wet[where, :] > 0
+            for layer in range(LAYERS):
+                g = layer, half
+                active = water & deep[g]
+                diff[g] = jnp.where(active, kx[layer, where, :], 0.0)
+                flow[g] = jnp.where(active, co[layer, where, :], 0.0)
+        return diff, flow
+
+    def put_all(part, values):
+        for layer in range(LAYERS):
+            put(mine, theirs, part, layer, [values[layer, half] for half in range(2)])
+
+    before, flow = load(0)
+    put_all(CD0, before)
+    put_all(WA0, flow)
+    now, flow = load(1)
+    first = {g: jnp.minimum(before[g], now[g]) for g in groups}
+    for layer, half in groups:
+        gain[layer, row_of(half, 0), :] = first[layer, half]
+    down = dict(first)
+    ratio, fills, sums, chain = {}, {}, {}, {}
+    for row in range(1, ROWS - 1):
+        after, flow_after = load(row + 1)
+        for g in groups:
+            layer, half = g
+            where = row_of(half, row)
+            up = jnp.minimum(now[g], after[g])
+            low = down[g] + jnp.where(before[g] > 0.0, flow[g], 0.0)
+            if row == 1:
+                inverse = 1.0 / (1.0 + up + low)
+                ratio[g] = up * inverse
+                gained = low * inverse
+                fills[g] = gained
+                sums[g] = gained
+                chain[g] = ratio[g]
             else:
-                faces.append(jnp.where(tail, 0.0, jnp.minimum(now, pltpu.roll(now, 127, 1))))
-        for t in range(TRACERS):
-            now = tr[t, layer, tile(i, 0), :]
-            shifted = pltpu.roll(now, 127, 1)
-            before = jnp.zeros((8, 128), F32)
-            for j in range(16):
-                if j < 15:
-                    following = tr[t, layer, tile(i, j + 1), :]
-                    shifted_following = pltpu.roll(following, 127, 1)
-                    flux = faces[j] * (jnp.where(tail, shifted_following, shifted) - now)
-                else:
-                    flux = faces[j] * (shifted - now)
-                behind = pltpu.roll(flux, 1, 1)
-                side[t, tile(i, j), :] = now + flux - jnp.where(head, before, behind)
-                before = behind
-                now, shifted = following, shifted_following
-
-
-def eliminate(layer, kx, co, wet, lev, red, fill, rho, inv, gain, mine, theirs, side):
-    first_core = is_first_core()
-    halves = []
+                inverse = 1.0 / (1.0 + up + low * (1.0 - ratio[g]))
+                ratio[g] = up * inverse
+                gained = low * inverse
+                fills[g] = gained * fills[g]
+                sums[g] = sums[g] + chain[g] * fills[g]
+                chain[g] = chain[g] * ratio[g]
+            inv[layer, where, :] = inverse
+            gain[layer, where, :] = gained
+            rho[layer, where, :] = ratio[g]
+            fill[layer, where, :] = fills[g]
+            down[g] = up
+        before, now, flow = now, after, flow_after
+    low = {g: down[g] + jnp.where(before[g] > 0.0, flow[g], 0.0) for g in groups}
+    for layer, half in groups:
+        gain[layer, row_of(half, ROWS - 1), :] = low[layer, half]
+    put_all(CDN, now)
+    put_all(D0, {g: 1.0 + first[g] * (1.0 - sums[g]) for g in groups})
+    put_all(F0, {g: first[g] * chain[g] for g in groups})
+    put_all(DN, {g: 1.0 + low[g] * (1.0 - ratio[g]) for g in groups})
+    put_all(EN, {g: low[g] * fills[g] for g in groups})
+
+
+def eliminate_sides(layer, red, rho, inv, gain, mine, theirs, side):
+    edges_of = []
     for half in range(2):
-
-        def load(row):
-            where = line(row, half)
-            active = (wet[where, :] > 0) & (lev[where, :] > layer)
-            act = jnp.where(active, 1.0, 0.0).astype(F32)
-            return act, kx[layer, where, :] * act, co[layer, where, :]
-
-        out = [None] * PARTS
-        act_prev, cd_prev, co_prev = load(0)
-        act, cd, cour = load(1)
-        out[CD0] = cd_prev
-        out[WA0] = act_prev * co_prev
-        face_first = jnp.minimum(cd_prev, cd)
-        face_down = face_first
-        rho_row = None
+        get = lambda t, row: side[layer, t, line(row, half), :]
         for row in range(1, ROWS - 1):
-            act_next, cd_next, co_next = load(row + 1)
-            face_up = jnp.minimum(cd, cd_next)
-            low = act * (face_down + cour * act_prev)
-            where = pl.ds((half * ROWS + row) * 8, 8)
+            where = row_of(half, row)
+            inverse, ratio = inv[layer, where, :], rho[layer, where, :]
             if row == 1:
-                inverse = 1.0 / (1.0 + face_up + low)
-                rho_row = face_up * inverse
-                gain_row = low * inverse
-                fill_row = gain_row
-                reds = [side[t, line(row, half), :] * inverse for t in range(TRACERS)]
+                reds = [get(t, row) * inverse for t in range(TRACERS)]
                 sums = list(reds)
-                sum_fill = fill_row
-                chain = rho_row
+                chain = ratio
             else:
-                inverse = 1.0 / (1.0 + face_up + low * (1.0 - rho_row))
-                rho_row = face_up * inverse
-                gain_row = low * inverse
-                fill_row = gain_row * fill_row
-                reds = [side[t, line(row, half), :] * inverse + gain_row * reds[t] for t in range(TRACERS)]
+                gained = gain[layer, where, :]
+                reds = [get(t, row) * inverse + gained * reds[t] for t in range(TRACERS)]
                 sums = [sums[t] + chain * reds[t] for t in range(TRACERS)]
-                sum_fill = sum_fill + chain * fill_row
-                chain = chain * rho_row
-            rho[layer, where, :] = rho_row
-            fill[layer, where, :] = fill_row
-            inv[layer, where, :] = inverse
-            gain[layer, where, :] = gain_row
+                chain = chain * ratio
             for t in range(TRACERS):
                 red[t, layer, where, :] = reds[t]
-            act_prev = act
-            act, cd, cour = act_next, cd_next, co_next
-            face_down = face_up
-        low = act * (face_down + cour * act_prev)
-        gain[layer, pl.ds(half * ROWS * 8, 8), :] = face_first
-        gain[layer, pl.ds((half * ROWS + ROWS - 1) * 8, 8), :] = low
-        out[D0] = 1.0 + face_first * (1.0 - sum_fill)
-        out[F0] = face_first * chain
-        out[CDN] = cd
-        out[DN] = 1.0 + low * (1.0 - rho_row)
-        out[EN] = low * fill_row
-        for t in range(TRACERS):
-            out[R0 + t] = side[t, line(0, half), :] + face_first * sums[t]
-            out[RN + t] = side[t, line(ROWS - 1, half), :] + low * reds[t]
-        halves.append(out)
-    for part in range(PARTS):
-        mine[part, layer] = jnp.where(first_core, halves[0][part], halves[1][part])
-        theirs[part, layer] = jnp.where(first_core, halves[1][part], halves[0][part])
+        first, low = gain[layer, row_of(half, 0), :], gain[layer, row_of(half, ROWS - 1), :]
+        edges_of.append(
+            [get(t, 0) + first * sums[t] for t in range(TRACERS)]
+            + [get(t, ROWS - 1) + low * reds[t] for t in range(TRACERS)]
+        )
+    for t in range(TRACERS):
+        for part, k in ((R0 + t, t), (RN + t, TRACERS + t)):
+            put(mine, theirs, part, layer, [edges_of[0][k], edges_of[1][k]])
 
 
 def local_part(tracers, kappa_x, kappa_y, courant, wet, levels):
@@ -229,9 +268,11 @@
         out_specs=[vmem] * 7,
         out_shape=[jax.ShapeDtypeStruct((TRACERS, LAYERS, 256, 128), F32)] + [layered] * 4 + [packed] * 2,
         scratch_shapes=[
-            pltpu.VMEM((TRACERS, 256, 128), F32),
+            pltpu.VMEM((LAYERS, TRACERS, 256, 128), F32),
             pltpu.VMEM((LAYERS, 256, 128), F32),
             pltpu.VMEM((LAYERS, 256, 128), F32),
+            pltpu.VMEM((256, 256), jnp.bfloat16),
+            pltpu.VMEM((TRACERS + 1, 256, 256), F32),
             pltpu.SemaphoreType.DMA((2,)),
         ],
         compiler_params=pltpu.CompilerParams(vmem_limit_bytes=12 * 1024 * 1024),

time: 52.1 us -> 49.3 us (0.946)
  Pallas kernels: 9.82 us -> 7.02 us
    pallas_call x1, Pallas kernels: 5.43 us -> 2.62 us  [local_part(): pl.pallas_call(local_kernel, in_specs=[vmem, hbm, vmem, hbm, vmem, vmem],...]
  transfers between devices with their start and end apart: 4 -> 4, of which waited for: 2 -> 2; matrix products, arithmetic and copies ran while one was open for 0% -> 0% of each run, Pallas kernels for 12% -> 7%
where the time goes in v4:
time: 49.3 us; the launch traced here: 49.2 us
  blocking collectives  28.9 us (59%)
  starting transfers between devices  11.5 us (23%)
  Pallas kernels  7.02 us (14%)
  waiting for transfers between devices  1.59 us (3%)
    all_to_all x1, blocking collectives, on_device(): lax.all_to_all(sent.reshape(CHIPS, LAYERS * SENT, 128), 'chan', 0, 0, axi...  18.5 us
    all_to_all x1, blocking collectives, on_device(): lax.all_to_all(solved.reshape(CHIPS, LAYERS * BACK, 128), 'chan', 0, 0, a...  10.4 us
    ppermute x2, starting transfers between devices, on_device(): other = lax.ppermute(theirs, 'chan', pairs)  5.59 us
    ppermute x1, starting transfers between devices, on_device(): lax.ppermute(lowest, 'cross', [((i + 1) % count, i) for i in range(count)])  3.72 us
    pallas_call x1, Pallas kernels, local_part(): pl.pallas_call(local_kernel, in_specs=[vmem, hbm, vmem, hbm, vmem, vmem],...  2.62 us
    ppermute x1, starting transfers between devices, on_device(): lax.ppermute(highest, 'cross', [(i, (i + 1) % count) for i in range(count)])  2.2 us
    pallas_call x1, Pallas kernels, final_part(): pl.pallas_call(final_kernel, in_specs=[vmem] * 5, out_specs=pl.BlockSpec(...  1.62 us
    ppermute x2, waiting for transfers between devices, on_device(): other = lax.ppermute(theirs, 'chan', pairs)  1.59 us
  transfers between devices with their start and end apart: 4, of which 2 were waited for; matrix products, arithmetic and copies ran while one was open for 0% of the time, Pallas kernels for 7%

profile of v4, /device:TPU:1, one launch (start us, length us, event | category | flops | bytes accessed | tf_op | source)
XLA Modules:
  0.0 49.2 jit_solution(655827822928860077)
XLA Ops:
  0.0 0.0 copy-start.2
  0.0 0.0 copy-start.3
  0.0 0.0 copy-start
  0.0 0.0 copy-start.1
  0.0 1.3 %edges.1 = (f32[4,16,128]{2,1,0:T(8,128)S(1)}, f32[4,16,128]{2,1,0:T(8,128)S(1)}) custom-call(f32[5,4,16,2048]{3,2,1,0:T(8,128)} %tr_hi.1, f32[5,4,16,2048]{3,2,1,0:T(8,128)} %tr_hi.1, f32[4,16,2048]{2,1,0:T(8,128)} %ky_hi.1, f32[4,16,2048]{2,1,0:T(8,128)} %ky_hi.1, s32[16,2048]{1,0:T(8,128)} %wet_hi.1, s32[16,2048]{1,0:T(8,128)} %wet_hi.1, ...), custom_call_target="tpu_custom_call" | custom-call | tf_op jit(solution)/shard_map/edges/pallas_call | solution.py:72
  1.4 2.2 %collective-permute-start = (f32[4,16,128]{2,1,0:T(8,128)S(1)}, f32[4,16,128]{2,1,0:T(8,128)S(1)}, u32[]{:S(2)}, u32[]{:S(2)}) collective-permute-start(f32[4,16,128]{2,1,0:T(8,128)S(1)} %get-tuple-element.29), channel_id=1, source_target_pairs={{0,1},{1,2},{2,3},{3,4},{4,5},{5,6},{6,7},{7,8},{8,9},{9,10},{10,1... | collective-permute-start | bytes 98312 | tf_op jit(solution)/shard_map/ppermute | solution.py:578
  3.6 3.7 %collective-permute-start.1 = (f32[4,16,128]{2,1,0:T(8,128)S(1)}, f32[4,16,128]{2,1,0:T(8,128)S(1)}, u32[]{:S(2)}, u32[]{:S(2)}) collective-permute-start(f32[4,16,128]{2,1,0:T(8,128)S(1)} %get-tuple-element.28), channel_id=1, source_target_pairs={{1,0},{2,1},{3,2},{4,3},{5,4},{6,5},{7,6},{8,7},{9,8},{10,9},{11,1... | collective-permute-start | bytes 98312 | tf_op jit(solution)/shard_map/ppermute | solution.py:579
  7.3 0.0 copy-done.2
  7.3 0.0 copy-done.3
  7.3 0.0 copy-done
  7.3 0.0 copy-done.1
  7.3 2.6 %local_part.1 = (f32[5,4,256,128]{3,2,1,0:T(8,128)S(1)}, f32[4,256,128]{2,1,0:T(8,128)S(1)}, f32[4,256,128]{2,1,0:T(8,128)S(1)}, f32[4,256,128]{2,1,0:T(8,128)S(...) custom-call(f32[5,4,256,128]{3,2,1,0:T(8,128)S(1)} %bitcast.50, ...), custom_call_target="tpu_custom_call" | custom-call | tf_op jit(solution)/shard_map/local_part/pallas_call | solution.py:265
  9.9 0.0 collective-permute-done
  10.0 0.0 collective-permute-done.1
  10.0 0.5 outer_part.1
  10.4 2.8 %collective-permute-start.2 = (f32[17,4,8,128]{3,2,1,0:T(8,128)S(1)}, f32[17,4,8,128]{3,2,1,0:T(8,128)S(1)}, u32[]{:S(2)}, u32[]{:S(2)}) collective-permute-start(f32[17,4,8,128]{3,2,1,0:T(8,128)S(1)} %bitcast.68), channel_id=1, source_target_pairs={{0,16},{16,0},{32,48},{48,32},{64,80},{80,64},{96,112},{112,96},{1... | collective-permute-start | bytes 835592 | tf_op jit(solution)/shard_map/ppermute | solution.py:591
  13.2 1.2 %collective-permute-done.2.other = f32[17,4,8,128]{3,2,1,0:T(8,128)S(1)} collective-permute-done((f32[17,4,8,128]{3,2,1,0:T(8,128)S(1)}, f32[17,4,8,128]{3,2,1,0:T(8,128)S(1)}, u32[]{:S(2)}, u32[]{:S(2)}) %collective-permute-start.2) | collective-permute-done | bytes 278560 | tf_op jit(solution)/shard_map/ppermute | solution.py:591
  14.4 0.1 pair_part.1
  14.5 18.5 %all_to_all.10 = f32[8,72,128]{2,1,0:T(8,128)S(1)} all-to-all(f32[8,72,128]{2,1,0:T(8,128)S(1)} %bitcast.60), channel_id=1, replica_groups={{0,32,64,96,128,160,192,224},{16,48,80,112,144,176,208,240},{1,33,65,97..., dimensions={0} | all-to-all | bytes 589824 | tf_op jit(solution)/shard_map/all_to_all | solution.py:594
  33.0 0.2 chain_part.1
  33.2 10.4 %all_to_all.11 = f32[8,40,128]{2,1,0:T(8,128)S(1)} all-to-all(f32[8,40,128]{2,1,0:T(8,128)S(1)} %bitcast.56), channel_id=1, replica_groups={{0,32,64,96,128,160,192,224},{16,48,80,112,144,176,208,240},{1,33,65,97..., dimensions={0} | all-to-all | bytes 327680 | tf_op jit(solution)/shard_map/all_to_all | solution.py:598
  43.6 0.1 middle_part.1
  43.7 2.8 %collective-permute-start.3 = (f32[10,4,8,128]{3,2,1,0:T(8,128)S(1)}, f32[10,4,8,128]{3,2,1,0:T(8,128)S(1)}, u32[]{:S(2)}, u32[]{:S(2)}) collective-permute-start(f32[10,4,8,128]{3,2,1,0:T(8,128)S(1)} %get-tuple-element.44), channel_id=1, source_target_pairs={{0,16},{16,0},{32,48},{48,32},{64,80},{80,64},{96,112},{112,96},{1... | collective-permute-start | bytes 491528 | tf_op jit(solution)/shard_map/ppermute | solution.py:602
  46.5 0.6 %spread_part.1 = (f32[5,4,256,128]{3,2,1,0:T(8,128)S(1)}, f32[4,256,128]{2,1,0:T(8,128)S(1)}, f32[4,256,128]{2,1,0:T(8,128)S(1)}) custom-call(f32[5,4,256,128]{3,2,1,0:T(8,128)S(1)} %get-tuple-element.25.red, f32[4,256,128]{2,1,0:T(8,128)S(1)} %get-tuple-element.26.fill, f32[4,256,128]{2,1,0:T(8,128)S(1)} %get-tuple-element.27.rho, ...), custom_call_target="tpu_custom_call" | custom-call | tf_op jit(solution)/shard_map/spread_part/pallas_call | solution.py:516
  47.1 0.4 collective-permute-done.3.other
  47.5 1.6 %final_part.1 = f32[5,4,256,128]{3,2,1,0:T(8,128)} custom-call(f32[5,4,256,128]{3,2,1,0:T(8,128)S(1)} %get-tuple-element.36.base, f32[4,256,128]{2,1,0:T(8,128)S(1)} %get-tuple-element.37.of_first, f32[4,256,128]{2,1,0:T(8,128)S(1)} %get-tuple-element.38.of_last, f32[10,4,8,128]{3,2,1,0:T(8,128)S(1)} %get-tuple-element.43.mine, ...), custom_call_target="tpu_custom_call" | custom-call | tf_op jit(solution)/shard_map/final_part/pallas_call | solution.py:558
Async XLA Ops:
  0.0 7.3 %copy-start.2 = (s32[16,2048]{1,0:T(8,128)S(1)}, s32[16,2048]{1,0:T(8,128)}, u32[]{:S(2)}) copy-start(s32[16,2048]{1,0:T(8,128)} %wet_hi.1) | copy-start | bytes 393220
  0.0 7.3 %copy-start.3 = (s32[16,2048]{1,0:T(8,128)S(1)}, s32[16,2048]{1,0:T(8,128)}, u32[]{:S(2)}) copy-start(s32[16,2048]{1,0:T(8,128)} %lev_hi.1) | copy-start | bytes 393220
  0.0 7.3 %copy-start = (f32[5,4,16,2048]{3,2,1,0:T(8,128)S(1)}, f32[5,4,16,2048]{3,2,1,0:T(8,128)}, u32[]{:S(2)}) copy-start(f32[5,4,16,2048]{3,2,1,0:T(8,128)} %tr_hi.1) | copy-start | bytes 7864324
  0.0 7.3 %copy-start.1 = (f32[4,16,2048]{2,1,0:T(8,128)S(1)}, f32[4,16,2048]{2,1,0:T(8,128)}, u32[]{:S(2)}) copy-start(f32[4,16,2048]{2,1,0:T(8,128)} %ky_hi.1) | copy-start | bytes 1572868
  1.4 8.6 %collective-permute-start = (f32[4,16,128]{2,1,0:T(8,128)S(1)}, f32[4,16,128]{2,1,0:T(8,128)S(1)}, u32[]{:S(2)}, u32[]{:S(2)}) collective-permute-start(f32[4,16,128]{2,1,0:T(8,128)S(1)} %get-tuple-element.29), channel_id=1, source_target_pairs={{0,1},{1,2},{2,3},{3,4},{4,5},{5,6},{6,7},{7,8},{8,9},{9,10},{10,1... | collective-permute-start | bytes 98312 | tf_op jit(solution)/shard_map/ppermute | solution.py:578
  3.6 6.4 %collective-permute-start.1 = (f32[4,16,128]{2,1,0:T(8,128)S(1)}, f32[4,16,128]{2,1,0:T(8,128)S(1)}, u32[]{:S(2)}, u32[]{:S(2)}) collective-permute-start(f32[4,16,128]{2,1,0:T(8,128)S(1)} %get-tuple-element.28), channel_id=1, source_target_pairs={{1,0},{2,1},{3,2},{4,3},{5,4},{6,5},{7,6},{8,7},{9,8},{10,9},{11,1... | collective-permute-start | bytes 98312 | tf_op jit(solution)/shard_map/ppermute | solution.py:579
  10.4 4.0 %collective-permute-start.2 = (f32[17,4,8,128]{3,2,1,0:T(8,128)S(1)}, f32[17,4,8,128]{3,2,1,0:T(8,128)S(1)}, u32[]{:S(2)}, u32[]{:S(2)}) collective-permute-start(f32[17,4,8,128]{3,2,1,0:T(8,128)S(1)} %bitcast.68), channel_id=1, source_target_pairs={{0,16},{16,0},{32,48},{48,32},{64,80},{80,64},{96,112},{112,96},{1... | collective-permute-start | bytes 835592 | tf_op jit(solution)/shard_map/ppermute | solution.py:591
  43.7 3.8 %collective-permute-start.3 = (f32[10,4,8,128]{3,2,1,0:T(8,128)S(1)}, f32[10,4,8,128]{3,2,1,0:T(8,128)S(1)}, u32[]{:S(2)}, u32[]{:S(2)}) collective-permute-start(f32[10,4,8,128]{3,2,1,0:T(8,128)S(1)} %get-tuple-element.44), channel_id=1, source_target_pairs={{0,16},{16,0},{32,48},{48,32},{64,80},{80,64},{96,112},{112,96},{1... | collective-permute-start | bytes 491528 | tf_op jit(solution)/shard_map/ppermute | solution.py:602

commit v5 on v4

--- a/solution.py
+++ b/solution.py
@@ -47,7 +47,8 @@
     return pl.ds(row_tile * 128 + column_tile * 8, 8)
 
 
-def edges_kernel(tr_lo, tr_hi, ky_lo, ky_hi, wet_lo, wet_hi, lev_lo, lev_hi, out_lo, out_hi):
+def edges_kernel(tr_lo, tr_hi, ky_lo, ky_hi, wet_lo, wet_hi, lev_lo, lev_hi, out_lo, out_hi, swap_a, swap_b):
+    even = lax.axis_index("cross") % 2 == 0
     lane = lax.broadcasted_iota(jnp.int32, (8, 128), 1)
     for tr, ky, wet, lev, out, at in (
         (tr_lo, ky_lo, wet_lo, lev_lo, out_lo, 0),
@@ -62,6 +63,12 @@
                 for t in range(TRACERS):
                     packed = jnp.where(lane == t, pltpu.roll(tr[t, l, rows, :], (t - at) % 128, 1), packed)
                 out[l, rows, :] = packed
+    for l in range(LAYERS):
+        for i in range(2):
+            rows = pl.ds(i * 8, 8)
+            lo, hi = out_lo[l, rows, :], out_hi[l, rows, :]
+            swap_a[l, rows, :] = jnp.where(even, hi, lo)
+            swap_b[l, rows, :] = jnp.where(even, lo, hi)
 
 
 def edges(tracers, kappa_y, wet, levels):
@@ -82,8 +89,8 @@
             spec((), 0),
             spec((), 15),
         ],
-        out_specs=[pl.BlockSpec((LAYERS, 16, 128), lambda i: (0, 0, 0))] * 2,
-        out_shape=[jax.ShapeDtypeStruct((LAYERS, 16, 128), F32)] * 2,
+        out_specs=[pl.BlockSpec((LAYERS, 16, 128), lambda i: (0, 0, 0))] * 4,
+        out_shape=[jax.ShapeDtypeStruct((LAYERS, 16, 128), F32)] * 4,
         compiler_params=SMALL,
         name="edges",
     )(*(in_hbm(x) for x in (tracers, tracers, kappa_y, kappa_y, wet, wet, levels, levels)))
@@ -280,17 +287,34 @@
     )(tracers, in_hbm(kappa_x), kappa_y, in_hbm(courant), wet, levels)
 
 
+def inner_kernel(cells, out):
+    place = lax.axis_index("cross")
+    inner = (place > 0) & (place < lax.axis_size("cross") - 1)
+    out[...] = jnp.where(inner, cells[...], 0.0)
+
+
+def inner_part(cells):
+    vmem = pl.BlockSpec(memory_space=pltpu.VMEM)
+    return pl.pallas_call(
+        inner_kernel,
+        in_specs=[vmem],
+        out_specs=vmem,
+        out_shape=jax.ShapeDtypeStruct(cells.shape, F32),
+        compiler_params=SMALL,
+        name="inner_part",
+    )(cells)
+
+
 def outer_kernel(
-    own_lo, own_hi, left, right, inv, gain, rho, mine_in, theirs_in, mine, theirs, fix_lo, fix_hi
+    own_lo, own_hi, from_a, from_b, inv, gain, rho, mine_in, theirs_in, mine, theirs, fix_lo, fix_hi
 ):
-    place = lax.axis_index("cross")
+    even = lax.axis_index("cross") % 2 == 0
     first_core = is_first_core()
     mine[...] = mine_in[...]
     theirs[...] = theirs_in[...]
     lane = lax.broadcasted_iota(jnp.int32, (LAYERS, 128), 1)
-    for e, (own, halo, fix) in enumerate(((own_lo, left, fix_lo), (own_hi, right, fix_hi))):
+    for e, (own, (of_even, of_odd), fix) in enumerate(((own_lo, (from_b, from_a), fix_lo), (own_hi, (from_a, from_b), fix_hi))):
         at, sub = (0, 0) if e == 0 else (127, 7)
-        inside = (place > 0) if e == 0 else (place < lax.axis_size("cross") - 1)
 
         def coefficient(ref, row):
             values = ref[pl.ds((e * ROWS + row) * 8 + sub, LAYERS, stride=256), :]
@@ -299,7 +323,8 @@
         deltas = []
         for row in range(ROWS):
             here = own[pl.ds(row, LAYERS, stride=ROWS), :]
-            there = jnp.where(inside, halo[pl.ds(row, LAYERS, stride=ROWS), :], 0.0)
+            cells = pl.ds(row, LAYERS, stride=ROWS)
+            there = jnp.where(even, of_even[cells, :], of_odd[cells, :])
             face = pltpu.roll(jnp.minimum(here, there), 64, 1)
             deltas.append(face * (there - here))
         rhos = [None] + [coefficient(rho, row) for row in range(1, ROWS - 1)]
@@ -332,7 +357,7 @@
         pl.when(jnp.logical_not(first_core) if e == 0 else first_core)(lambda: add_to(theirs))
 
 
-def outer_part(own_lo, own_hi, left, right, inv, gain, rho, mine, theirs):
+def outer_part(own_lo, own_hi, from_a, from_b, inv, gain, rho, mine, theirs):
     vmem = pl.BlockSpec(memory_space=pltpu.VMEM)
     flat = lambda x: x.reshape(-1, 128)
     mine, theirs, fix_lo, fix_hi = pl.pallas_call(
@@ -343,7 +368,7 @@
         + [jax.ShapeDtypeStruct((LAYERS * ROWS, 128), F32)] * 2,
         compiler_params=SMALL,
         name="outer_part",
-    )(*(flat(x) for x in (own_lo, own_hi, left, right, inv, gain, rho, mine, theirs)))
+    )(*(flat(x) for x in (own_lo, own_hi, from_a, from_b, inv, gain, rho, mine, theirs)))
     packed = (PARTS, LAYERS, 8, 128)
     return mine.reshape(packed), theirs.reshape(packed), fix_lo, fix_hi
 
@@ -523,50 +548,59 @@
     )(red, fill, rho, fix_lo, fix_hi)
 
 
-def final_kernel(base, of_first, of_last, mine, other, out, ready, sems):
-    first_core = is_first_core()
-
-    def copy_of(layer):
-        return pltpu.make_async_copy(ready.at[:, layer], out.at[:, layer], sems.at[layer])
+def final_kernel(own, base, of_first, of_last, ends, *refs):
+    out, ready, sems = refs[-3:]
+    half = lax.axis_index("chan") % 2
+    if not own:
+        half = 1 - half
+
+    def start_of(i):
+        return pl.multiple_of(i * 128 + half * 64, 64)
+
+    def copy_of(layer, i):
+        rows = pl.ds(start_of(i), 64)
+        return pltpu.make_async_copy(
+            ready.at[:, layer, pl.ds(i * 64, 64)], out.at[:, layer, rows], sems.at[layer, i]
+        )
 
     def one_layer(layer, none):
-        def fill_in(low, high):
-            for half, ends in ((0, low), (1, high)):
-                for j in range(8):
-                    spread = lambda k: jnp.broadcast_to(ends[k, layer, pl.ds(j, 1), :], (8, 128))
-                    firsts = [spread(t) for t in range(TRACERS)]
-                    lasts = [spread(TRACERS + t) for t in range(TRACERS)]
-                    for i in range(2):
-                        where = tile(i, half * 8 + j)
-                        by_first, by_last = of_first[layer, where, :], of_last[layer, where, :]
-                        for t in range(TRACERS):
-                            ready[t, layer, where, :] = (
-                                base[t, layer, where, :] + by_first * firsts[t] + by_last * lasts[t]
-                            )
-
-        pl.when(first_core)(lambda: fill_in(mine, other))
-        pl.when(jnp.logical_not(first_core))(lambda: fill_in(other, mine))
-        copy_of(layer).start()
+        for j in range(8):
+            spread = lambda k: jnp.broadcast_to(ends[k, layer, pl.ds(j, 1), :], (8, 128))
+            firsts = [spread(t) for t in range(TRACERS)]
+            lasts = [spread(TRACERS + t) for t in range(TRACERS)]
+            for i in range(2):
+                where = pl.ds(pl.multiple_of(start_of(i) + j * 8, 8), 8)
+                by_first, by_last = of_first[layer, where, :], of_last[layer, where, :]
+                for t in range(TRACERS):
+                    ready[t, layer, pl.ds(i * 64 + j * 8, 8), :] = (
+                        base[t, layer, where, :] + by_first * firsts[t] + by_last * lasts[t]
+                    )
+        for i in range(2):
+            copy_of(layer, i).start()
 
     lax.fori_loop(0, LAYERS, one_layer, None)
     for layer in range(LAYERS):
-        copy_of(layer).wait()
-
-
-def final_part(base, of_first, of_last, mine, other):
-    vmem = pl.BlockSpec(memory_space=pltpu.VMEM)
-    return pl.pallas_call(
-        final_kernel,
-        in_specs=[vmem] * 5,
-        out_specs=pl.BlockSpec(memory_space=pltpu.HBM),
+        for i in range(2):
+            copy_of(layer, i).wait()
+
+
+def final_part(base, of_first, of_last, ends, partial=None):
+    vmem = pl.BlockSpec(memory_space=pltpu.VMEM)
+    hbm = pl.BlockSpec(memory_space=pltpu.HBM)
+    own = partial is None
+    return pl.pallas_call(
+        functools.partial(final_kernel, own),
+        in_specs=[vmem] * 4 + ([] if own else [hbm]),
+        out_specs=hbm,
         out_shape=jax.ShapeDtypeStruct((TRACERS, LAYERS, 256, 128), F32),
+        input_output_aliases={} if own else {4: 0},
         scratch_shapes=[
-            pltpu.VMEM((TRACERS, LAYERS, 256, 128), F32),
-            pltpu.SemaphoreType.DMA((LAYERS,)),
+            pltpu.VMEM((TRACERS, LAYERS, 128, 128), F32),
+            pltpu.SemaphoreType.DMA((LAYERS, 2)),
         ],
-        compiler_params=pltpu.CompilerParams(vmem_limit_bytes=12 * 1024 * 1024),
-        name="final_part",
-    )(base, of_first, of_last, mine, other)
+        compiler_params=pltpu.CompilerParams(vmem_limit_bytes=8 * 1024 * 1024),
+        name="final_own" if own else "final_other",
+    )(base, of_first, of_last, ends, *(() if own else (partial,)))
 
 
 def on_device(tracers, kappa_x, kappa_y, courant, wet_mask, levels):
@@ -574,9 +608,16 @@
     pairs = [(i, i ^ 1) for i in range(2 * CHIPS)]
     lines = [[c + 2 * z for z in range(CHIPS)] for c in range(2)]
 
-    lowest, highest = edges(tracers, kappa_y, wet_mask, levels)
-    left = lax.ppermute(highest, "cross", [(i, (i + 1) % count) for i in range(count)])
-    right = lax.ppermute(lowest, "cross", [((i + 1) % count, i) for i in range(count)])
+    lowest, highest, to_a, to_b = edges(tracers, kappa_y, wet_mask, levels)
+    swap_a = [(i, i ^ 1) for i in range(count)]
+    swap_b = []
+    for along in range(2 * CHIPS):
+        for i in range(count):
+            inner = 0 < i < count - 1
+            partner = along * count + ((i + 1) ^ 1) - 1 if inner else (along ^ 1) * count + i
+            swap_b.append((along * count + i, partner))
+    from_b = inner_part(lax.ppermute(to_b, ("chan", "cross"), swap_b))
+    from_a = lax.ppermute(to_a, "cross", swap_a)
     red, fill, rho, inv, gain, mine, theirs = local_part(
         folded(tracers),
         folded(kappa_x),
@@ -586,10 +627,11 @@
         folded(levels),
     )
     mine, theirs, fix_lo, fix_hi = outer_part(
-        lowest, highest, left, right, inv, gain, rho, mine, theirs
+        lowest, highest, from_a, from_b, inv, gain, rho, mine, theirs
     )
     other = lax.ppermute(theirs, "chan", pairs)
     base, of_first, of_last = spread_part(red, fill, rho, fix_lo, fix_hi)
+    other, base, of_first, of_last = lax.optimization_barrier((other, base, of_first, of_last))
     sent, kept = pair_part(mine, other)
     parts = lax.all_to_all(
         sent.reshape(CHIPS, LAYERS * SENT, 128), "chan", 0, 0, axis_index_groups=lines, tiled=True
@@ -600,7 +642,8 @@
     )
     mine, theirs = middle_part(back.reshape(CHIPS * LAYERS * BACK, 128), kept)
     other = lax.ppermute(theirs, "chan", pairs)
-    return unfolded(final_part(base, of_first, of_last, mine, other))
+    partial = final_part(base, of_first, of_last, mine)
+    return unfolded(final_part(base, of_first, of_last, other, partial))
 
 
 def solution(mesh):

time: 49.3 us -> 47.4 us (0.961); the launches traced: 49.2 us -> 46.7 us
  starting transfers between devices: 11.5 us -> 7.64 us
  blocking collectives: 28.9 us -> 30.6 us
  waiting for transfers between devices: 1.59 us -> 0.57 us
  Pallas kernels: 7.02 us -> 7.76 us
    ppermute x2, starting transfers between devices: 5.93 us -> 3.51 us  [the longest x1 3.31 us: on_device(): from_b = inner_part(lax.ppermute(to_b, ('chan', 'cross'), swap_b))]
    all_to_all x1, blocking collectives: 18.5 us -> 20.2 us  [on_device(): lax.all_to_all(sent.reshape(CHIPS, LAYERS * SENT, 128), 'chan', 0, 0, axi...]
    ppermute x2, starting transfers between devices: 5.59 us -> 4.13 us  [on_device(): other = lax.ppermute(theirs, 'chan', pairs)]
    ppermute x2, waiting for transfers between devices: 1.59 us -> 0.56 us  [on_device(): other = lax.ppermute(theirs, 'chan', pairs)]
    pallas_call x1 -> x3, Pallas kernels: 1.62 us -> 2.37 us  [the longest x2 2.35 us: final_part(): pl.pallas_call(functools.partial(final_kernel, own), in_specs=[vmem] * 4...]
  transfers between devices with their start and end apart: 4 -> 4, of which waited for: 2 -> 1; matrix products, arithmetic and copies ran while one was open for 0% -> 0% of each run, Pallas kernels for 7% -> 9%
where the time goes in v5:
time: 47.4 us; the launch traced here: 46.7 us
  blocking collectives  30.6 us (65%)
  Pallas kernels  7.76 us (16%)
  starting transfers between devices  7.64 us (16%)
  waiting for transfers between devices  0.57 us (1%)
    all_to_all x1, blocking collectives, on_device(): lax.all_to_all(sent.reshape(CHIPS, LAYERS * SENT, 128), 'chan', 0, 0, axi...  20.2 us
    all_to_all x1, blocking collectives, on_device(): lax.all_to_all(solved.reshape(CHIPS, LAYERS * BACK, 128), 'chan', 0, 0, a...  10.4 us
    ppermute x2, starting transfers between devices, on_device(): other = lax.ppermute(theirs, 'chan', pairs)  4.13 us
    ppermute x1, starting transfers between devices, on_device(): from_b = inner_part(lax.ppermute(to_b, ('chan', 'cross'), swap_b))  3.31 us
    pallas_call x1, Pallas kernels, local_part(): pl.pallas_call(local_kernel, in_specs=[vmem, hbm, vmem, hbm, vmem, vmem],...  2.61 us
    pallas_call x2, Pallas kernels, final_part(): pl.pallas_call(functools.partial(final_kernel, own), in_specs=[vmem] * 4...  2.35 us
    pallas_call x1, Pallas kernels, edges(): pl.pallas_call(edges_kernel, grid=(1,), in_specs=[spec((TRACERS, LAYERS),...  1.35 us
  transfers between devices with their start and end apart: 4, of which 1 were waited for; matrix products, arithmetic and copies ran while one was open for 0% of the time, Pallas kernels for 9%

profile of v5, /device:TPU:1, one launch (start us, length us, event | category | flops | bytes accessed | tf_op | source)
XLA Modules:
  0.0 46.7 jit_solution(9519990130126948169)
XLA Ops:
  0.0 0.0 copy-start.3
  0.0 0.0 copy-start.2
  0.0 0.0 copy-start.1
  0.0 0.0 copy-start
  0.0 1.3 %edges.1 = (f32[4,16,128]{2,1,0:T(8,128)S(1)}, f32[4,16,128]{2,1,0:T(8,128)S(1)}, f32[4,16,128]{2,1,0:T(8,128)S(1)}, f32[4,16,128]{2,1,0:T(8,128)S(1)}) custom-call(f32[5,4,16,2048]{3,2,1,0:T(8,128)} %tr_hi.1, f32[5,4,16,2048]{3,2,1,0:T(8,128)} %tr_hi.1, f32[4,16,2048]{2,1,0:T(8,128)} %ky_hi.1, f32[4,16,2048]{2,1,0:T(8,128)} %ky_hi.1, s32[16,2048]{1,0:T(8,128)} %wet_hi.1, ...), custom_call_target="tpu_custom_call" | custom-call | tf_op jit(solution)/shard_map/edges/pallas_call | solution.py:79
  1.4 3.3 %collective-permute-start.1 = (f32[4,16,128]{2,1,0:T(8,128)S(1)}, f32[4,16,128]{2,1,0:T(8,128)S(1)}, u32[]{:S(2)}, u32[]{:S(2)}) collective-permute-start(f32[4,16,128]{2,1,0:T(8,128)S(1)} %get-tuple-element.34), channel_id=1, source_target_pairs={{0,16},{1,2},{2,1},{3,4},{4,3},{5,6},{6,5},{7,8},{8,7},{9,10},{10,... | collective-permute-start | bytes 98312 | tf_op jit(solution)/shard_map/ppermute | solution.py:619
  4.7 0.2 collective-permute-start
  4.9 0.0 copy-done.3
  4.9 0.0 copy-done.2
  4.9 0.0 copy-done.1
  4.9 0.0 copy-done
  4.9 2.6 %local_part.1 = (f32[5,4,256,128]{3,2,1,0:T(8,128)S(1)}, f32[4,256,128]{2,1,0:T(8,128)S(1)}, f32[4,256,128]{2,1,0:T(8,128)S(1)}, f32[4,256,128]{2,1,0:T(8,128)S(...) custom-call(f32[5,4,256,128]{3,2,1,0:T(8,128)S(1)} %bitcast.50, ...), custom_call_target="tpu_custom_call" | custom-call | tf_op jit(solution)/shard_map/local_part/pallas_call | solution.py:272
  7.5 0.0 collective-permute-done.1.cells
  7.5 0.0 collective-permute-done
  7.6 0.5 %outer_part.1 = (f32[544,128]{1,0:T(8,128)S(1)}, f32[544,128]{1,0:T(8,128)S(1)}, f32[64,128]{1,0:T(8,128)S(1)}, f32[64,128]{1,0:T(8,128)S(1)}) custom-call(f32[64,128]{1,0:T(8,128)S(1)} %bitcast.65, f32[64,128]{1,0:T(8,128)S(1)} %bitcast.66, f32[64,128]{1,0:T(8,128)S(1)} %bitcast.67, f32[64,128]{1,0:T(8,128)S(1)} %bitcast.64, f32[1024,128]{1,0:T(8,128)S(1)} %bitcast.58, ...), custom_call_target="tpu_custom_call" | custom-call | tf_op jit(solution)/shard_map/outer_part/pallas_call | solution.py:363
  8.0 1.3 %collective-permute-start.2 = (f32[17,4,8,128]{3,2,1,0:T(8,128)S(1)}, f32[17,4,8,128]{3,2,1,0:T(8,128)S(1)}, u32[]{:S(2)}, u32[]{:S(2)}) collective-permute-start(f32[17,4,8,128]{3,2,1,0:T(8,128)S(1)} %bitcast.68), channel_id=1, source_target_pairs={{0,16},{16,0},{32,48},{48,32},{64,80},{80,64},{96,112},{112,96},{1... | collective-permute-start | bytes 835592 | tf_op jit(solution)/shard_map/ppermute | solution.py:632
  9.4 0.6 %spread_part.1 = (f32[5,4,256,128]{3,2,1,0:T(8,128)S(1)}, f32[4,256,128]{2,1,0:T(8,128)S(1)}, f32[4,256,128]{2,1,0:T(8,128)S(1)}) custom-call(f32[5,4,256,128]{3,2,1,0:T(8,128)S(1)} %get-tuple-element.41.red, f32[4,256,128]{2,1,0:T(8,128)S(1)} %get-tuple-element.42.fill, f32[4,256,128]{2,1,0:T(8,128)S(1)} %get-tuple-element.37.rho, ...), custom_call_target="tpu_custom_call" | custom-call | tf_op jit(solution)/shard_map/spread_part/pallas_call | solution.py:541
  10.0 0.6 %collective-permute-done.2.other = f32[17,4,8,128]{3,2,1,0:T(8,128)S(1)} collective-permute-done((f32[17,4,8,128]{3,2,1,0:T(8,128)S(1)}, f32[17,4,8,128]{3,2,1,0:T(8,128)S(1)}, u32[]{:S(2)}, u32[]{:S(2)}) %collective-permute-start.2) | collective-permute-done | bytes 278560 | tf_op jit(solution)/shard_map/ppermute | solution.py:632
  10.5 0.1 pair_part.1
  10.7 20.2 %all_to_all.10 = f32[8,72,128]{2,1,0:T(8,128)S(1)} all-to-all(f32[8,72,128]{2,1,0:T(8,128)S(1)} %bitcast.60), channel_id=1, replica_groups={{0,32,64,96,128,160,192,224},{16,48,80,112,144,176,208,240},{1,33,65,97..., dimensions={0} | all-to-all | bytes 589824 | tf_op jit(solution)/shard_map/all_to_all | solution.py:636
  30.8 0.2 chain_part.1
  31.0 10.4 %all_to_all.11 = f32[8,40,128]{2,1,0:T(8,128)S(1)} all-to-all(f32[8,40,128]{2,1,0:T(8,128)S(1)} %bitcast.56), channel_id=1, replica_groups={{0,32,64,96,128,160,192,224},{16,48,80,112,144,176,208,240},{1,33,65,97..., dimensions={0} | all-to-all | bytes 327680 | tf_op jit(solution)/shard_map/all_to_all | solution.py:640
  41.5 0.1 middle_part.1
  41.6 2.8 %collective-permute-start.3 = (f32[10,4,8,128]{3,2,1,0:T(8,128)S(1)}, f32[10,4,8,128]{3,2,1,0:T(8,128)S(1)}, u32[]{:S(2)}, u32[]{:S(2)}) collective-permute-start(f32[10,4,8,128]{3,2,1,0:T(8,128)S(1)} %get-tuple-element.55), channel_id=1, source_target_pairs={{0,16},{16,0},{32,48},{48,32},{64,80},{80,64},{96,112},{112,96},{1... | collective-permute-start | bytes 491528 | tf_op jit(solution)/shard_map/ppermute | solution.py:644
  44.3 1.2 %final_own.1.refs_0_ = f32[5,4,256,128]{3,2,1,0:T(8,128)} custom-call(f32[5,4,256,128]{3,2,1,0:T(8,128)S(1)} %get-tuple-element.48.base, f32[4,256,128]{2,1,0:T(8,128)S(1)} %get-tuple-element.49.of_first, f32[4,256,128]{2,1,0:T(8,128)S(1)} %get-tuple-element.50.of_last, f32[10,4,8,128]{3,2,1,0:T(8,128)S(1)} %get-tuple-element.56.ends), custom_call_target="tpu_custom_call" | custom-call | tf_op jit(solution)/shard_map/final_own/pallas_call | solution.py:591
  45.5 0.0 collective-permute-done.3.ends
  45.5 1.2 %final_other.1 = f32[5,4,256,128]{3,2,1,0:T(8,128)} custom-call(f32[5,4,256,128]{3,2,1,0:T(8,128)S(1)} %get-tuple-element.48.base, f32[4,256,128]{2,1,0:T(8,128)S(1)} %get-tuple-element.49.of_first, f32[4,256,128]{2,1,0:T(8,128)S(1)} %get-tuple-element.50.of_last, f32[10,4,8,128]{3,2,1,0:T(8,128)S(1)} %collective-permute-done.3.ends, ...), custom_call_target="tpu_custom_call", output_to_operand_aliasing={{}: (4, {})} | custom-call | tf_op jit(solution)/shard_map/final_other/pallas_call | solution.py:591
  (1 shorter events, 0.0 us)
Async XLA Ops:
  0.0 4.9 %copy-start.3 = (s32[16,2048]{1,0:T(8,128)S(1)}, s32[16,2048]{1,0:T(8,128)}, u32[]{:S(2)}) copy-start(s32[16,2048]{1,0:T(8,128)} %lev_hi.1) | copy-start | bytes 393220
  0.0 4.9 %copy-start.2 = (s32[16,2048]{1,0:T(8,128)S(1)}, s32[16,2048]{1,0:T(8,128)}, u32[]{:S(2)}) copy-start(s32[16,2048]{1,0:T(8,128)} %wet_hi.1) | copy-start | bytes 393220
  0.0 4.9 %copy-start.1 = (f32[4,16,2048]{2,1,0:T(8,128)S(1)}, f32[4,16,2048]{2,1,0:T(8,128)}, u32[]{:S(2)}) copy-start(f32[4,16,2048]{2,1,0:T(8,128)} %ky_hi.1) | copy-start | bytes 1572868
  0.0 4.9 %copy-start = (f32[5,4,16,2048]{3,2,1,0:T(8,128)S(1)}, f32[5,4,16,2048]{3,2,1,0:T(8,128)}, u32[]{:S(2)}) copy-start(f32[5,4,16,2048]{3,2,1,0:T(8,128)} %tr_hi.1) | copy-start | bytes 7864324
  1.4 6.1 %collective-permute-start.1 = (f32[4,16,128]{2,1,0:T(8,128)S(1)}, f32[4,16,128]{2,1,0:T(8,128)S(1)}, u32[]{:S(2)}, u32[]{:S(2)}) collective-permute-start(f32[4,16,128]{2,1,0:T(8,128)S(1)} %get-tuple-element.34), channel_id=1, source_target_pairs={{0,16},{1,2},{2,1},{3,4},{4,3},{5,6},{6,5},{7,8},{8,7},{9,10},{10,... | collective-permute-start | bytes 98312 | tf_op jit(solution)/shard_map/ppermute | solution.py:619
  4.7 2.9 %collective-permute-start = (f32[4,16,128]{2,1,0:T(8,128)S(1)}, f32[4,16,128]{2,1,0:T(8,128)S(1)}, u32[]{:S(2)}, u32[]{:S(2)}) collective-permute-start(f32[4,16,128]{2,1,0:T(8,128)S(1)} %get-tuple-element.33), channel_id=1, source_target_pairs={{0,1},{1,0},{2,3},{3,2},{4,5},{5,4},{6,7},{7,6},{8,9},{9,8},{10,11... | collective-permute-start | bytes 98312 | tf_op jit(solution)/shard_map/ppermute | solution.py:620
  8.0 2.5 %collective-permute-start.2 = (f32[17,4,8,128]{3,2,1,0:T(8,128)S(1)}, f32[17,4,8,128]{3,2,1,0:T(8,128)S(1)}, u32[]{:S(2)}, u32[]{:S(2)}) collective-permute-start(f32[17,4,8,128]{3,2,1,0:T(8,128)S(1)} %bitcast.68), channel_id=1, source_target_pairs={{0,16},{16,0},{32,48},{48,32},{64,80},{80,64},{96,112},{112,96},{1... | collective-permute-start | bytes 835592 | tf_op jit(solution)/shard_map/ppermute | solution.py:632
  41.6 4.0 %collective-permute-start.3 = (f32[10,4,8,128]{3,2,1,0:T(8,128)S(1)}, f32[10,4,8,128]{3,2,1,0:T(8,128)S(1)}, u32[]{:S(2)}, u32[]{:S(2)}) collective-permute-start(f32[10,4,8,128]{3,2,1,0:T(8,128)S(1)} %get-tuple-element.55), channel_id=1, source_target_pairs={{0,16},{16,0},{32,48},{48,32},{64,80},{80,64},{96,112},{112,96},{1... | collective-permute-start | bytes 491528 | tf_op jit(solution)/shard_map/ppermute | solution.py:644

commit v6 on v5

--- a/solution.py
+++ b/solution.py
@@ -47,28 +47,32 @@
     return pl.ds(row_tile * 128 + column_tile * 8, 8)
 
 
-def edges_kernel(tr_lo, tr_hi, ky_lo, ky_hi, wet_lo, wet_hi, lev_lo, lev_hi, out_lo, out_hi, swap_a, swap_b):
+def edges_kernel(
+    tr_lo, tr_hi, ky_lo, ky_hi, wet_lo, wet_hi, lev_lo, lev_hi, out_lo, out_hi, swap_a, swap_b
+):
     even = lax.axis_index("cross") % 2 == 0
     lane = lax.broadcasted_iota(jnp.int32, (8, 128), 1)
-    for tr, ky, wet, lev, out, at in (
-        (tr_lo, ky_lo, wet_lo, lev_lo, out_lo, 0),
-        (tr_hi, ky_hi, wet_hi, lev_hi, out_hi, 127),
-    ):
-        for l in range(LAYERS):
-            for i in range(2):
-                rows = pl.ds(i * 8, 8)
+    for i in range(2):
+        rows = pl.ds(i * 8, 8)
+        sent = []
+        for tr, ky, wet, lev, out, at in (
+            (tr_lo, ky_lo, wet_lo, lev_lo, out_lo, 0),
+            (tr_hi, ky_hi, wet_hi, lev_hi, out_hi, 127),
+        ):
+            together = jnp.zeros((8, 128), F32)
+            for l in range(LAYERS):
                 active = (wet[rows, :] > 0) & (lev[rows, :] > l)
                 cross = jnp.where(active, ky[l, rows, :], 0.0)
-                packed = jnp.where(lane < 64, 0.0, jnp.broadcast_to(cross[:, at : at + 1], (8, 128)))
+                packed = jnp.where(lane < 8, 0.0, jnp.broadcast_to(cross[:, at : at + 1], (8, 128)))
                 for t in range(TRACERS):
                     packed = jnp.where(lane == t, pltpu.roll(tr[t, l, rows, :], (t - at) % 128, 1), packed)
                 out[l, rows, :] = packed
-    for l in range(LAYERS):
-        for i in range(2):
-            rows = pl.ds(i * 8, 8)
-            lo, hi = out_lo[l, rows, :], out_hi[l, rows, :]
-            swap_a[l, rows, :] = jnp.where(even, hi, lo)
-            swap_b[l, rows, :] = jnp.where(even, lo, hi)
+                moved = packed if l == 0 else pltpu.roll(packed, 16 * l, 1)
+                together = jnp.where(lane // 16 == l, moved, together)
+            sent.append(together)
+        lo, hi = sent
+        swap_a[rows, :] = jnp.where(even, hi, lo)
+        swap_b[rows, :] = jnp.where(even, lo, hi)
 
 
 def edges(tracers, kappa_y, wet, levels):
@@ -89,8 +93,10 @@
             spec((), 0),
             spec((), 15),
         ],
-        out_specs=[pl.BlockSpec((LAYERS, 16, 128), lambda i: (0, 0, 0))] * 4,
-        out_shape=[jax.ShapeDtypeStruct((LAYERS, 16, 128), F32)] * 4,
+        out_specs=[pl.BlockSpec((LAYERS, 16, 128), lambda i: (0, 0, 0))] * 2
+        + [pl.BlockSpec((16, 128), lambda i: (0, 0))] * 2,
+        out_shape=[jax.ShapeDtypeStruct((LAYERS, 16, 128), F32)] * 2
+        + [jax.ShapeDtypeStruct((16, 128), F32)] * 2,
         compiler_params=SMALL,
         name="edges",
     )(*(in_hbm(x) for x in (tracers, tracers, kappa_y, kappa_y, wet, wet, levels, levels)))
@@ -109,9 +115,8 @@
     target = lax.broadcasted_iota(jnp.int32, (256, 256), 1)
     wanted = jnp.where(target < 128, target + 1, target + 127) % 128
     shift[...] = jnp.where(source == wanted, 1.0, 0.0).astype(jnp.bfloat16)
-    lax.fori_loop(
-        0, LAYERS, lambda layer, none: right_sides(layer, tr, ky, wet, lev, side, shift, moved), None
-    )
+    for layer in range(LAYERS):
+        right_sides(layer, tr, ky, wet, lev, side, shift, moved.at[layer % 2])
     for copy in copies:
         copy.wait()
     eliminate_bands(kx, co, wet, lev, fill, rho, inv, gain, mine, theirs)
@@ -279,7 +284,7 @@
             pltpu.VMEM((LAYERS, 256, 128), F32),
             pltpu.VMEM((LAYERS, 256, 128), F32),
             pltpu.VMEM((256, 256), jnp.bfloat16),
-            pltpu.VMEM((TRACERS + 1, 256, 256), F32),
+            pltpu.VMEM((2, TRACERS + 1, 256, 256), F32),
             pltpu.SemaphoreType.DMA((2,)),
         ],
         compiler_params=pltpu.CompilerParams(vmem_limit_bytes=12 * 1024 * 1024),
@@ -287,10 +292,15 @@
     )(tracers, in_hbm(kappa_x), kappa_y, in_hbm(courant), wet, levels)
 
 
+def unpacked(cells, l):
+    return cells if l == 0 else pltpu.roll(cells, 128 - 16 * l, 1)
+
+
 def inner_kernel(cells, out):
     place = lax.axis_index("cross")
     inner = (place > 0) & (place < lax.axis_size("cross") - 1)
-    out[...] = jnp.where(inner, cells[...], 0.0)
+    for l in range(LAYERS):
+        out[l * ROWS : (l + 1) * ROWS, :] = jnp.where(inner, unpacked(cells[...], l), 0.0)
 
 
 def inner_part(cells):
@@ -299,17 +309,19 @@
         inner_kernel,
         in_specs=[vmem],
         out_specs=vmem,
-        out_shape=jax.ShapeDtypeStruct(cells.shape, F32),
+        out_shape=jax.ShapeDtypeStruct((LAYERS * ROWS, 128), F32),
         compiler_params=SMALL,
         name="inner_part",
     )(cells)
 
 
 def outer_kernel(
-    own_lo, own_hi, from_a, from_b, inv, gain, rho, mine_in, theirs_in, mine, theirs, fix_lo, fix_hi
+    own_lo, own_hi, sent_a, from_b, inv, gain, rho, mine_in, theirs_in, mine, theirs, fix_lo, fix_hi, from_a
 ):
     even = lax.axis_index("cross") % 2 == 0
     first_core = is_first_core()
+    for l in range(LAYERS):
+        from_a[l * ROWS : (l + 1) * ROWS, :] = unpacked(sent_a[...], l)
     mine[...] = mine_in[...]
     theirs[...] = theirs_in[...]
     lane = lax.broadcasted_iota(jnp.int32, (LAYERS, 128), 1)
@@ -325,7 +337,7 @@
             here = own[pl.ds(row, LAYERS, stride=ROWS), :]
             cells = pl.ds(row, LAYERS, stride=ROWS)
             there = jnp.where(even, of_even[cells, :], of_odd[cells, :])
-            face = pltpu.roll(jnp.minimum(here, there), 64, 1)
+            face = pltpu.roll(jnp.minimum(here, there), 120, 1)
             deltas.append(face * (there - here))
         rhos = [None] + [coefficient(rho, row) for row in range(1, ROWS - 1)]
         reds = [None] * ROWS
@@ -366,6 +378,7 @@
         out_specs=[vmem] * 4,
         out_shape=[jax.ShapeDtypeStruct((PARTS * LAYERS * 8, 128), F32)] * 2
         + [jax.ShapeDtypeStruct((LAYERS * ROWS, 128), F32)] * 2,
+        scratch_shapes=[pltpu.VMEM((LAYERS * ROWS, 128), F32)],
         compiler_params=SMALL,
         name="outer_part",
     )(*(flat(x) for x in (own_lo, own_hi, from_a, from_b, inv, gain, rho, mine, theirs)))

time: 47.4 us -> 47.3 us (level)
  no operation moved by 1% of the time
where the time goes in v6:
time: 47.3 us; the launch traced here: 46.6 us
  blocking collectives  30.6 us (65%)
  Pallas kernels  7.67 us (16%)
  starting transfers between devices  7.65 us (16%)
  waiting for transfers between devices  0.57 us (1%)
    all_to_all x1, blocking collectives, on_device(): lax.all_to_all(sent.reshape(CHIPS, LAYERS * SENT, 128), 'chan', 0, 0, axi...  20.2 us
    all_to_all x1, blocking collectives, on_device(): lax.all_to_all(solved.reshape(CHIPS, LAYERS * BACK, 128), 'chan', 0, 0, a...  10.4 us
    ppermute x2, starting transfers between devices, on_device(): other = lax.ppermute(theirs, 'chan', pairs)  4.14 us
    ppermute x1, starting transfers between devices, on_device(): from_b = inner_part(lax.ppermute(to_b, ('chan', 'cross'), swap_b))  3.31 us
    pallas_call x2, Pallas kernels, final_part(): pl.pallas_call(functools.partial(final_kernel, own), in_specs=[vmem] * 4...  2.35 us
    pallas_call x1, Pallas kernels, local_part(): pl.pallas_call(local_kernel, in_specs=[vmem, hbm, vmem, hbm, vmem, vmem],...  2.32 us
    pallas_call x1, Pallas kernels, edges(): pl.pallas_call(edges_kernel, grid=(1,), in_specs=[spec((TRACERS, LAYERS),...  1.44 us
  transfers between devices with their start and end apart: 4, of which 1 were waited for; matrix products, arithmetic and copies ran while one was open for 0% of the time, Pallas kernels for 9%

profile of v6, /device:TPU:1, one launch (start us, length us, event | category | flops | bytes accessed | tf_op | source)
XLA Modules:
  0.0 46.6 jit_solution(16196723878197433405)
XLA Ops:
  0.0 0.0 copy-start.3
  0.0 0.0 copy-start.2
  0.0 0.0 copy-start.1
  0.0 0.0 copy-start
  0.0 1.4 %edges.1 = (f32[4,16,128]{2,1,0:T(8,128)S(1)}, f32[4,16,128]{2,1,0:T(8,128)S(1)}, f32[16,128]{1,0:T(8,128)S(1)}, f32[16,128]{1,0:T(8,128)S(1)}) custom-call(f32[5,4,16,2048]{3,2,1,0:T(8,128)} %tr_hi.1, f32[5,4,16,2048]{3,2,1,0:T(8,128)} %tr_hi.1, f32[4,16,2048]{2,1,0:T(8,128)} %ky_hi.1, f32[4,16,2048]{2,1,0:T(8,128)} %ky_hi.1, s32[16,2048]{1,0:T(8,128)} %wet_hi.1, ...), custom_call_target="tpu_custom_call" | custom-call | tf_op jit(solution)/shard_map/edges/pallas_call | solution.py:83
  1.5 3.3 %collective-permute-start.1 = (f32[16,128]{1,0:T(8,128)S(1)}, f32[16,128]{1,0:T(8,128)S(1)}, u32[]{:S(2)}, u32[]{:S(2)}) collective-permute-start(f32[16,128]{1,0:T(8,128)S(1)} %get-tuple-element.34), channel_id=1, source_target_pairs={{0,16},{1,2},{2,1},{3,4},{4,3},{5,6},{6,5},{7,8},{8,7},{9,10},{10,... | collective-permute-start | bytes 24584 | tf_op jit(solution)/shard_map/ppermute | solution.py:632
  4.8 0.2 collective-permute-start
  5.0 0.0 copy-done.3
  5.0 0.0 copy-done.2
  5.0 0.0 copy-done.1
  5.0 0.0 copy-done
  5.0 2.3 %local_part.1 = (f32[5,4,256,128]{3,2,1,0:T(8,128)S(1)}, f32[4,256,128]{2,1,0:T(8,128)S(1)}, f32[4,256,128]{2,1,0:T(8,128)S(1)}, f32[4,256,128]{2,1,0:T(8,128)S(...) custom-call(f32[5,4,256,128]{3,2,1,0:T(8,128)S(1)} %bitcast.48, ...), custom_call_target="tpu_custom_call" | custom-call | tf_op jit(solution)/shard_map/local_part/pallas_call | solution.py:277
  7.3 0.0 collective-permute-done.1.cells
  7.3 0.1 inner_part.1.from_b
  7.4 0.0 collective-permute-done.sent_a
  7.4 0.5 %outer_part.1 = (f32[544,128]{1,0:T(8,128)S(1)}, f32[544,128]{1,0:T(8,128)S(1)}, f32[64,128]{1,0:T(8,128)S(1)}, f32[64,128]{1,0:T(8,128)S(1)}) custom-call(f32[64,128]{1,0:T(8,128)S(1)} %bitcast.62, f32[64,128]{1,0:T(8,128)S(1)} %bitcast.63, f32[16,128]{1,0:T(8,128)S(1)} %collective-permute-done.sent_a, f32[64,128]{1,0:T(8,128)S(1)} %inner_part.1.from_b, ...), custom_call_target="tpu_custom_call" | custom-call | tf_op jit(solution)/shard_map/outer_part/pallas_call | solution.py:375
  7.9 1.3 %collective-permute-start.2 = (f32[17,4,8,128]{3,2,1,0:T(8,128)S(1)}, f32[17,4,8,128]{3,2,1,0:T(8,128)S(1)}, u32[]{:S(2)}, u32[]{:S(2)}) collective-permute-start(f32[17,4,8,128]{3,2,1,0:T(8,128)S(1)} %bitcast.64), channel_id=1, source_target_pairs={{0,16},{16,0},{32,48},{48,32},{64,80},{80,64},{96,112},{112,96},{1... | collective-permute-start | bytes 835592 | tf_op jit(solution)/shard_map/ppermute | solution.py:645
  9.3 0.6 %spread_part.1 = (f32[5,4,256,128]{3,2,1,0:T(8,128)S(1)}, f32[4,256,128]{2,1,0:T(8,128)S(1)}, f32[4,256,128]{2,1,0:T(8,128)S(1)}) custom-call(f32[5,4,256,128]{3,2,1,0:T(8,128)S(1)} %get-tuple-element.41.red, f32[4,256,128]{2,1,0:T(8,128)S(1)} %get-tuple-element.42.fill, f32[4,256,128]{2,1,0:T(8,128)S(1)} %get-tuple-element.37.rho, ...), custom_call_target="tpu_custom_call" | custom-call | tf_op jit(solution)/shard_map/spread_part/pallas_call | solution.py:554
  9.9 0.6 %collective-permute-done.2.other = f32[17,4,8,128]{3,2,1,0:T(8,128)S(1)} collective-permute-done((f32[17,4,8,128]{3,2,1,0:T(8,128)S(1)}, f32[17,4,8,128]{3,2,1,0:T(8,128)S(1)}, u32[]{:S(2)}, u32[]{:S(2)}) %collective-permute-start.2) | collective-permute-done | bytes 278560 | tf_op jit(solution)/shard_map/ppermute | solution.py:645
  10.4 0.1 pair_part.1
  10.6 20.2 %all_to_all.10 = f32[8,72,128]{2,1,0:T(8,128)S(1)} all-to-all(f32[8,72,128]{2,1,0:T(8,128)S(1)} %bitcast.58), channel_id=1, replica_groups={{0,32,64,96,128,160,192,224},{16,48,80,112,144,176,208,240},{1,33,65,97..., dimensions={0} | all-to-all | bytes 589824 | tf_op jit(solution)/shard_map/all_to_all | solution.py:649
  30.7 0.2 chain_part.1
  30.9 10.4 %all_to_all.11 = f32[8,40,128]{2,1,0:T(8,128)S(1)} all-to-all(f32[8,40,128]{2,1,0:T(8,128)S(1)} %bitcast.54), channel_id=1, replica_groups={{0,32,64,96,128,160,192,224},{16,48,80,112,144,176,208,240},{1,33,65,97..., dimensions={0} | all-to-all | bytes 327680 | tf_op jit(solution)/shard_map/all_to_all | solution.py:653
  41.4 0.1 middle_part.1
  41.4 2.8 %collective-permute-start.3 = (f32[10,4,8,128]{3,2,1,0:T(8,128)S(1)}, f32[10,4,8,128]{3,2,1,0:T(8,128)S(1)}, u32[]{:S(2)}, u32[]{:S(2)}) collective-permute-start(f32[10,4,8,128]{3,2,1,0:T(8,128)S(1)} %get-tuple-element.55), channel_id=1, source_target_pairs={{0,16},{16,0},{32,48},{48,32},{64,80},{80,64},{96,112},{112,96},{1... | collective-permute-start | bytes 491528 | tf_op jit(solution)/shard_map/ppermute | solution.py:657
  44.2 1.2 %final_own.1.refs_0_ = f32[5,4,256,128]{3,2,1,0:T(8,128)} custom-call(f32[5,4,256,128]{3,2,1,0:T(8,128)S(1)} %get-tuple-element.48.base, f32[4,256,128]{2,1,0:T(8,128)S(1)} %get-tuple-element.49.of_first, f32[4,256,128]{2,1,0:T(8,128)S(1)} %get-tuple-element.50.of_last, f32[10,4,8,128]{3,2,1,0:T(8,128)S(1)} %get-tuple-element.56.ends), custom_call_target="tpu_custom_call" | custom-call | tf_op jit(solution)/shard_map/final_own/pallas_call | solution.py:604
  45.4 0.0 collective-permute-done.3.ends
  45.4 1.2 %final_other.1 = f32[5,4,256,128]{3,2,1,0:T(8,128)} custom-call(f32[5,4,256,128]{3,2,1,0:T(8,128)S(1)} %get-tuple-element.48.base, f32[4,256,128]{2,1,0:T(8,128)S(1)} %get-tuple-element.49.of_first, f32[4,256,128]{2,1,0:T(8,128)S(1)} %get-tuple-element.50.of_last, f32[10,4,8,128]{3,2,1,0:T(8,128)S(1)} %collective-permute-done.3.ends, ...), custom_call_target="tpu_custom_call", output_to_operand_aliasing={{}: (4, {})} | custom-call | tf_op jit(solution)/shard_map/final_other/pallas_call | solution.py:604
Async XLA Ops:
  0.0 5.0 %copy-start.3 = (s32[16,2048]{1,0:T(8,128)S(1)}, s32[16,2048]{1,0:T(8,128)}, u32[]{:S(2)}) copy-start(s32[16,2048]{1,0:T(8,128)} %lev_hi.1) | copy-start | bytes 393220
  0.0 5.0 %copy-start.2 = (s32[16,2048]{1,0:T(8,128)S(1)}, s32[16,2048]{1,0:T(8,128)}, u32[]{:S(2)}) copy-start(s32[16,2048]{1,0:T(8,128)} %wet_hi.1) | copy-start | bytes 393220
  0.0 5.0 %copy-start.1 = (f32[4,16,2048]{2,1,0:T(8,128)S(1)}, f32[4,16,2048]{2,1,0:T(8,128)}, u32[]{:S(2)}) copy-start(f32[4,16,2048]{2,1,0:T(8,128)} %ky_hi.1) | copy-start | bytes 1572868
  0.0 5.0 %copy-start = (f32[5,4,16,2048]{3,2,1,0:T(8,128)S(1)}, f32[5,4,16,2048]{3,2,1,0:T(8,128)}, u32[]{:S(2)}) copy-start(f32[5,4,16,2048]{3,2,1,0:T(8,128)} %tr_hi.1) | copy-start | bytes 7864324
  1.5 5.9 %collective-permute-start.1 = (f32[16,128]{1,0:T(8,128)S(1)}, f32[16,128]{1,0:T(8,128)S(1)}, u32[]{:S(2)}, u32[]{:S(2)}) collective-permute-start(f32[16,128]{1,0:T(8,128)S(1)} %get-tuple-element.34), channel_id=1, source_target_pairs={{0,16},{1,2},{2,1},{3,4},{4,3},{5,6},{6,5},{7,8},{8,7},{9,10},{10,... | collective-permute-start | bytes 24584 | tf_op jit(solution)/shard_map/ppermute | solution.py:632
  4.8 2.6 %collective-permute-start = (f32[16,128]{1,0:T(8,128)S(1)}, f32[16,128]{1,0:T(8,128)S(1)}, u32[]{:S(2)}, u32[]{:S(2)}) collective-permute-start(f32[16,128]{1,0:T(8,128)S(1)} %get-tuple-element.33), channel_id=1, source_target_pairs={{0,1},{1,0},{2,3},{3,2},{4,5},{5,4},{6,7},{7,6},{8,9},{9,8},{10,11... | collective-permute-start | bytes 24584 | tf_op jit(solution)/shard_map/ppermute | solution.py:633
  7.9 2.5 %collective-permute-start.2 = (f32[17,4,8,128]{3,2,1,0:T(8,128)S(1)}, f32[17,4,8,128]{3,2,1,0:T(8,128)S(1)}, u32[]{:S(2)}, u32[]{:S(2)}) collective-permute-start(f32[17,4,8,128]{3,2,1,0:T(8,128)S(1)} %bitcast.64), channel_id=1, source_target_pairs={{0,16},{16,0},{32,48},{48,32},{64,80},{80,64},{96,112},{112,96},{1... | collective-permute-start | bytes 835592 | tf_op jit(solution)/shard_map/ppermute | solution.py:645
  41.4 4.0 %collective-permute-start.3 = (f32[10,4,8,128]{3,2,1,0:T(8,128)S(1)}, f32[10,4,8,128]{3,2,1,0:T(8,128)S(1)}, u32[]{:S(2)}, u32[]{:S(2)}) collective-permute-start(f32[10,4,8,128]{3,2,1,0:T(8,128)S(1)} %get-tuple-element.55), channel_id=1, source_target_pairs={{0,16},{16,0},{32,48},{48,32},{64,80},{80,64},{96,112},{112,96},{1... | collective-permute-start | bytes 491528 | tf_op jit(solution)/shard_map/ppermute | solution.py:657
